TPU v7x, 32 devices: a whole 2x2x4 slice. The times are simulated.
32 devices in a mesh: rows: 8 (over z, y), cols: 4 (over x, core).
Axes of the slice: x: 2, y: 2, z: 4, core: 2. Of those that a mesh axis runs over, the one named last changes fastest.
Arguments:
- residual_block: float32 [65536, 64], P('rows', 'cols'), may hold values from -6 to 6
- basis: bfloat16 [65536, 64], P('rows', 'cols'), may hold values from -0.0234375 to 0.0234375
- fine_tiles: bfloat16 [512, 4, 128, 128], P('rows')
- fine_index: int32 [512, 4], P('rows'), may hold values from 0 to 511, as said below
- mid_tiles: bfloat16 [64, 3, 128, 128], P('rows')
- fine_owner: int32 [65536], P('rows'), may hold values from 0 to 8191, as said below
- mid_owner: int32 [8192], P('rows'), may hold values from 0 to 1023, as said below
- coarse_inverse: float32 [1024, 1024], P('rows'), as said below
Outputs:
- directions: float32 [65536, 64], P('rows', 'cols')
- gram: float32 [64, 64], P(None, 'cols')
Inputs may be any that keep to these rules, and one draw needn't show every extreme that they name: `fine_index`: slot 0 of block row g names g itself; every block named in a block row of partition p (block rows p*64 to p*64 + 63) belongs to partition p - 1, p or p + 1. `fine_owner`: the fine vertices of partition p map to level-one rows p*1024 to p*1024 + 1023; every level-one row receives exactly 8 vertices. `mid_owner`: the level-one rows of partitions 2q and 2q + 1 map to level-two rows 2q*128 to 2q*128 + 2*128 - 1; every level-two row receives exactly 8 level-one rows. coarse_inverse is symmetric.
All inputs are finite; a program needn't handle non-finite values.
Results may differ from a plain program's by a relative error of at most 0.013.
Values may be sent and summed in bfloat16 or wider, within the bound.
No kernel may reach another device: no remote copies, remote signals or barrier semaphores. Data moves between devices by JAX's collectives and lax.ppermute only.
A program may use at most 64 MiB of HBM per device.

v0:
```python
import jax
import jax.numpy as jnp
from jax import lax
from jax.sharding import PartitionSpec as P

DAMPING = 0.6666666666666666


def with_halo(array, sides, width):
    for axis, dim in sides:
        peers, length = (lax.axis_size(axis), array.shape[dim])
        up = [(i, (i + 1) % peers) for i in range(peers - 1)]
        down = [(j, i) for i, j in up]
        last = lax.slice_in_dim(array, length - width, length, axis=dim)
        leading = lax.slice_in_dim(array, 0, width, axis=dim)
        before = lax.ppermute(last, axis, up)
        after = lax.ppermute(leading, axis, down)
        array = jnp.concatenate([before, array, after], axis=dim)
    return array


def swapped(value, axis, apart):
    mask = 2**apart
    pairs = [(source, source ^ mask) for source in range(lax.axis_size(axis))]
    return lax.ppermute(value, axis, pairs)


def fine_apply(vector, matrix, window_index):
    extent = matrix.shape[2]
    packed = vector.astype(jnp.bfloat16).reshape(-1, extent, vector.shape[1])
    window = with_halo(packed, (("rows", 0),), packed.shape[0])
    picked = window[window_index]
    product = jnp.einsum("bkij,bkjc->bic", matrix, picked, preferred_element_type=jnp.float32)
    return product.reshape(vector.shape)


def mid_apply(vector, matrix):
    blocks = matrix.shape[0]
    extent = matrix.shape[2]
    packed = vector.astype(jnp.bfloat16).reshape(blocks, extent, vector.shape[1])
    window = with_halo(packed, (("rows", 0),), 1)
    product = jnp.einsum(
        "bij,bjc->bic", matrix[:, 0], window[:-2], preferred_element_type=jnp.float32
    )
    product = product + jnp.einsum(
        "bij,bjc->bic", matrix[:, 1], window[1:-1], preferred_element_type=jnp.float32
    )
    product = product + jnp.einsum(
        "bij,bjc->bic", matrix[:, 2], window[2:], preferred_element_type=jnp.float32
    )
    return product.reshape(vector.shape)


def on_device(
    residual_block, basis, fine_tiles, fine_index, mid_tiles, fine_owner, mid_owner, coarse_inverse
):
    device = lax.axis_index("rows")
    blocks = fine_tiles.shape[0]
    mid_count = mid_tiles.shape[0] * mid_tiles.shape[2]
    coarse_count = coarse_inverse.shape[0]
    col_width = residual_block.shape[1]
    parity = device % 2
    window_index = fine_index - (device - 1) * blocks
    fine_local = fine_owner - device * mid_count
    mid_local = mid_owner - (device - parity) * coarse_count
    fine_inv = 1.0 / jnp.diagonal(fine_tiles[:, 0], axis1=1, axis2=2).astype(jnp.float32).reshape(
        -1, 1
    )
    mid_inv = 1.0 / jnp.diagonal(mid_tiles[:, 1], axis1=1, axis2=2).astype(jnp.float32).reshape(
        -1, 1
    )
    fine_x = DAMPING * fine_inv * residual_block
    fine_x = fine_x + DAMPING * fine_inv * (
        residual_block - fine_apply(fine_x, fine_tiles, window_index)
    )
    fine_res = residual_block - fine_apply(fine_x, fine_tiles, window_index)
    partial_mid = jax.ops.segment_sum(fine_res, fine_local, num_segments=mid_count)
    mid_x = DAMPING * mid_inv * partial_mid
    mid_x = mid_x + DAMPING * mid_inv * (partial_mid - mid_apply(mid_x, mid_tiles))
    mid_res = partial_mid - mid_apply(mid_x, mid_tiles)
    partial_value = jax.ops.segment_sum(mid_res, mid_local, num_segments=2 * coarse_count)
    halves = partial_value.reshape(2, coarse_count, col_width)
    own_half = jnp.where(parity == 0, halves[0], halves[1])
    other_half = jnp.where(parity == 0, halves[1], halves[0])
    coarse_rhs = own_half + swapped(other_half, "rows", 0)
    coarse_fix = jnp.dot(
        coarse_inverse,
        lax.all_gather(coarse_rhs, "rows", axis=0, tiled=True),
        precision=lax.Precision.HIGHEST,
        preferred_element_type=jnp.float32,
    )
    partner_fix = swapped(coarse_fix, "rows", 0)
    pair_values = jnp.where(
        parity == 0,
        jnp.concatenate([coarse_fix, partner_fix], axis=0),
        jnp.concatenate([partner_fix, coarse_fix], axis=0),
    )
    mid_x = mid_x + pair_values[mid_local]
    mid_x = mid_x + DAMPING * mid_inv * (partial_mid - mid_apply(mid_x, mid_tiles))
    fine_x = fine_x + mid_x[fine_local]
    finished = fine_x + DAMPING * fine_inv * (
        residual_block - fine_apply(fine_x, fine_tiles, window_index)
    )
    rounded = finished.astype(jnp.bfloat16)
    partial_gram = lax.dot_general(
        lax.all_gather(basis, "cols", axis=1, tiled=True),
        rounded,
        (((0,), (0,)), ((), ())),
        preferred_element_type=jnp.float32,
    )
    gram = lax.psum(partial_gram, "rows")
    return (finished, gram)


def solution(mesh):
    in_specs = (
        P("rows", "cols"),
        P("rows", "cols"),
        P("rows", None, None, None),
        P("rows", None),
        P("rows", None, None, None),
        P("rows"),
        P("rows"),
        P("rows", None),
    )
    out_specs = (P("rows", "cols"), P(None, "cols"))
    return jax.shard_map(
        on_device, mesh=mesh, in_specs=in_specs, out_specs=out_specs, check_vma=False
    )
```

profile of v0, /device:TPU:0, one launch (start us, length us, event | category | flops | bytes accessed | tf_op | source)
XLA Modules:
  0.0 277.5 jit_solution(13953990770068478665)
XLA Ops:
  7.3 1.8 slice.89
  9.1 3.9 %copy.204 = bf16[64,1,128,128]{0,3,2,1:T(8,128)(2,1)} copy(bf16[64,1,128,128]{3,2,1,0:T(8,128)(2,1)S(1)} %slice.89) | data formatting | bytes 4194304
  13.0 1.9 gather_fusion
  15.1 4.9 %collective-permute-start = (bf16[64,128,16]{1,2,0:T(8,128)(2,1)S(1)}, bf16[64,128,16]{1,2,0:T(8,128)(2,1)S(1)}, u32[]{:S(2)}, u32[]{:S(2)}) collective-permute-start(bf16[64,128,16]{1,2,0:T(8,128)(2,1)S(1)} %copy_bitcast_fusion.2), channel_id=1, source_target_pairs={{0,4},{4,8},{8,12},{12,16},{16,20},{20,24},{24,28},{1,5},{5,9},{9,... | collective-permute-start | bytes 786440 | tf_op jit(solution)/shard_map/ppermute | solution.py:16
  20.0 1.3 collective-permute-start.1
  21.5 1.0 slice_bitcast_fusion
  22.5 3.1 %copy.166 = bf16[8,128,128]{0,2,1:T(8,128)(2,1)} copy(bf16[8,128,128]{2,1,0:T(8,128)(2,1)S(1)} %slice_bitcast_fusion) | data formatting | bytes 524288 | tf_op jit(solution)/shard_map/squeeze | solution.py:69
  25.6 1.9 gather_fusion.2
  27.7 3.5 %collective-permute-done = bf16[64,128,16]{1,2,0:T(8,128)(2,1)S(1)} collective-permute-done((bf16[64,128,16]{1,2,0:T(8,128)(2,1)S(1)}, bf16[64,128,16]{1,2,0:T(8,128)(2,1)S(1)}, u32[]{:S(2)}, u32[]{:S(2)}) %collective-permute-start) | collective-permute-done | bytes 262176 | tf_op jit(solution)/shard_map/ppermute | solution.py:16
  31.2 0.9 gather_fusion.1
  32.1 5.7 %convolution_bitcast_fusion.2 = f32[64,2,8,128]{3,2,1,0:T(8,128)S(1)} fusion(bf16[64,4,128,16]{2,3,1,0:T(8,128)(2,1)S(1)} %bitcast.177, bf16[64,4,128,128]{3,2,1,0:T(8,128)(2,1)} %param.10), kind=kOutput, calls=%fused_computation.11 | convolution fusion | flops 134217728 | bytes 9961472 | tf_op jit(solution)/shard_map/bkij,bkjc->bic/dot_general | solution.py:33
  37.9 4.4 %collective-permute-start.2 = (bf16[64,128,16]{1,2,0:T(8,128)(2,1)S(1)}, bf16[64,128,16]{1,2,0:T(8,128)(2,1)S(1)}, u32[]{:S(2)}, u32[]{:S(2)}) collective-permute-start(bf16[64,128,16]{1,2,0:T(8,128)(2,1)S(1)} %copy_bitcast_fusion.1), channel_id=1, source_target_pairs={{0,4},{4,8},{8,12},{12,16},{16,20},{20,24},{24,28},{1,5},{5,9},{9,... | collective-permute-start | bytes 786440 | tf_op jit(solution)/shard_map/ppermute | solution.py:16
  42.3 1.3 collective-permute-start.3
  43.7 3.3 %collective-permute-done.2 = bf16[64,128,16]{1,2,0:T(8,128)(2,1)S(1)} collective-permute-done((bf16[64,128,16]{1,2,0:T(8,128)(2,1)S(1)}, bf16[64,128,16]{1,2,0:T(8,128)(2,1)S(1)}, u32[]{:S(2)}, u32[]{:S(2)}) %collective-permute-start.2) | collective-permute-done | bytes 262176 | tf_op jit(solution)/shard_map/ppermute | solution.py:16
  47.0 5.8 %collective-permute-done.3 = bf16[64,128,16]{1,2,0:T(8,128)(2,1)S(1)} collective-permute-done((bf16[64,128,16]{1,2,0:T(8,128)(2,1)S(1)}, bf16[64,128,16]{1,2,0:T(8,128)(2,1)S(1)}, u32[]{:S(2)}, u32[]{:S(2)}) %collective-permute-start.3) | collective-permute-done | bytes 262176 | tf_op jit(solution)/shard_map/ppermute | solution.py:17
  53.8 5.7 %convolution_bitcast_fusion.1 = f32[64,2,8,128]{3,2,1,0:T(8,128)S(1)} fusion(bf16[64,4,128,16]{2,3,1,0:T(8,128)(2,1)S(1)} %bitcast.178, bf16[64,4,128,128]{3,2,1,0:T(8,128)(2,1)} %param.10), kind=kOutput, calls=%fused_computation.10 | convolution fusion | flops 134217728 | bytes 9961472 | tf_op jit(solution)/shard_map/bkij,bkjc->bic/dot_general | solution.py:33
  59.6 2.6 copy.172
  62.2 44.4 %scatter_custom_fusion = f32[1024,16]{1,0:T(8,128)S(1)} fusion(s32[8192]{0:T(1024)S(1)} %get-tuple-element.11, f32[8192,16]{1,0:T(8,128)} %copy.172, f32[]{:T(128)} %constant.25.clone.1), kind=kCustom, calls=%fused_computation.51 | custom fusion | flops 131072 | bytes 66048 | tf_op jit(solution)/shard_map/scatter-add | solution.py:77
  107.1 1.3 collective-permute-start.5
  108.4 5.2 %collective-permute-start.4 = (bf16[1,128,16]{1,2,0:T(8,128)(2,1)S(1)}, bf16[1,128,16]{1,2,0:T(8,128)(2,1)S(1)}, u32[]{:S(2)}, u32[]{:S(2)}) collective-permute-start(bf16[1,128,16]{1,2,0:T(8,128)(2,1)S(1)} %get-tuple-element.18), channel_id=1, source_target_pairs={{0,4},{4,8},{8,12},{12,16},{16,20},{20,24},{24,28},{1,5},{5,9},{9,... | collective-permute-start | bytes 12296 | tf_op jit(solution)/shard_map/ppermute | solution.py:16
  113.8 1.1 collective-permute-done.4
  115.4 1.3 collective-permute-start.7
  116.7 6.5 %collective-permute-start.6 = (bf16[1,128,16]{1,2,0:T(8,128)(2,1)S(1)}, bf16[1,128,16]{1,2,0:T(8,128)(2,1)S(1)}, u32[]{:S(2)}, u32[]{:S(2)}) collective-permute-start(bf16[1,128,16]{1,2,0:T(8,128)(2,1)S(1)} %get-tuple-element.16), channel_id=1, source_target_pairs={{0,4},{4,8},{8,12},{12,16},{16,20},{20,24},{24,28},{1,5},{5,9},{9,... | collective-permute-start | bytes 12296 | tf_op jit(solution)/shard_map/ppermute | solution.py:16
  123.5 1.1 collective-permute-done.6
  124.8 1.0 copy.202
  125.8 1.9 bitcast_subtract_fusion.3
  127.7 6.4 %scatter_custom_fusion.1 = f32[256,16]{1,0:T(8,128)S(1)} fusion(s32[1024]{0:T(1024)S(1)} %get-tuple-element.13, f32[1024,16]{1,0:T(8,128)} %bitcast_subtract_fusion.3, f32[]{:T(128)} %constant.25.clone.1), kind=kCustom, calls=%fused_computation.70 | custom fusion | flops 16384 | bytes 16896 | tf_op jit(solution)/shard_map/scatter-add | solution.py:81
  134.2 3.2 %collective-permute-start.8 = (f32[128,16]{1,0:T(8,128)S(1)}, f32[128,16]{1,0:T(8,128)S(1)}, u32[]{:S(2)}, u32[]{:S(2)}) collective-permute-start(f32[128,16]{1,0:T(8,128)S(1)} %slice_select_fusion), channel_id=1, source_target_pairs={{0,4},{4,0},{8,12},{12,8},{16,20},{20,16},{24,28},{28,24},{1,5},{5... | collective-permute-start | bytes 24584 | tf_op jit(solution)/shard_map/ppermute | solution.py:25
  137.4 2.2 collective-permute-done.8
  139.7 35.5 %all_gather.6 = f32[1024,16]{1,0:T(8,128)S(1)} all-gather(f32[128,16]{1,0:T(8,128)S(1)} %select_add_fusion), channel_id=1, replica_groups=mesh['rows'=8,'cols'=4] {'rows'}, dimensions={0}, use_global_device_ids=true | all-gather | bytes 73728 | tf_op jit(solution)/shard_map/all_gather | solution.py:88
  175.2 1.0 convolution_bitcast_fusion.4
  176.1 3.7 %collective-permute-done.9 = f32[128,16]{0,1:T(8,128)S(1)} collective-permute-done((f32[128,16]{0,1:T(8,128)S(1)}, f32[128,16]{0,1:T(8,128)S(1)}, u32[]{:S(2)}, u32[]{:S(2)}) %collective-permute-start.9) | collective-permute-done | bytes 8224 | tf_op jit(solution)/shard_map/ppermute | solution.py:25
  179.9 4.0 %gather_fusion.4 = f32[1024,16]{1,0:T(8,128)} fusion(f32[256,16]{1,0:T(8,128)S(1)} %copy.186, s32[1024]{0:T(1024)S(1)} %get-tuple-element.12), kind=kCustom, calls=%fused_computation.4 | custom fusion | bytes 135168 | tf_op jit(solution)/shard_map/gather | solution.py:98
  183.9 1.2 copy.187
  185.4 1.3 collective-permute-start.11
  186.7 4.5 %collective-permute-start.10 = (bf16[1,128,16]{1,2,0:T(8,128)(2,1)S(1)}, bf16[1,128,16]{1,2,0:T(8,128)(2,1)S(1)}, u32[]{:S(2)}, u32[]{:S(2)}) collective-permute-start(bf16[1,128,16]{1,2,0:T(8,128)(2,1)S(1)} %get-tuple-element.14), channel_id=1, source_target_pairs={{0,4},{4,8},{8,12},{12,16},{16,20},{20,24},{24,28},{1,5},{5,9},{9,... | collective-permute-start | bytes 12296 | tf_op jit(solution)/shard_map/ppermute | solution.py:16
  191.5 1.1 collective-permute-done.10
  193.1 27.9 %gather_fusion.5 = f32[8192,16]{1,0:T(8,128)} fusion(f32[1024,16]{1,0:T(8,128)S(1)} %copy.193, s32[8192]{0:T(1024)S(1)} %get-tuple-element.10), kind=kCustom, calls=%fused_computation.5 | custom fusion | bytes 1081344 | tf_op jit(solution)/shard_map/gather | solution.py:100
  221.0 2.8 %copy.194 = f32[8192,16]{0,1:T(8,128)S(1)} copy(f32[8192,16]{1,0:T(8,128)} %gather_fusion.5) | data formatting | bytes 1048576 | tf_op jit(solution)/shard_map/gather | solution.py:100
  223.9 4.2 %collective-permute-start.12 = (bf16[64,128,16]{1,2,0:T(8,128)(2,1)S(1)}, bf16[64,128,16]{1,2,0:T(8,128)(2,1)S(1)}, u32[]{:S(2)}, u32[]{:S(2)}) collective-permute-start(bf16[64,128,16]{1,2,0:T(8,128)(2,1)S(1)} %copy_bitcast_fusion), channel_id=1, source_target_pairs={{0,4},{4,8},{8,12},{12,16},{16,20},{20,24},{24,28},{1,5},{5,9},{9,... | collective-permute-start | bytes 786440 | tf_op jit(solution)/shard_map/ppermute | solution.py:16
  228.1 1.3 collective-permute-start.13
  229.4 2.5 collective-permute-done.12
  232.0 4.5 %collective-permute-done.13 = bf16[64,128,16]{1,2,0:T(8,128)(2,1)} collective-permute-done((bf16[64,128,16]{1,2,0:T(8,128)(2,1)S(1)}, bf16[64,128,16]{1,2,0:T(8,128)(2,1)}, u32[]{:S(2)}, u32[]{:S(2)}) %collective-permute-start.13) | collective-permute-done | bytes 262176 | tf_op jit(solution)/shard_map/ppermute | solution.py:17
  236.5 1.1 pad_maximum_fusion.2
  238.4 5.7 %convolution_bitcast_fusion = f32[64,2,8,128]{3,2,1,0:T(8,128)S(1)} fusion(bf16[64,4,128,16]{2,3,1,0:T(8,128)(2,1)S(1)} %bitcast.176, bf16[64,4,128,128]{3,2,1,0:T(8,128)(2,1)} %param.10), kind=kOutput, calls=%fused_computation.9 | convolution fusion | flops 134217728 | bytes 9961472 | tf_op jit(solution)/shard_map/bkij,bkjc->bic/dot_general | solution.py:33
  244.4 2.5 all-gather.2.cloned.1.call-done
  246.9 1.6 convolution_bitcast_fusion.3
  248.5 22.2 %psum.7 = f32[64,16]{0,1:T(8,128)} all-reduce(f32[64,16]{0,1:T(8,128)S(1)} %convolution_bitcast_fusion.3), channel_id=1, replica_groups=mesh['rows'=8,'cols'=4] {'rows'}, use_global_device_ids=true, to_apply=%region_2.3 | all-reduce | flops 1024 | bytes 8192 | tf_op jit(solution)/shard_map/psum | solution.py:111
  (70 shorter events, 5.7 us)
Async XLA Ops:
  7.2 168.0 %copy-start = (f32[128,1024]{1,0:T(8,128)S(1)}, f32[128,1024]{1,0:T(8,128)}, u32[]{:S(2)}) copy-start(f32[128,1024]{1,0:T(8,128)} %param.15) | copy-start | bytes 1572868
  7.2 7.9 %copy-start.1 = (f32[8192,16]{0,1:T(8,128)S(1)}, f32[8192,16]{0,1:T(8,128)}, u32[]{:S(2)}) copy-start(f32[8192,16]{0,1:T(8,128)} %param.8) | copy-start | bytes 1572868
  7.2 14.1 %copy-start.8 = (s32[64,4]{0,1:T(4,128)S(1)}, s32[64,4]{0,1:T(4,128)}, u32[]{:S(2)}) copy-start(s32[64,4]{0,1:T(4,128)} %param.11) | copy-start | bytes 3076
  7.2 239.7 %all-gather.2.cloned.1.call-start = ((), (), s32[]{:S(2)}) async-start(), calls=%async_computation | async-start | bytes 1310720 | tf_op jit(solution)/shard_map/all_gather | solution.py:106
  7.3 20.4 %copy-start.7 = (s32[1024]{0:T(1024)S(1)}, s32[1024]{0:T(1024)}, u32[]{:S(2)}) copy-start(s32[1024]{0:T(1024)} %param.14) | copy-start | bytes 12292
  15.1 16.0 %collective-permute-start = (bf16[64,128,16]{1,2,0:T(8,128)(2,1)S(1)}, bf16[64,128,16]{1,2,0:T(8,128)(2,1)S(1)}, u32[]{:S(2)}, u32[]{:S(2)}) collective-permute-start(bf16[64,128,16]{1,2,0:T(8,128)(2,1)S(1)} %copy_bitcast_fusion.2), channel_id=1, source_target_pairs={{0,4},{4,8},{8,12},{12,16},{16,20},{20,24},{24,28},{1,5},{5,9},{9,... | collective-permute-start | bytes 786440 | tf_op jit(solution)/shard_map/ppermute | solution.py:16
  20.0 11.2 %collective-permute-start.1 = (bf16[64,128,16]{1,2,0:T(8,128)(2,1)S(1)}, bf16[64,128,16]{1,2,0:T(8,128)(2,1)S(1)}, u32[]{:S(2)}, u32[]{:S(2)}) collective-permute-start(bf16[64,128,16]{1,2,0:T(8,128)(2,1)S(1)} %copy_bitcast_fusion.2), channel_id=1, source_target_pairs={{4,0},{8,4},{12,8},{16,12},{20,16},{24,20},{28,24},{5,1},{9,5},{13... | collective-permute-start | bytes 786440 | tf_op jit(solution)/shard_map/ppermute | solution.py:17
  32.1 11.5 %copy-start.6 = (s32[8192]{0:T(1024)S(1)}, s32[8192]{0:T(1024)}, u32[]{:S(2)}) copy-start(s32[8192]{0:T(1024)} %param.13) | copy-start | bytes 98308
  37.9 9.1 %collective-permute-start.2 = (bf16[64,128,16]{1,2,0:T(8,128)(2,1)S(1)}, bf16[64,128,16]{1,2,0:T(8,128)(2,1)S(1)}, u32[]{:S(2)}, u32[]{:S(2)}) collective-permute-start(bf16[64,128,16]{1,2,0:T(8,128)(2,1)S(1)} %copy_bitcast_fusion.1), channel_id=1, source_target_pairs={{0,4},{4,8},{8,12},{12,16},{16,20},{20,24},{24,28},{1,5},{5,9},{9,... | collective-permute-start | bytes 786440 | tf_op jit(solution)/shard_map/ppermute | solution.py:16
  42.3 10.5 %collective-permute-start.3 = (bf16[64,128,16]{1,2,0:T(8,128)(2,1)S(1)}, bf16[64,128,16]{1,2,0:T(8,128)(2,1)S(1)}, u32[]{:S(2)}, u32[]{:S(2)}) collective-permute-start(bf16[64,128,16]{1,2,0:T(8,128)(2,1)S(1)} %copy_bitcast_fusion.1), channel_id=1, source_target_pairs={{4,0},{8,4},{12,8},{16,12},{20,16},{24,20},{28,24},{5,1},{9,5},{13... | collective-permute-start | bytes 786440 | tf_op jit(solution)/shard_map/ppermute | solution.py:17
  53.8 53.1 %copy-start.4 = (bf16[8,3,128,128]{3,2,1,0:T(8,128)(2,1)S(1)}, bf16[8,3,128,128]{3,2,1,0:T(8,128)(2,1)}, u32[]{:S(2)}) copy-start(bf16[8,3,128,128]{3,2,1,0:T(8,128)(2,1)} %param.12) | copy-start | bytes 2359300
  107.1 6.5 %collective-permute-start.5 = (bf16[1,128,16]{1,2,0:T(8,128)(2,1)S(1)}, bf16[1,128,16]{1,2,0:T(8,128)(2,1)S(1)}, u32[]{:S(2)}, u32[]{:S(2)}) collective-permute-start(bf16[1,128,16]{1,2,0:T(8,128)(2,1)S(1)} %get-tuple-element.19), channel_id=1, source_target_pairs={{4,0},{8,4},{12,8},{16,12},{20,16},{24,20},{28,24},{5,1},{9,5},{13... | collective-permute-start | bytes 12296 | tf_op jit(solution)/shard_map/ppermute | solution.py:17
  108.4 6.5 %collective-permute-start.4 = (bf16[1,128,16]{1,2,0:T(8,128)(2,1)S(1)}, bf16[1,128,16]{1,2,0:T(8,128)(2,1)S(1)}, u32[]{:S(2)}, u32[]{:S(2)}) collective-permute-start(bf16[1,128,16]{1,2,0:T(8,128)(2,1)S(1)} %get-tuple-element.18), channel_id=1, source_target_pairs={{0,4},{4,8},{8,12},{12,16},{16,20},{20,24},{24,28},{1,5},{5,9},{9,... | collective-permute-start | bytes 12296 | tf_op jit(solution)/shard_map/ppermute | solution.py:16
  115.4 7.8 %collective-permute-start.7 = (bf16[1,128,16]{1,2,0:T(8,128)(2,1)S(1)}, bf16[1,128,16]{1,2,0:T(8,128)(2,1)S(1)}, u32[]{:S(2)}, u32[]{:S(2)}) collective-permute-start(bf16[1,128,16]{1,2,0:T(8,128)(2,1)S(1)} %get-tuple-element.17), channel_id=1, source_target_pairs={{4,0},{8,4},{12,8},{16,12},{20,16},{24,20},{28,24},{5,1},{9,5},{13... | collective-permute-start | bytes 12296 | tf_op jit(solution)/shard_map/ppermute | solution.py:17
  116.7 7.8 %collective-permute-start.6 = (bf16[1,128,16]{1,2,0:T(8,128)(2,1)S(1)}, bf16[1,128,16]{1,2,0:T(8,128)(2,1)S(1)}, u32[]{:S(2)}, u32[]{:S(2)}) collective-permute-start(bf16[1,128,16]{1,2,0:T(8,128)(2,1)S(1)} %get-tuple-element.16), channel_id=1, source_target_pairs={{0,4},{4,8},{8,12},{12,16},{16,20},{20,24},{24,28},{1,5},{5,9},{9,... | collective-permute-start | bytes 12296 | tf_op jit(solution)/shard_map/ppermute | solution.py:16
  134.2 5.5 %collective-permute-start.8 = (f32[128,16]{1,0:T(8,128)S(1)}, f32[128,16]{1,0:T(8,128)S(1)}, u32[]{:S(2)}, u32[]{:S(2)}) collective-permute-start(f32[128,16]{1,0:T(8,128)S(1)} %slice_select_fusion), channel_id=1, source_target_pairs={{0,4},{4,0},{8,12},{12,8},{16,20},{20,16},{24,28},{28,24},{1,5},{5... | collective-permute-start | bytes 24584 | tf_op jit(solution)/shard_map/ppermute | solution.py:25
  176.1 3.7 %collective-permute-start.9 = (f32[128,16]{0,1:T(8,128)S(1)}, f32[128,16]{0,1:T(8,128)S(1)}, u32[]{:S(2)}, u32[]{:S(2)}) collective-permute-start(f32[128,16]{0,1:T(8,128)S(1)} %convolution_bitcast_fusion.4), channel_id=1, source_target_pairs={{0,4},{4,0},{8,12},{12,8},{16,20},{20,16},{24,28},{28,24},{1,5},{5... | collective-permute-start | bytes 24584 | tf_op jit(solution)/shard_map/ppermute | solution.py:25
  185.4 5.9 %collective-permute-start.11 = (bf16[1,128,16]{1,2,0:T(8,128)(2,1)S(1)}, bf16[1,128,16]{1,2,0:T(8,128)(2,1)S(1)}, u32[]{:S(2)}, u32[]{:S(2)}) collective-permute-start(bf16[1,128,16]{1,2,0:T(8,128)(2,1)S(1)} %get-tuple-element.15), channel_id=1, source_target_pairs={{4,0},{8,4},{12,8},{16,12},{20,16},{24,20},{28,24},{5,1},{9,5},{13... | collective-permute-start | bytes 12296 | tf_op jit(solution)/shard_map/ppermute | solution.py:17
  186.7 5.9 %collective-permute-start.10 = (bf16[1,128,16]{1,2,0:T(8,128)(2,1)S(1)}, bf16[1,128,16]{1,2,0:T(8,128)(2,1)S(1)}, u32[]{:S(2)}, u32[]{:S(2)}) collective-permute-start(bf16[1,128,16]{1,2,0:T(8,128)(2,1)S(1)} %get-tuple-element.14), channel_id=1, source_target_pairs={{0,4},{4,8},{8,12},{12,16},{16,20},{20,24},{24,28},{1,5},{5,9},{9,... | collective-permute-start | bytes 12296 | tf_op jit(solution)/shard_map/ppermute | solution.py:16
  223.8 12.7 %copy-start.2 = (f32[8192,16]{0,1:T(8,128)}, f32[8192,16]{0,1:T(8,128)S(1)}, u32[]{:S(2)}) copy-start(f32[8192,16]{0,1:T(8,128)S(1)} %copy.194) | copy-start | bytes 1572868
  223.9 8.1 %collective-permute-start.12 = (bf16[64,128,16]{1,2,0:T(8,128)(2,1)S(1)}, bf16[64,128,16]{1,2,0:T(8,128)(2,1)S(1)}, u32[]{:S(2)}, u32[]{:S(2)}) collective-permute-start(bf16[64,128,16]{1,2,0:T(8,128)(2,1)S(1)} %copy_bitcast_fusion), channel_id=1, source_target_pairs={{0,4},{4,8},{8,12},{12,16},{16,20},{20,24},{24,28},{1,5},{5,9},{9,... | collective-permute-start | bytes 786440 | tf_op jit(solution)/shard_map/ppermute | solution.py:16
  228.1 8.4 %collective-permute-start.13 = (bf16[64,128,16]{1,2,0:T(8,128)(2,1)S(1)}, bf16[64,128,16]{1,2,0:T(8,128)(2,1)}, u32[]{:S(2)}, u32[]{:S(2)}) collective-permute-start(bf16[64,128,16]{1,2,0:T(8,128)(2,1)S(1)} %copy_bitcast_fusion), channel_id=1, source_target_pairs={{4,0},{8,4},{12,8},{16,12},{20,16},{24,20},{28,24},{5,1},{9,5},{13... | collective-permute-start | bytes 786440 | tf_op jit(solution)/shard_map/ppermute | solution.py:17
  238.4 5.7 %copy-start.3 = (f32[8192,16]{0,1:T(8,128)S(1)}, f32[8192,16]{0,1:T(8,128)}, u32[]{:S(2)}) copy-start(f32[8192,16]{0,1:T(8,128)} %copy-done.2) | copy-start | bytes 1572868
  244.3 26.3 %copy-start.5 = (f32[8192,16]{0,1:T(8,128)}, f32[8192,16]{0,1:T(8,128)S(1)}, u32[]{:S(2)}) copy-start(f32[8192,16]{0,1:T(8,128)S(1)} %fusion.7) | copy-start | bytes 1572868
Sparse Core Ops, SparseCore 0:
  229.5 17.2 all-gather.1
where the time goes:
time: 278 us
  blocking collectives  57.7 us (21%)
  local copies, waits for them, and re-layouts  56.6 us (20%)
  other arithmetic  54.8 us (20%)
  starting transfers between devices  40.8 us (15%)
  waiting for transfers between devices  31.3 us (11%)
  matrix products  21.8 us (8%)
  between operations  14.5 us (5%)
    scatter-add x1, other arithmetic, on_device(): jax.ops.segment_sum(fine_res, fine_local, num_segments=mid_count)  44.4 us
    all_gather x1, blocking collectives, on_device(): lax.all_gather(coarse_rhs, 'rows', axis=0, tiled=True)  35.5 us
    gather x2, local copies, waits for them, and re-layouts, on_device(): fine_x = fine_x + mid_x[fine_local]  30.7 us
    ppermute x6, starting transfers between devices, with_halo(): before = lax.ppermute(last, axis, up)  29.7 us
    psum x1, blocking collectives, on_device(): gram = lax.psum(partial_gram, 'rows')  22.2 us
    dot_general x3, matrix products, fine_apply(): jnp.einsum('bkij,bkjc->bic', matrix, picked, preferred_element_type=jnp.f...  17.1 us
    ppermute x6, waiting for transfers between devices, with_halo(): before = lax.ppermute(last, axis, up)  12.5 us
    ppermute x6, waiting for transfers between devices, with_halo(): after = lax.ppermute(leading, axis, down)  10.4 us
  transfers between devices with their start and end apart: 15, of which 11 were waited for; matrix products, arithmetic and copies ran while one was open for 5% of the time, Pallas kernels for 0%

commit v1 on v0

v1 whole, which is shorter than its diff:
```python
import jax
import jax.numpy as jnp
from jax import lax
from jax.experimental import pallas as pl
from jax.experimental.pallas import tpu as pltpu
from jax.sharding import PartitionSpec as P

DAMPING = 0.6666666666666666
F32 = jnp.float32
BF16 = jnp.bfloat16
NT = (((1,), (1,)), ((), ()))
VM = pl.BlockSpec(memory_space=pltpu.VMEM)
SM = pl.BlockSpec(memory_space=pltpu.SMEM)
ANY = pl.BlockSpec(memory_space=pl.ANY)

TILES_AT, HI_AT, LO_AT, MISC_AT = 0, 640, 704, 768
MESSAGE = 832


def dot_nt(a, b):
    return lax.dot_general(a, b, NT, preferred_element_type=F32)


def eye_mask(n):
    return lax.broadcasted_iota(jnp.int32, (n, n), 0) == lax.broadcasted_iota(jnp.int32, (n, n), 1)


def diag_row(tile, eye):
    return jnp.sum(jnp.where(eye, tile.astype(F32), 0.0), axis=0, keepdims=True)


def params(mib, flops, size):
    return dict(
        compiler_params=pltpu.CompilerParams(vmem_limit_bytes=mib << 20),
        cost_estimate=pl.CostEstimate(flops=flops, bytes_accessed=size, transcendentals=0),
    )


def first_kernel(res, tiles, a_out, winv_out, held, sems):
    blocks, ext = held.shape[0], held.shape[1]
    parts = sems.shape[0]
    per = blocks // parts

    def copy(part):
        rows = pl.ds(part * per, per)
        return pltpu.make_async_copy(tiles.at[rows, 0], held.at[rows], sems.at[part])

    for part in range(parts):
        copy(part).start()
    eye = eye_mask(ext)
    for part in range(parts):
        copy(part).wait()
        for g in range(part * per, (part + 1) * per):
            winv = DAMPING * (1.0 / diag_row(held[g], eye))
            winv_out[pl.ds(g, 1), :] = winv
            a_out[g] = (winv * res[:, g * ext : (g + 1) * ext]).astype(BF16)


def fill_window(window, left, own, right):
    blocks = own.shape[0]
    window[0:blocks] = left[...]
    window[blocks : 2 * blocks] = own[...]
    window[2 * blocks : 3 * blocks] = right[...]


def fine_row(index, offset, tiles, window, g):
    slots = tiles.shape[1]
    picked = [window[index[s, g] - offset] for s in range(slots)]
    return dot_nt(
        jnp.concatenate(picked, axis=1),
        jnp.concatenate([tiles[g, s] for s in range(slots)], axis=1),
    )


def second_kernel(index, place, tiles, left, own, right, res, winv, b_out, b16_out, window):
    blocks, ext = own.shape[0], own.shape[2]
    offset = (place[0] - 1) * blocks
    fill_window(window, left, own, right)
    for g in range(blocks):
        product = fine_row(index, offset, tiles, window, g)
        w = winv[pl.ds(g, 1), :]
        r = res[:, g * ext : (g + 1) * ext]
        b = w * r + w * (r - product)
        b_out[g] = b
        b16_out[g] = b.astype(BF16)


def split(row, ext):
    return lax.shift_right_logical(row, ext.bit_length() - 1), row & (ext - 1)


def one_hot(row, n):
    ids = lax.broadcasted_iota(jnp.int32, (n, row.shape[1]), 0)
    return jnp.where(ids == row, 1.0, 0.0).astype(BF16)


def spread(value, row, n):
    return jnp.concatenate(
        [jnp.where(row == l, value, 0.0).astype(BF16) for l in range(n)], axis=0
    )


def edge(message, row, n=128):
    return message[row : row + n, :]


def as_int(row):
    return row.astype(F32).astype(jnp.int32)


def inverse(row, present):
    return DAMPING * (1.0 / jnp.where(present, row, 1.0))


def mid_inverse(mid_tiles, eye):
    return [
        DAMPING * (1.0 / diag_row(mid_tiles[b, 1], eye)) for b in range(mid_tiles.shape[0])
    ]


def mid_product(mid_tiles, v, b):
    ext = mid_tiles.shape[2]
    count = mid_tiles.shape[0]
    ks = [k for k in range(3) if v.get(b - 1 + k) is not None]
    return dot_nt(
        jnp.concatenate([v[b - 1 + k] for k in ks], axis=1),
        jnp.concatenate([mid_tiles[b, k] for k in ks], axis=1),
    )


def third_kernel(
    index, place, tiles, left, own, right, res, b_in, owner, mid_tiles, mid_owner, from_left,
    from_right, fres_out, u_out, bpart_out, send, window, spread_rows, hot,
):
    blocks, ext = own.shape[0], own.shape[2]
    width = own.shape[1]
    mids = mid_tiles.shape[0]
    me = place[0]
    peers = place[1]
    offset = (me - 1) * blocks
    fill_window(window, left, own, right)
    for g in range(blocks):
        product = fine_row(index, offset, tiles, window, g)
        r = res[:, g * ext : (g + 1) * ext] - product
        fres_out[g] = r
        lo, hi = split(owner[pl.ds(g, 1), :] - me * (mids * ext), ext)
        cols = slice(g * ext, (g + 1) * ext)
        spread_rows[:, cols] = spread(r, lo, mids)
        hot[:, cols] = one_hot(hi, ext)
    total = dot_nt(spread_rows[...], hot[...])
    u = [total[b * width : (b + 1) * width] for b in range(mids)]
    eye = eye_mask(ext)
    winv = mid_inverse(mid_tiles, eye)
    has_left, has_right = me > 0, me < peers - 1
    left_prev, left_mid, left_next = (edge(from_left, 128 * k) for k in range(3))
    left_far = edge(from_left, 384)
    right_prev, right_mid, right_next = (edge(from_right, 128 * k) for k in range(3))
    right_far = edge(from_right, 384)
    winv_left = inverse(diag_row(left_mid, eye), has_left)
    winv_right = inverse(diag_row(right_mid, eye), has_right)
    a = [winv[b] * u[b] for b in range(mids)]
    a16 = {b: a[b].astype(BF16) for b in range(mids)}
    part = {}
    for b in range(mids):
        part[b] = a[b] + winv[b] * (u[b] - mid_product(mid_tiles, a16, b))
        u_out[b] = u[b]
        bpart_out[b] = part[b]
    part[-1] = -winv_left * dot_nt(a16[0], left_next)
    part[mids] = -winv_right * dot_nt(a16[mids - 1], right_prev)
    p16 = {b: v.astype(BF16) for b, v in part.items()}
    rest = {b: u[b] - mid_product(mid_tiles, p16, b) for b in range(mids)}
    rest[-1] = -(dot_nt(p16[-1], left_mid) + dot_nt(p16[0], left_next))
    rest[-2] = -dot_nt(p16[-1], left_far)
    rest[mids] = -(dot_nt(p16[mids], right_mid) + dot_nt(p16[mids - 1], right_prev))
    rest[mids + 1] = -dot_nt(p16[mids], right_far)
    start = me - 2 + me % 2
    order = list(range(-2, mids + 2))
    spreads, hots = [], []
    for b in order:
        if b < 0:
            at = MISC_AT + 2 + b
            hi, block = as_int(from_left[at : at + 1, :]), as_int(from_left[at + 2 : at + 3, :])
        elif b >= mids:
            at = MISC_AT + b - mids
            hi, block = as_int(from_right[at : at + 1, :]), as_int(from_right[at + 2 : at + 3, :])
        else:
            block, hi = split(mid_owner[b : b + 1, :], ext)
        spreads.append(spread(rest[b], block - start, 4))
        hots.append(one_hot(hi, ext))
    coarse = dot_nt(jnp.concatenate(spreads, axis=1), jnp.concatenate(hots, axis=1))
    coarse16 = coarse.astype(BF16)
    first, last = u[0].astype(BF16), u[mids - 1].astype(BF16)
    none = jnp.zeros_like(first)
    for d in range(send.shape[0]):
        for k in range(4):
            send[d, k] = coarse16[k * width : (k + 1) * width]
        send[d, 4] = jnp.where(me + 1 == d, last, jnp.where(me - 1 == d, first, none))


def coarse_kernel(place, got, inverse_rows, mid_tiles, u, bpart, from_left, from_right, fix_out, b_out):
    ext = mid_tiles.shape[2]
    mids = mid_tiles.shape[0]
    peers = got.shape[0]
    me = place[0]
    rhs = []
    for k in range(peers):
        terms = [
            got[s, k - (s - 2 + s % 2)].astype(F32)
            for s in range(peers)
            if 0 <= k - (s - 2 + s % 2) < 4
        ]
        rhs.append(sum(terms[1:], terms[0]))
    rhs16 = jnp.concatenate([r.astype(BF16) for r in rhs], axis=1)
    fix_out[...] = dot_nt(rhs16, inverse_rows[...].astype(BF16)).astype(BF16)
    eye = eye_mask(ext)
    winv_left = inverse(diag_row(edge(from_left, 128), eye), me > 0)
    winv_right = inverse(diag_row(edge(from_right, 128), eye), me < peers - 1)
    before = got[lax.rem(me + peers - 1, peers), 4].astype(F32)
    after = got[lax.rem(me + 1, peers), 4].astype(F32)
    a_before = (winv_left * before).astype(BF16)
    a_after = (winv_right * after).astype(BF16)
    for b in range(mids):
        value = bpart[b]
        if b == 0 or b == mids - 1:
            winv = DAMPING * (1.0 / diag_row(mid_tiles[b, 1], eye))
            if b == 0:
                value = value - winv * dot_nt(a_before, mid_tiles[b, 0])
            if b == mids - 1:
                value = value - winv * dot_nt(a_after, mid_tiles[b, 2])
        b_out[b] = value


def mid_kernel(place, fix, partner, mid_tiles, mid_owner, u, b_in, dpart_out, edges_out, send):
    ext = mid_tiles.shape[2]
    width = fix.shape[0]
    mids = mid_tiles.shape[0]
    me = place[0]
    odd = me % 2
    mine, other = fix[...], partner[...]
    pair = jnp.concatenate(
        [jnp.where(odd == 0, mine, other), jnp.where(odd == 0, other, mine)], axis=0
    )
    eye = eye_mask(ext)
    winv = mid_inverse(mid_tiles, eye)
    c, c16 = {}, {}
    for b in range(mids):
        block, hi = split(mid_owner[b : b + 1, :], ext)
        both = jnp.dot(pair, one_hot(hi, ext), preferred_element_type=F32)
        c[b] = b_in[b] + jnp.where(block - (me - odd) == 0, both[:width], both[width:])
        c16[b] = c[b].astype(BF16)
    d16 = []
    for b in range(mids):
        d = c[b] + winv[b] * (u[b] - mid_product(mid_tiles, c16, b))
        dpart_out[b] = d
        d16.append(d.astype(BF16))
    edges_out[0] = c16[0]
    edges_out[1] = c16[mids - 1]
    none = jnp.zeros_like(c16[0])
    for t in range(send.shape[0]):
        for b in range(mids):
            send[t, b] = d16[b]
        ahead = jnp.logical_or(me + 1 == t, me + 2 == t)
        behind = jnp.logical_or(me - 1 == t, me - 2 == t)
        send[t, mids] = jnp.where(ahead, c16[mids - 1], jnp.where(behind, c16[0], none))


def prolong(values, hi, lo, width, mids, ext):
    both = jnp.dot(values, one_hot(hi, ext), preferred_element_type=F32)
    result = jnp.where(lo == 0, both[:width], 0.0)
    for l in range(1, mids):
        result = jnp.where(lo == l, both[l * width : (l + 1) * width], result)
    return result


def last_kernel(
    index, place, tiles, got, dpart, c_edges, mid_tiles, owner, from_left, from_right, b_in, fres, winv,
    basis, out, gram_out, window, added, rounded,
):
    blocks, width, ext = b_in.shape
    mids = mid_tiles.shape[0]
    peers = got.shape[0]
    me = place[0]
    at = lambda shift: lax.rem(me + shift + peers, peers)
    eye = eye_mask(ext)
    left, right, far_left, far_right = (at(k) for k in (-1, 1, -2, 2))
    has_left, has_right = me > 0, me < peers - 1
    minv = lambda b: DAMPING * (1.0 / diag_row(mid_tiles[b, 1], eye))
    own = [dpart[b] for b in range(mids)]
    own[0] = own[0] - minv(0) * dot_nt(got[left, mids], mid_tiles[0, 0])
    own[-1] = own[-1] - minv(mids - 1) * dot_nt(got[right, mids], mid_tiles[mids - 1, 2])
    lefts = [got[left, b].astype(F32) for b in range(mids)]
    lefts[0] = lefts[0] - inverse(
        from_left[MISC_AT + 4 : MISC_AT + 5, :].astype(F32), has_left
    ) * dot_nt(got[far_left, mids], edge(from_left, 512))
    lefts[-1] = lefts[-1] - inverse(diag_row(edge(from_left, 128), eye), has_left) * dot_nt(
        c_edges[0], edge(from_left, 256)
    )
    rights = [got[right, b].astype(F32) for b in range(mids)]
    rights[0] = rights[0] - inverse(diag_row(edge(from_right, 128), eye), has_right) * dot_nt(
        c_edges[1], edge(from_right, 0)
    )
    rights[-1] = rights[-1] - inverse(
        from_right[MISC_AT + 4 : MISC_AT + 5, :].astype(F32), has_right
    ) * dot_nt(got[far_right, mids], edge(from_right, 512))
    own16, left16, right16 = (
        jnp.concatenate([v.astype(BF16) for v in side], axis=0) for side in (own, lefts, rights)
    )
    for g in range(blocks):
        lo, hi = split(owner[pl.ds(g, 1), :] - me * (mids * ext), ext)
        value = prolong(own16, hi, lo, width, mids, ext)
        added[g] = value
        window[blocks + g] = value.astype(BF16)
        for message, values, base in ((from_left, left16, 0), (from_right, right16, 2 * blocks)):
            hi = as_int(message[HI_AT + g : HI_AT + g + 1, :])
            lo = as_int(message[LO_AT + g : LO_AT + g + 1, :])
            window[base + g] = prolong(values, hi, lo, width, mids, ext).astype(BF16)
    offset = (me - 1) * blocks
    for g in range(blocks):
        product = fine_row(index, offset, tiles, window, g)
        value = b_in[g] + added[g] + winv[pl.ds(g, 1), :] * (fres[g] - product)
        cols = slice(g * ext, (g + 1) * ext)
        out[:, cols] = value
        rounded[:, cols] = value.astype(BF16)
    gram = dot_nt(rounded[...], basis[...])
    for d in range(gram_out.shape[0]):
        gram_out[d] = gram


def halo(value):
    peers = lax.axis_size("rows")
    odd = [(i, i + 1) for i in range(1, peers - 1, 2)]
    even = [(i, i + 1) for i in range(0, peers - 1, 2)]
    swap = lambda pairs: pairs + [(j, i) for i, j in pairs]
    far = lax.ppermute(value, "rows", swap(odd))
    near = lax.ppermute(value, "rows", swap(even))
    return near, far


def shifted(value):
    peers = lax.axis_size("rows")
    up = [(i, i + 1) for i in range(peers - 1)]
    down = [(j, i) for i, j in up]
    return up, down


def on_device(
    residual_block, basis, fine_tiles, fine_index, mid_tiles, fine_owner, mid_owner, coarse_inverse
):
    peers = lax.axis_size("rows")
    me = lax.axis_index("rows")
    blocks, slots, ext, _ = fine_tiles.shape
    mids = mid_tiles.shape[0]
    count = blocks * ext
    width = residual_block.shape[1]
    res = residual_block.T
    index = fine_index.T
    place = jnp.stack([me, jnp.int32(peers)])
    owner = fine_owner.reshape(blocks, ext)
    mid_rows = mid_owner.reshape(mids, ext)
    shape = jax.ShapeDtypeStruct
    tile_bytes = fine_tiles.size * 2
    fine_flops = 2 * fine_tiles.size * width

    hi = (owner % ext).astype(BF16)
    lo = (owner // ext - me * mids).astype(BF16)
    mid_hi = (mid_rows % ext).astype(BF16)
    mid_block = (mid_rows // ext).astype(BF16)
    diag = lambda b: jnp.diagonal(mid_tiles[b, 1])[None]

    def message(picks, pair, far):
        rows = [mid_tiles[b, k] for b, k in picks] + [hi, lo]
        rows += [mid_hi[pair[0] : pair[1]], mid_block[pair[0] : pair[1]], diag(far)]
        filled = MISC_AT + 5
        rows.append(jnp.zeros((MESSAGE - filled, ext), BF16))
        return jnp.concatenate(rows, axis=0)

    last = mids - 1
    to_right = message(
        [(last, 0), (last, 1), (last, 2), (last - 1, 2), (0, 0)], (last - 1, last + 1), 0
    )
    to_left = message([(0, 0), (0, 1), (0, 2), (1, 0), (last, 2)], (0, 2), last)
    shares = lax.axis_size("cols")
    share = MESSAGE // shares
    begin = lax.axis_index("cols") * share
    up, down = shifted(res)
    from_left = lax.ppermute(lax.dynamic_slice_in_dim(to_right, begin, share), "rows", up)
    from_right = lax.ppermute(lax.dynamic_slice_in_dim(to_left, begin, share), "rows", down)
    both = lax.all_gather(jnp.stack([from_left, from_right]), "cols", axis=1, tiled=True)
    from_left, from_right = both[0], both[1]
    all_basis = lax.all_gather(basis.T, "cols", axis=0, tiled=True)

    a16, winv = pl.pallas_call(
        first_kernel,
        in_specs=[VM, ANY],
        out_specs=[VM, VM],
        out_shape=[shape((blocks, width, ext), BF16), shape((blocks, ext), F32)],
        scratch_shapes=[pltpu.VMEM((blocks, ext, ext), BF16), pltpu.SemaphoreType.DMA((4,))],
        name="first_smoothing",
        **params(8, count * ext, tile_bytes // 4),
    )(res, fine_tiles)

    odd = me % 2

    def sides(value):
        near, far = halo(value)
        return (
            jnp.where(odd == 1, near, far),
            jnp.where(odd == 1, far, near),
        )

    left, right = sides(a16)
    b32, b16 = pl.pallas_call(
        second_kernel,
        in_specs=[SM, SM] + [VM] * 6,
        out_specs=[VM, VM],
        out_shape=[shape((blocks, width, ext), F32), shape((blocks, width, ext), BF16)],
        scratch_shapes=[pltpu.VMEM((3 * blocks, width, ext), BF16)],
        name="second_smoothing",
        **params(12, fine_flops, tile_bytes),
    )(index, place, fine_tiles, left, a16, right, res, winv)

    left, right = sides(b16)
    fres, u, bpart, send = pl.pallas_call(
        third_kernel,
        in_specs=[SM, SM] + [VM] * 11,
        out_specs=[VM] * 4,
        out_shape=[
            shape((blocks, width, ext), F32),
            shape((mids, width, ext), F32),
            shape((mids, width, ext), F32),
            shape((peers, 5, width, ext), BF16),
        ],
        scratch_shapes=[
            pltpu.VMEM((3 * blocks, width, ext), BF16),
            pltpu.VMEM((mids * width, count), BF16),
            pltpu.VMEM((ext, count), BF16),
        ],
        name="residual_and_restriction",
        **params(20, fine_flops, tile_bytes),
    )(
        index, place, fine_tiles, left, b16, right, res, b32, owner, mid_tiles, mid_rows,
        from_left, from_right,
    )

    got = lax.all_to_all(send, "rows", 0, 0)
    fix, mid_b = pl.pallas_call(
        coarse_kernel,
        in_specs=[SM] + [VM] * 7,
        out_specs=[VM, VM],
        out_shape=[shape((width, ext), BF16), shape((mids, width, ext), F32)],
        name="coarse_product",
        **params(16, 2 * width * coarse_inverse.size, coarse_inverse.size * 4),
    )(place, got, coarse_inverse, mid_tiles, u, bpart, from_left, from_right)

    partner = lax.ppermute(fix, "rows", [(i, i ^ 1) for i in range(peers)])
    dpart, c_edges, send = pl.pallas_call(
        mid_kernel,
        in_specs=[SM] + [VM] * 6,
        out_specs=[VM] * 3,
        out_shape=[
            shape((mids, width, ext), F32),
            shape((2, width, ext), BF16),
            shape((peers, mids + 1, width, ext), BF16),
        ],
        name="mid_level",
        **params(12, 2 * width * mid_tiles.size, mid_tiles.size * 2),
    )(place, fix, partner, mid_tiles, mid_rows, u, mid_b)

    return finish(
        place, index, fine_tiles, send, dpart, c_edges, mid_tiles, owner, from_left, from_right,
        b32, fres, winv, all_basis,
    )


def finish(
    place, index, fine_tiles, send, dpart, c_edges, mid_tiles, owner, from_left, from_right, b32,
    fres, winv, all_basis,
):
    peers = lax.axis_size("rows")
    blocks, width, ext = b32.shape
    mids = mid_tiles.shape[0]
    count = blocks * ext
    shape = jax.ShapeDtypeStruct
    got = lax.all_to_all(send, "rows", 0, 0)
    out, grams = pl.pallas_call(
        last_kernel,
        in_specs=[SM, SM] + [VM] * 12,
        out_specs=[VM, VM],
        out_shape=[
            shape((width, count), F32),
            shape((peers, width, all_basis.shape[0]), F32),
        ],
        scratch_shapes=[
            pltpu.VMEM((3 * blocks, width, ext), BF16),
            pltpu.VMEM((blocks, width, ext), F32),
            pltpu.VMEM((width, count), BF16),
        ],
        name="prolongation_and_last_smoothing",
        **params(16, 2 * fine_tiles.size * width, fine_tiles.size * 2),
    )(
        index, place, fine_tiles, got, dpart, c_edges, mid_tiles, owner, from_left, from_right,
        b32, fres, winv, all_basis,
    )
    gram = jnp.sum(lax.all_to_all(grams, "rows", 0, 0), axis=0)
    return out.T, gram.T


def solution(mesh):
    in_specs = (
        P("rows", "cols"),
        P("rows", "cols"),
        P("rows", None, None, None),
        P("rows", None),
        P("rows", None, None, None),
        P("rows"),
        P("rows"),
        P("rows", None),
    )
    out_specs = (P("rows", "cols"), P(None, "cols"))
    return jax.shard_map(
        on_device, mesh=mesh, in_specs=in_specs, out_specs=out_specs, check_vma=False
    )
```

time: 278 us -> 115 us (0.41)
  other arithmetic: 54.8 us -> 1.56 us
  local copies, waits for them, and re-layouts: 56.6 us -> 17 us
  starting transfers between devices: 40.8 us -> 13 us
  matrix products: 21.8 us -> 0 us
  waiting for transfers between devices: 31.3 us -> 9.93 us
  Pallas kernels: 0 us -> 18 us
  blocking collectives: 57.7 us -> 40.8 us
    scatter-add x2 -> x0, other arithmetic: 50.9 us -> none  [the longest x1 44.4 us: on_device(): jax.ops.segment_sum(fine_res, fine_local, num_segments=mid_count)]
    gather x10 -> x2, local copies, waits for them, and re-layouts: 42.4 us -> 3.01 us  [on_device(): diag = lambda b: jnp.diagonal(mid_tiles[b, 1])[None]]
    all_to_all x0 -> x3, blocking collectives: none -> 33.8 us  [the longest x1 13.5 us: on_device(): got = lax.all_to_all(send, 'rows', 0, 0)]
    all_gather x1, blocking collectives: 35.5 us -> 7.01 us  [on_device(): lax.all_gather(jnp.stack([from_left, from_right]), 'cols', axis=1, tiled=...]
    ppermute x14 -> x7, starting transfers between devices: 40.7 us -> 13 us  [the longest x1 6.18 us: on_device(): lax.ppermute(lax.dynamic_slice_in_dim(to_right, begin, share), 'rows', up)]
    psum x1 -> x0, blocking collectives: 22.2 us -> none  [on_device(): gram = lax.psum(partial_gram, 'rows')]
    dot_general x14 -> x0, matrix products: 21.8 us -> none  [the longest x3 17.1 us: fine_apply(): jnp.einsum('bkij,bkjc->bic', matrix, picked, preferred_element_type=jnp.f...]
    ppermute x14 -> x7, waiting for transfers between devices: 28.8 us -> 9.91 us  [the longest x1 4.49 us: on_device(): lax.ppermute(lax.dynamic_slice_in_dim(to_left, begin, share), 'rows', down)]
  transfers between devices with their start and end apart: 15 -> 8, of which waited for: 11 -> 4; matrix products, arithmetic and copies ran while one was open for 5% -> 3% of each run, Pallas kernels for 0% -> 9%
where the time goes in v1:
time: 115 us
  blocking collectives  40.8 us (35%)
  Pallas kernels  18 us (16%)
  local copies, waits for them, and re-layouts  17 us (15%)
  between operations  14.3 us (12%)
  starting transfers between devices  13 us (11%)
  waiting for transfers between devices  9.93 us (9%)
  other arithmetic  1.56 us (1%)
    all_to_all x1, blocking collectives, on_device(): got = lax.all_to_all(send, 'rows', 0, 0)  13.5 us
    unnamed x26, local copies, waits for them, and re-layouts  12.7 us
    all_to_all x1, blocking collectives, finish(): got = lax.all_to_all(send, 'rows', 0, 0)  11.2 us
    all_to_all x1, blocking collectives, finish(): gram = jnp.sum(lax.all_to_all(grams, 'rows', 0, 0), axis=0)  9.13 us
    pallas_call x1, Pallas kernels, finish(): pl.pallas_call(last_kernel, in_specs=[SM, SM] + [VM] * 12, out_specs=[VM,...  7.13 us
    all_gather x1, blocking collectives, on_device(): lax.all_gather(jnp.stack([from_left, from_right]), 'cols', axis=1, tiled=...  7.01 us
    ppermute x1, starting transfers between devices, on_device(): lax.ppermute(lax.dynamic_slice_in_dim(to_right, begin, share), 'rows', up)  6.18 us
    pallas_call x1, Pallas kernels, on_device(): pl.pallas_call(third_kernel, in_specs=[SM, SM] + [VM] * 11, out_specs=[VM...  5.49 us
  transfers between devices with their start and end apart: 8, of which 4 were waited for; matrix products, arithmetic and copies ran while one was open for 3% of the time, Pallas kernels for 9%

profile of v1, /device:TPU:0, one launch (start us, length us, event | category | flops | bytes accessed | tf_op | source)
XLA Modules:
  0.0 114.6 jit_solution(314349553392302877)
XLA Ops:
  7.2 0.0 all-gather.2.cloned.1.call-start
  7.2 0.0 copy-start
  7.2 3.4 %copy-done = bf16[64,4,128,128]{3,2,1,0:T(8,128)(2,1)S(1)} copy-done((bf16[64,4,128,128]{3,2,1,0:T(8,128)(2,1)S(1)}, bf16[64,4,128,128]{3,2,1,0:T(8,128)(2,1)}, u32[]{:S(2)}) %copy-start) | copy-done | bytes 8388632
  10.6 1.0 copy-done.5
  11.6 0.0 copy-start.11
  11.7 0.8 first_smoothing.1
  12.4 3.0 %collective-permute-start = (bf16[64,16,128]{2,1,0:T(8,128)(2,1)S(1)}, bf16[64,16,128]{2,1,0:T(8,128)(2,1)S(1)}, u32[]{:S(2)}, u32[]{:S(2)}) collective-permute-start(bf16[64,16,128]{2,1,0:T(8,128)(2,1)S(1)} %get-tuple-element.17.own), channel_id=1, source_target_pairs={{0,4},{8,12},{16,20},{24,28},{4,0},{12,8},{20,16},{28,24},{1,5},{9... | collective-permute-start | bytes 786440 | tf_op jit(solution)/shard_map/ppermute | solution.py:335
  15.5 0.7 collective-permute-start.1
  16.1 0.0 copy-done.4
  16.2 0.0 copy-done.10
  16.2 1.5 %gather_fusion = bf16[128]{0:T(256)(128)(2,1)S(1)} fusion(bf16[128,128]{1,0:T(8,128)(2,1)S(1)} %get-tuple-element.35, s32[128]{0:T(128)S(1)} %or_bitcast_fusion), kind=kCustom, calls=%fused_computation | custom fusion | bytes 1536 | tf_op jit(solution)/shard_map/jit(diagonal)/cond/branch_0_fun/gather | solution.py:368
  17.8 0.3 concatenate.12
  18.2 6.2 %collective-permute-start.4 = (bf16[208,128]{1,0:T(8,128)(2,1)S(1)}, bf16[208,128]{1,0:T(8,128)(2,1)S(1)}, u32[]{:S(2)}, u32[]{:S(2)}) collective-permute-start(bf16[208,128]{1,0:T(8,128)(2,1)S(1)} %constant_dynamic-slice_fusion.1), channel_id=1, source_target_pairs={{0,4},{4,8},{8,12},{12,16},{16,20},{20,24},{24,28},{1,5},{5,9},{9,... | collective-permute-start | bytes 159752 | tf_op jit(solution)/shard_map/ppermute | solution.py:386
  24.4 1.5 %gather_fusion.1 = bf16[128]{0:T(256)(128)(2,1)S(1)} fusion(bf16[128,128]{1,0:T(8,128)(2,1)S(1)} %get-tuple-element.38, s32[128]{0:T(128)S(1)} %or_bitcast_fusion), kind=kCustom, calls=%fused_computation.1 | custom fusion | bytes 1536 | tf_op jit(solution)/shard_map/jit(diagonal)/cond/branch_0_fun/gather | solution.py:368
  25.9 0.3 concatenate.13
  26.2 1.3 %collective-permute-start.5 = (bf16[208,128]{1,0:T(8,128)(2,1)S(1)}, bf16[208,128]{1,0:T(8,128)(2,1)S(1)}, u32[]{:S(2)}, u32[]{:S(2)}) collective-permute-start(bf16[208,128]{1,0:T(8,128)(2,1)S(1)} %constant_dynamic-slice_fusion), channel_id=1, source_target_pairs={{4,0},{8,4},{12,8},{16,12},{20,16},{24,20},{28,24},{5,1},{9,5},{13... | collective-permute-start | bytes 159752 | tf_op jit(solution)/shard_map/ppermute | solution.py:387
  27.5 0.0 all-gather.2.cloned.1.call-update
  27.6 0.1 pad_add_fusion.place
  27.6 0.1 collective-permute-done.4
  27.8 4.5 %collective-permute-done.5 = bf16[208,128]{1,0:T(8,128)(2,1)S(1)} collective-permute-done((bf16[208,128]{1,0:T(8,128)(2,1)S(1)}, bf16[208,128]{1,0:T(8,128)(2,1)S(1)}, u32[]{:S(2)}, u32[]{:S(2)}) %collective-permute-start.5) | collective-permute-done | bytes 53280 | tf_op jit(solution)/shard_map/ppermute | solution.py:387
  32.3 0.0 collective-permute-done
  32.3 0.0 collective-permute-done.1
  32.4 0.0 copy-start.1
  32.4 3.5 %copy-done.1 = bf16[64,4,128,128]{3,2,1,0:T(8,128)(2,1)S(1)} copy-done((bf16[64,4,128,128]{3,2,1,0:T(8,128)(2,1)S(1)}, bf16[64,4,128,128]{3,2,1,0:T(8,128)(2,1)}, u32[]{:S(2)}) %copy-start.1) | copy-done | bytes 8388632
  35.9 2.9 %second_smoothing.1 = (f32[64,16,128]{2,1,0:T(8,128)S(1)}, bf16[64,16,128]{2,1,0:T(8,128)(2,1)S(1)}) custom-call(s32[4,64]{1,0:T(4,128)S(1)} %bitcast.45, s32[2]{0:T(128)S(1)} %pad_add_fusion.place, bf16[64,4,128,128]{3,2,1,0:T(8,128)(2,1)S(1)} %copy-done.1, bf16[64,16,128]{2,1,0:T(8,128)(2,1)S(1)} %get-tuple-element.43.left, ...), custom_call_target="tpu_custom_call" | custom-call | flops 134217728 | bytes 8388608 | tf_op jit(solution)/shard_map/second_smoothing/pallas_call | solution.py:412
  38.8 0.0 copy-start.8
  38.8 1.0 collective-permute-start.2
  39.8 0.7 collective-permute-start.3
  40.5 7.0 %all_gather.6 = bf16[2,832,128]{2,1,0:T(8,128)(2,1)S(1)} all-gather(bf16[2,208,128]{2,1,0:T(8,128)(2,1)S(1)} %pad_maximum_fusion), channel_id=1, replica_groups=mesh['rows'=8,'cols'=4] {'cols'}, dimensions={1}, use_global_device_ids=true | all-gather | bytes 532480 | tf_op jit(solution)/shard_map/all_gather | solution.py:388
  47.5 1.8 %collective-permute-done.2 = bf16[64,16,128]{2,1,0:T(8,128)(2,1)S(1)} collective-permute-done((bf16[64,16,128]{2,1,0:T(8,128)(2,1)S(1)}, bf16[64,16,128]{2,1,0:T(8,128)(2,1)S(1)}, u32[]{:S(2)}, u32[]{:S(2)}) %collective-permute-start.2) | collective-permute-done | bytes 262176 | tf_op jit(solution)/shard_map/ppermute | solution.py:335
  49.3 0.0 collective-permute-done.3
  49.3 0.0 copy-done.2
  49.3 5.5 %residual_and_restriction.1 = (f32[64,16,128]{2,1,0:T(8,128)S(1)}, f32[8,16,128]{2,1,0:T(8,128)S(1)}, f32[8,16,128]{2,1,0:T(8,128)S(1)}, bf16[8,5,16,128]{3,2,1,0:T(8,128)(2,1)S(1)}) custom-call(s32[4,64]{1,0:T(4,128)S(1)} %bitcast.46, s32[2]{0:T(128)S(1)} %pad_add_fusion.place, bf16[64,4,128,128]{3,2,1,0:T(8,128)(2,1)S(1)} %copy-done.2, ...), custom_call_target="tpu_custom_call" | custom-call | flops 134217728 | bytes 8388608 | tf_op jit(solution)/shard_map/residual_and_restriction/pallas_call | solution.py:423
  54.8 13.5 %all_to_all.15.got = bf16[8,5,16,128]{3,2,1,0:T(8,128)(2,1)S(1)} all-to-all(bf16[8,5,16,128]{3,2,1,0:T(8,128)(2,1)S(1)} %get-tuple-element.21), channel_id=1, replica_groups=mesh['rows'=8,'cols'=4] {'rows'}, dimensions={0} | all-to-all | bytes 327680 | tf_op jit(solution)/shard_map/all_to_all | solution.py:445
  68.3 0.8 coarse_product.1
  69.1 0.2 collective-permute-start.6
  69.2 3.5 %collective-permute-done.6.partner = bf16[16,128]{1,0:T(8,128)(2,1)S(1)} collective-permute-done((bf16[16,128]{1,0:T(8,128)(2,1)S(1)}, bf16[16,128]{1,0:T(8,128)(2,1)S(1)}, u32[]{:S(2)}, u32[]{:S(2)}) %collective-permute-start.6) | collective-permute-done | bytes 4128 | tf_op jit(solution)/shard_map/ppermute | solution.py:455
  72.7 1.0 mid_level.1
  73.7 11.2 %all_to_all.16.got = bf16[8,9,16,128]{3,2,1,0:T(8,128)(2,1)S(1)} all-to-all(bf16[8,9,16,128]{3,2,1,0:T(8,128)(2,1)S(1)} %get-tuple-element.26), channel_id=1, replica_groups=mesh['rows'=8,'cols'=4] {'rows'}, dimensions={0} | all-to-all | bytes 589824 | tf_op jit(solution)/shard_map/all_to_all | solution.py:484
  84.9 3.4 %copy-done.3 = bf16[64,4,128,128]{3,2,1,0:T(8,128)(2,1)S(1)} copy-done((bf16[64,4,128,128]{3,2,1,0:T(8,128)(2,1)S(1)}, bf16[64,4,128,128]{3,2,1,0:T(8,128)(2,1)}, u32[]{:S(2)}) %copy-start.3) | copy-done | bytes 8388632
  88.3 1.2 %copy-done.7 = bf16[64,8192]{1,0:T(8,128)(2,1)S(1)} copy-done((bf16[64,8192]{1,0:T(8,128)(2,1)S(1)}, bf16[64,8192]{1,0:T(8,128)(2,1)}, u32[]{:S(2)}) %copy-start.7) | copy-done | bytes 1048600
  89.5 7.1 %prolongation_and_last_smoothing.1 = (f32[16,8192]{1,0:T(8,128)}, f32[8,16,64]{2,1,0:T(8,128)S(1)}) custom-call(s32[4,64]{1,0:T(4,128)S(1)} %bitcast.47, s32[2]{0:T(128)S(1)} %pad_add_fusion.place, bf16[64,4,128,128]{3,2,1,0:T(8,128)(2,1)S(1)} %copy-done.3, bf16[8,9,16,128]{3,2,1,0:T(8,128)(2,1)S(1)} %all_to_all.16.got, ...), custom_call_target="tpu_custom_call" | custom-call | flops 134217728 | bytes 8388608 | tf_op jit(solution)/shard_map/prolongation_and_last_smoothing/pallas_call | solution.py:485
  96.6 0.1 reshape.24
  96.7 9.1 %all_to_all.17 = f32[8,1,1024]{2,1,0:T(1,128)S(1)} all-to-all(f32[8,1,1024]{2,1,0:T(1,128)S(1)} %reshape.24), channel_id=1, replica_groups=mesh['rows'=8,'cols'=4] {'rows'}, dimensions={0} | all-to-all | bytes 65536 | tf_op jit(solution)/shard_map/all_to_all | solution.py:504
  105.9 0.5 broadcast.77
  106.4 0.7 reduce
  107.1 0.1 reshape.25
  107.2 0.6 reduce_sum.9
  (25 shorter events, 0.3 us)
Async XLA Ops:
  7.2 77.7 %all-gather.2.cloned.1.call-start = ((), (), s32[]{:S(2)}) async-start(), calls=%async_computation.3 | async-start | bytes 1310720 | tf_op jit(solution)/shard_map/all_gather | solution.py:390
  7.2 3.4 %copy-start = (bf16[64,4,128,128]{3,2,1,0:T(8,128)(2,1)S(1)}, bf16[64,4,128,128]{3,2,1,0:T(8,128)(2,1)}, u32[]{:S(2)}) copy-start(bf16[64,4,128,128]{3,2,1,0:T(8,128)(2,1)} %tiles.7) | copy-start | bytes 25165828
  10.6 1.0 copy-start.5
  11.6 4.5 %copy-start.4 = (bf16[8,3,128,128]{3,2,1,0:T(8,128)(2,1)S(1)}, bf16[8,3,128,128]{3,2,1,0:T(8,128)(2,1)}, u32[]{:S(2)}) copy-start(bf16[8,3,128,128]{3,2,1,0:T(8,128)(2,1)} %mid_tiles.7) | copy-start | bytes 2359300
  11.6 4.6 %copy-start.10 = (s32[1024]{0:T(1024)S(1)}, s32[1024]{0:T(1024)}, u32[]{:S(2)}) copy-start(s32[1024]{0:T(1024)} %param.14) | copy-start | bytes 12292
  11.6 6.1 %copy-start.9 = (s32[8192]{0:T(1024)S(1)}, s32[8192]{0:T(1024)}, u32[]{:S(2)}) copy-start(s32[8192]{0:T(1024)} %param.13) | copy-start | bytes 98308
  11.6 20.7 %copy-start.6 = (f32[8192,16]{0,1:T(8,128)S(1)}, f32[8192,16]{0,1:T(8,128)}, u32[]{:S(2)}) copy-start(f32[8192,16]{0,1:T(8,128)} %param.8) | copy-start | bytes 1572868
  11.6 20.7 %copy-start.11 = (s32[64,4]{0,1:T(4,128)S(1)}, s32[64,4]{0,1:T(4,128)}, u32[]{:S(2)}) copy-start(s32[64,4]{0,1:T(4,128)} %param.11) | copy-start | bytes 3076
  12.4 19.9 %collective-permute-start = (bf16[64,16,128]{2,1,0:T(8,128)(2,1)S(1)}, bf16[64,16,128]{2,1,0:T(8,128)(2,1)S(1)}, u32[]{:S(2)}, u32[]{:S(2)}) collective-permute-start(bf16[64,16,128]{2,1,0:T(8,128)(2,1)S(1)} %get-tuple-element.17.own), channel_id=1, source_target_pairs={{0,4},{8,12},{16,20},{24,28},{4,0},{12,8},{20,16},{28,24},{1,5},{9... | collective-permute-start | bytes 786440 | tf_op jit(solution)/shard_map/ppermute | solution.py:335
  15.5 16.8 %collective-permute-start.1 = (bf16[64,16,128]{2,1,0:T(8,128)(2,1)S(1)}, bf16[64,16,128]{2,1,0:T(8,128)(2,1)S(1)}, u32[]{:S(2)}, u32[]{:S(2)}) collective-permute-start(bf16[64,16,128]{2,1,0:T(8,128)(2,1)S(1)} %get-tuple-element.17.own), channel_id=1, source_target_pairs={{4,8},{12,16},{20,24},{8,4},{16,12},{24,20},{5,9},{13,17},{21,25},... | collective-permute-start | bytes 786440 | tf_op jit(solution)/shard_map/ppermute | solution.py:334
  18.2 9.6 %collective-permute-start.4 = (bf16[208,128]{1,0:T(8,128)(2,1)S(1)}, bf16[208,128]{1,0:T(8,128)(2,1)S(1)}, u32[]{:S(2)}, u32[]{:S(2)}) collective-permute-start(bf16[208,128]{1,0:T(8,128)(2,1)S(1)} %constant_dynamic-slice_fusion.1), channel_id=1, source_target_pairs={{0,4},{4,8},{8,12},{12,16},{16,20},{20,24},{24,28},{1,5},{5,9},{9,... | collective-permute-start | bytes 159752 | tf_op jit(solution)/shard_map/ppermute | solution.py:386
  26.2 6.0 %collective-permute-start.5 = (bf16[208,128]{1,0:T(8,128)(2,1)S(1)}, bf16[208,128]{1,0:T(8,128)(2,1)S(1)}, u32[]{:S(2)}, u32[]{:S(2)}) collective-permute-start(bf16[208,128]{1,0:T(8,128)(2,1)S(1)} %constant_dynamic-slice_fusion), channel_id=1, source_target_pairs={{4,0},{8,4},{12,8},{16,12},{20,16},{24,20},{28,24},{5,1},{9,5},{13... | collective-permute-start | bytes 159752 | tf_op jit(solution)/shard_map/ppermute | solution.py:387
  32.4 3.5 %copy-start.1 = (bf16[64,4,128,128]{3,2,1,0:T(8,128)(2,1)S(1)}, bf16[64,4,128,128]{3,2,1,0:T(8,128)(2,1)}, u32[]{:S(2)}) copy-start(bf16[64,4,128,128]{3,2,1,0:T(8,128)(2,1)} %tiles.7) | copy-start | bytes 25165828
  35.9 13.5 %copy-start.2 = (bf16[64,4,128,128]{3,2,1,0:T(8,128)(2,1)S(1)}, bf16[64,4,128,128]{3,2,1,0:T(8,128)(2,1)}, u32[]{:S(2)}) copy-start(bf16[64,4,128,128]{3,2,1,0:T(8,128)(2,1)} %tiles.7) | copy-start | bytes 25165828
  38.8 29.5 %copy-start.8 = (f32[128,1024]{1,0:T(8,128)S(1)}, f32[128,1024]{1,0:T(8,128)}, u32[]{:S(2)}) copy-start(f32[128,1024]{1,0:T(8,128)} %inverse_rows.1) | copy-start | bytes 1572868
  38.8 10.5 %collective-permute-start.2 = (bf16[64,16,128]{2,1,0:T(8,128)(2,1)S(1)}, bf16[64,16,128]{2,1,0:T(8,128)(2,1)S(1)}, u32[]{:S(2)}, u32[]{:S(2)}) collective-permute-start(bf16[64,16,128]{2,1,0:T(8,128)(2,1)S(1)} %get-tuple-element.19.own), channel_id=1, source_target_pairs={{0,4},{8,12},{16,20},{24,28},{4,0},{12,8},{20,16},{28,24},{1,5},{9... | collective-permute-start | bytes 786440 | tf_op jit(solution)/shard_map/ppermute | solution.py:335
  39.8 9.5 %collective-permute-start.3 = (bf16[64,16,128]{2,1,0:T(8,128)(2,1)S(1)}, bf16[64,16,128]{2,1,0:T(8,128)(2,1)S(1)}, u32[]{:S(2)}, u32[]{:S(2)}) collective-permute-start(bf16[64,16,128]{2,1,0:T(8,128)(2,1)S(1)} %get-tuple-element.19.own), channel_id=1, source_target_pairs={{4,8},{12,16},{20,24},{8,4},{16,12},{24,20},{5,9},{13,17},{21,25},... | collective-permute-start | bytes 786440 | tf_op jit(solution)/shard_map/ppermute | solution.py:334
  69.1 3.6 %collective-permute-start.6 = (bf16[16,128]{1,0:T(8,128)(2,1)S(1)}, bf16[16,128]{1,0:T(8,128)(2,1)S(1)}, u32[]{:S(2)}, u32[]{:S(2)}) collective-permute-start(bf16[16,128]{1,0:T(8,128)(2,1)S(1)} %get-tuple-element.24.fix), channel_id=1, source_target_pairs={{0,4},{4,0},{8,12},{12,8},{16,20},{20,16},{24,28},{28,24},{1,5},{5... | collective-permute-start | bytes 12296 | tf_op jit(solution)/shard_map/ppermute | solution.py:455
  84.9 3.4 %copy-start.3 = (bf16[64,4,128,128]{3,2,1,0:T(8,128)(2,1)S(1)}, bf16[64,4,128,128]{3,2,1,0:T(8,128)(2,1)}, u32[]{:S(2)}) copy-start(bf16[64,4,128,128]{3,2,1,0:T(8,128)(2,1)} %tiles.7) | copy-start | bytes 25165828
  88.3 1.2 %copy-start.7 = (bf16[64,8192]{1,0:T(8,128)(2,1)S(1)}, bf16[64,8192]{1,0:T(8,128)(2,1)}, u32[]{:S(2)}) copy-start(bf16[64,8192]{1,0:T(8,128)(2,1)} %all-gather.2.cloned.1.call-done.basis) | copy-start | bytes 3145732
Sparse Core Ops, SparseCore 0:
  27.7 18.1 all-gather.1

commit v2 on v1

--- a/solution.py
+++ b/solution.py
@@ -12,9 +12,11 @@
 VM = pl.BlockSpec(memory_space=pltpu.VMEM)
 SM = pl.BlockSpec(memory_space=pltpu.SMEM)
 ANY = pl.BlockSpec(memory_space=pl.ANY)
-
-TILES_AT, HI_AT, LO_AT, MISC_AT = 0, 640, 704, 768
-MESSAGE = 832
+HBM = pl.BlockSpec(memory_space=pltpu.HBM)
+
+HI_AT, LO_AT, MISC_AT = 512, 576, 640
+MESSAGE = 704
+FIRST_LIMIT = 52
 
 
 def dot_nt(a, b):
@@ -36,31 +38,98 @@
     )
 
 
-def first_kernel(res, tiles, a_out, winv_out, held, sems):
+def first_kernel(
+    place, res, tiles, mid_tiles, owner, mid_owner, a_out, near_out, far_out, winv_out, res_out, flat,
+    held, message, sems,
+):
     blocks, ext = held.shape[0], held.shape[1]
-    parts = sems.shape[0]
+    width = a_out.shape[1]
+    parts = sems.shape[0] - 1
     per = blocks // parts
 
     def copy(part):
         rows = pl.ds(part * per, per)
         return pltpu.make_async_copy(tiles.at[rows, 0], held.at[rows], sems.at[part])
 
+    whole = pltpu.make_async_copy(res, flat, sems.at[parts])
+    whole.start()
     for part in range(parts):
         copy(part).start()
     eye = eye_mask(ext)
+
+    mids = mid_tiles.shape[0]
+    last = mids - 1
+    lo, hi = split(owner[...] - place[0] * (mids * ext), ext)
+    mid_block, mid_hi = split(mid_owner[...], ext)
+    sides = (
+        ([(last, 1), (last, 2), (last - 1, 2), (0, 0)], last - 1, 0),
+        ([(0, 1), (0, 0), (1, 0), (last, 2)], 0, last),
+    )
+    for side, (picks, first, far) in enumerate(sides):
+        for n, (b, k) in enumerate(picks):
+            message[side, n * ext : (n + 1) * ext] = mid_tiles[b, k]
+        message[side, HI_AT : HI_AT + blocks] = hi.astype(F32).astype(BF16)
+        message[side, LO_AT : LO_AT + blocks] = lo.astype(F32).astype(BF16)
+        rows = [
+            mid_hi[first : first + 2].astype(F32),
+            mid_block[first : first + 2].astype(F32),
+            diag_row(mid_tiles[far, 1], eye),
+            jnp.zeros((MESSAGE - MISC_AT - 5, ext), F32),
+        ]
+        message[side, MISC_AT:MESSAGE] = jnp.concatenate(rows, axis=0).astype(BF16)
+    extra = near_out.shape[0] - blocks
+    odd = place[0] % 2
+    for n in range(extra):
+        part = pl.ds(pl.multiple_of((place[2] * extra + n) * width, width), width)
+        near_out[blocks + n] = message[odd, part]
+        far_out[blocks + n] = message[1 - odd, part]
+
     for part in range(parts):
         copy(part).wait()
+        if part == 0:
+            whole.wait()
         for g in range(part * per, (part + 1) * per):
             winv = DAMPING * (1.0 / diag_row(held[g], eye))
             winv_out[pl.ds(g, 1), :] = winv
-            a_out[g] = (winv * res[:, g * ext : (g + 1) * ext]).astype(BF16)
-
-
-def fill_window(window, left, own, right):
+            r = flat[:, g * ext : (g + 1) * ext]
+            res_out[g] = r
+            value = (winv * r).astype(BF16)
+            a_out[g] = value
+            near_out[g] = value
+            far_out[g] = value
+
+
+def hot_kernel(after, owner, hot_out):
+    del after
+    blocks, ext = owner.shape
+    _, hi = split(owner[...], ext)
+    for g in range(blocks):
+        hot_out[:, g * ext : (g + 1) * ext] = one_hot(hi[g : g + 1, :], ext)
+
+
+def sides_kernel(place, a, b, c, d, left_out, right_out, hot_left, hot_right, buffer):
+    extra, width, ext = a.shape[1:]
+    for n, piece in enumerate((a, b, c, d)):
+        at = place[2] ^ n
+        buffer[0, at] = piece[0]
+        buffer[1, at] = piece[1]
+    for n in range(4):
+        for k in range(extra):
+            rows = slice((n * extra + k) * width, (n * extra + k + 1) * width)
+            left_out[rows] = buffer[0, n, k]
+            right_out[rows] = buffer[1, n, k]
+    blocks = hot_left.shape[1] // ext
+    for message, hot in ((left_out, hot_left), (right_out, hot_right)):
+        hi = as_int(message[HI_AT : HI_AT + blocks, :])
+        for g in range(blocks):
+            hot[:, g * ext : (g + 1) * ext] = one_hot(hi[g : g + 1, :], ext)
+
+
+def fill_window(window, near, own, far, me):
     blocks = own.shape[0]
-    window[0:blocks] = left[...]
+    window[pl.ds((1 - me % 2) * (2 * blocks), blocks)] = near[0:blocks]
     window[blocks : 2 * blocks] = own[...]
-    window[2 * blocks : 3 * blocks] = right[...]
+    window[pl.ds((me % 2) * (2 * blocks), blocks)] = far[0:blocks]
 
 
 def fine_row(index, offset, tiles, window, g):
@@ -72,17 +141,24 @@
     )
 
 
-def second_kernel(index, place, tiles, left, own, right, res, winv, b_out, b16_out, window):
+def second_kernel(
+    index, place, tiles, near, own, far, res, winv, hot, basis_b, basis_c, basis_d, b_out, b16_out,
+    mine_out, window,
+):
+    del hot, basis_b, basis_c, basis_d
     blocks, ext = own.shape[0], own.shape[2]
     offset = (place[0] - 1) * blocks
-    fill_window(window, left, own, right)
+    fill_window(window, near, own, far, place[0])
     for g in range(blocks):
         product = fine_row(index, offset, tiles, window, g)
         w = winv[pl.ds(g, 1), :]
-        r = res[:, g * ext : (g + 1) * ext]
+        r = res[g]
         b = w * r + w * (r - product)
         b_out[g] = b
         b16_out[g] = b.astype(BF16)
+    odd = place[0] % 2
+    mine_out[1 - odd] = near[blocks:]
+    mine_out[odd] = far[blocks:]
 
 
 def split(row, ext):
@@ -129,8 +205,8 @@
 
 
 def third_kernel(
-    index, place, tiles, left, own, right, res, b_in, owner, mid_tiles, mid_owner, from_left,
-    from_right, fres_out, u_out, bpart_out, send, window, spread_rows, hot,
+    index, place, tiles, near, own, far, res, owner, hot, mid_tiles, mid_owner, from_left,
+    from_right, fres_out, u_out, bpart_out, send, window, spread_rows,
 ):
     blocks, ext = own.shape[0], own.shape[2]
     width = own.shape[1]
@@ -138,24 +214,20 @@
     me = place[0]
     peers = place[1]
     offset = (me - 1) * blocks
-    fill_window(window, left, own, right)
+    fill_window(window, near, own, far, place[0])
     for g in range(blocks):
         product = fine_row(index, offset, tiles, window, g)
-        r = res[:, g * ext : (g + 1) * ext] - product
+        r = res[g] - product
         fres_out[g] = r
-        lo, hi = split(owner[pl.ds(g, 1), :] - me * (mids * ext), ext)
-        cols = slice(g * ext, (g + 1) * ext)
-        spread_rows[:, cols] = spread(r, lo, mids)
-        hot[:, cols] = one_hot(hi, ext)
+        lo, _ = split(owner[pl.ds(g, 1), :] - me * (mids * ext), ext)
+        spread_rows[:, g * ext : (g + 1) * ext] = spread(r, lo, mids)
     total = dot_nt(spread_rows[...], hot[...])
     u = [total[b * width : (b + 1) * width] for b in range(mids)]
     eye = eye_mask(ext)
     winv = mid_inverse(mid_tiles, eye)
     has_left, has_right = me > 0, me < peers - 1
-    left_prev, left_mid, left_next = (edge(from_left, 128 * k) for k in range(3))
-    left_far = edge(from_left, 384)
-    right_prev, right_mid, right_next = (edge(from_right, 128 * k) for k in range(3))
-    right_far = edge(from_right, 384)
+    left_mid, left_next, left_far = (edge(from_left, 128 * k) for k in range(3))
+    right_mid, right_prev, right_far = (edge(from_right, 128 * k) for k in range(3))
     winv_left = inverse(diag_row(left_mid, eye), has_left)
     winv_right = inverse(diag_row(right_mid, eye), has_right)
     a = [winv[b] * u[b] for b in range(mids)]
@@ -213,8 +285,8 @@
     rhs16 = jnp.concatenate([r.astype(BF16) for r in rhs], axis=1)
     fix_out[...] = dot_nt(rhs16, inverse_rows[...].astype(BF16)).astype(BF16)
     eye = eye_mask(ext)
-    winv_left = inverse(diag_row(edge(from_left, 128), eye), me > 0)
-    winv_right = inverse(diag_row(edge(from_right, 128), eye), me < peers - 1)
+    winv_left = inverse(diag_row(edge(from_left, 0), eye), me > 0)
+    winv_right = inverse(diag_row(edge(from_right, 0), eye), me < peers - 1)
     before = got[lax.rem(me + peers - 1, peers), 4].astype(F32)
     after = got[lax.rem(me + 1, peers), 4].astype(F32)
     a_before = (winv_left * before).astype(BF16)
@@ -264,8 +336,8 @@
         send[t, mids] = jnp.where(ahead, c16[mids - 1], jnp.where(behind, c16[0], none))
 
 
-def prolong(values, hi, lo, width, mids, ext):
-    both = jnp.dot(values, one_hot(hi, ext), preferred_element_type=F32)
+def prolong(values, hot, lo, width, mids):
+    both = jnp.dot(values, hot, preferred_element_type=F32)
     result = jnp.where(lo == 0, both[:width], 0.0)
     for l in range(1, mids):
         result = jnp.where(lo == l, both[l * width : (l + 1) * width], result)
@@ -273,8 +345,9 @@
 
 
 def last_kernel(
-    index, place, tiles, got, dpart, c_edges, mid_tiles, owner, from_left, from_right, b_in, fres, winv,
-    basis, out, gram_out, window, added, rounded,
+    index, place, tiles, got, dpart, c_edges, mid_tiles, owner, hot_own, from_left, hot_left,
+    from_right, hot_right, b_in, fres, winv, basis_a, basis_b, basis_c, basis_d, out, gram_out, window,
+    added, rounded, grams,
 ):
     blocks, width, ext = b_in.shape
     mids = mid_tiles.shape[0]
@@ -291,29 +364,32 @@
     lefts = [got[left, b].astype(F32) for b in range(mids)]
     lefts[0] = lefts[0] - inverse(
         from_left[MISC_AT + 4 : MISC_AT + 5, :].astype(F32), has_left
-    ) * dot_nt(got[far_left, mids], edge(from_left, 512))
-    lefts[-1] = lefts[-1] - inverse(diag_row(edge(from_left, 128), eye), has_left) * dot_nt(
-        c_edges[0], edge(from_left, 256)
+    ) * dot_nt(got[far_left, mids], edge(from_left, 384))
+    lefts[-1] = lefts[-1] - inverse(diag_row(edge(from_left, 0), eye), has_left) * dot_nt(
+        c_edges[0], edge(from_left, 128)
     )
     rights = [got[right, b].astype(F32) for b in range(mids)]
-    rights[0] = rights[0] - inverse(diag_row(edge(from_right, 128), eye), has_right) * dot_nt(
-        c_edges[1], edge(from_right, 0)
+    rights[0] = rights[0] - inverse(diag_row(edge(from_right, 0), eye), has_right) * dot_nt(
+        c_edges[1], edge(from_right, 128)
     )
     rights[-1] = rights[-1] - inverse(
         from_right[MISC_AT + 4 : MISC_AT + 5, :].astype(F32), has_right
-    ) * dot_nt(got[far_right, mids], edge(from_right, 512))
+    ) * dot_nt(got[far_right, mids], edge(from_right, 384))
     own16, left16, right16 = (
         jnp.concatenate([v.astype(BF16) for v in side], axis=0) for side in (own, lefts, rights)
     )
     for g in range(blocks):
-        lo, hi = split(owner[pl.ds(g, 1), :] - me * (mids * ext), ext)
-        value = prolong(own16, hi, lo, width, mids, ext)
+        cols = slice(g * ext, (g + 1) * ext)
+        lo, _ = split(owner[pl.ds(g, 1), :] - me * (mids * ext), ext)
+        value = prolong(own16, hot_own[:, cols], lo, width, mids)
         added[g] = value
         window[blocks + g] = value.astype(BF16)
-        for message, values, base in ((from_left, left16, 0), (from_right, right16, 2 * blocks)):
-            hi = as_int(message[HI_AT + g : HI_AT + g + 1, :])
+        for message, hot, values, base in (
+            (from_left, hot_left, left16, 0),
+            (from_right, hot_right, right16, 2 * blocks),
+        ):
             lo = as_int(message[LO_AT + g : LO_AT + g + 1, :])
-            window[base + g] = prolong(values, hi, lo, width, mids, ext).astype(BF16)
+            window[base + g] = prolong(values, hot[:, cols], lo, width, mids).astype(BF16)
     offset = (me - 1) * blocks
     for g in range(blocks):
         product = fine_row(index, offset, tiles, window, g)
@@ -321,26 +397,37 @@
         cols = slice(g * ext, (g + 1) * ext)
         out[:, cols] = value
         rounded[:, cols] = value.astype(BF16)
-    gram = dot_nt(rounded[...], basis[...])
+    for n, piece in enumerate((basis_a, basis_b, basis_c, basis_d)):
+        grams[place[2] ^ n] = dot_nt(rounded[...], piece[...])
+    gram = jnp.concatenate(
+        [grams[n] for n in range(4)] + [jnp.zeros((width, ext - 4 * width), F32)], axis=1
+    )
     for d in range(gram_out.shape[0]):
         gram_out[d] = gram
 
 
-def halo(value):
+def sum_kernel(got, out):
+    total = got[0]
+    for s in range(1, got.shape[0]):
+        total = total + got[s]
+    out[...] = total[:, : out.shape[1]]
+
+
+def halo(for_partner, for_other):
     peers = lax.axis_size("rows")
     odd = [(i, i + 1) for i in range(1, peers - 1, 2)]
     even = [(i, i + 1) for i in range(0, peers - 1, 2)]
     swap = lambda pairs: pairs + [(j, i) for i, j in pairs]
-    far = lax.ppermute(value, "rows", swap(odd))
-    near = lax.ppermute(value, "rows", swap(even))
+    near = lax.ppermute(for_partner, "rows", swap(even))
+    far = lax.ppermute(for_other, "rows", swap(odd))
     return near, far
 
 
-def shifted(value):
-    peers = lax.axis_size("rows")
-    up = [(i, i + 1) for i in range(peers - 1)]
-    down = [(j, i) for i, j in up]
-    return up, down
+def from_columns(value):
+    peers = lax.axis_size("cols")
+    return [
+        lax.ppermute(value, "cols", [(i, i ^ n) for i in range(peers)]) for n in range(1, peers)
+    ]
 
 
 def on_device(
@@ -354,72 +441,77 @@
     width = residual_block.shape[1]
     res = residual_block.T
     index = fine_index.T
-    place = jnp.stack([me, jnp.int32(peers)])
+    place = jnp.stack([me, jnp.int32(peers), lax.axis_index("cols")])
     owner = fine_owner.reshape(blocks, ext)
     mid_rows = mid_owner.reshape(mids, ext)
     shape = jax.ShapeDtypeStruct
     tile_bytes = fine_tiles.size * 2
     fine_flops = 2 * fine_tiles.size * width
-
-    hi = (owner % ext).astype(BF16)
-    lo = (owner // ext - me * mids).astype(BF16)
-    mid_hi = (mid_rows % ext).astype(BF16)
-    mid_block = (mid_rows // ext).astype(BF16)
-    diag = lambda b: jnp.diagonal(mid_tiles[b, 1])[None]
-
-    def message(picks, pair, far):
-        rows = [mid_tiles[b, k] for b, k in picks] + [hi, lo]
-        rows += [mid_hi[pair[0] : pair[1]], mid_block[pair[0] : pair[1]], diag(far)]
-        filled = MISC_AT + 5
-        rows.append(jnp.zeros((MESSAGE - filled, ext), BF16))
-        return jnp.concatenate(rows, axis=0)
-
-    last = mids - 1
-    to_right = message(
-        [(last, 0), (last, 1), (last, 2), (last - 1, 2), (0, 0)], (last - 1, last + 1), 0
-    )
-    to_left = message([(0, 0), (0, 1), (0, 2), (1, 0), (last, 2)], (0, 2), last)
-    shares = lax.axis_size("cols")
-    share = MESSAGE // shares
-    begin = lax.axis_index("cols") * share
-    up, down = shifted(res)
-    from_left = lax.ppermute(lax.dynamic_slice_in_dim(to_right, begin, share), "rows", up)
-    from_right = lax.ppermute(lax.dynamic_slice_in_dim(to_left, begin, share), "rows", down)
-    both = lax.all_gather(jnp.stack([from_left, from_right]), "cols", axis=1, tiled=True)
-    from_left, from_right = both[0], both[1]
-    all_basis = lax.all_gather(basis.T, "cols", axis=0, tiled=True)
-
-    a16, winv = pl.pallas_call(
+    extra = MESSAGE // (lax.axis_size("cols") * width)
+
+    a16, for_partner, for_other, winv, res_blocks = pl.pallas_call(
         first_kernel,
-        in_specs=[VM, ANY],
-        out_specs=[VM, VM],
-        out_shape=[shape((blocks, width, ext), BF16), shape((blocks, ext), F32)],
-        scratch_shapes=[pltpu.VMEM((blocks, ext, ext), BF16), pltpu.SemaphoreType.DMA((4,))],
+        in_specs=[SM, HBM, HBM, VM, VM, VM],
+        out_specs=[VM] * 5,
+        out_shape=[
+            shape((blocks, width, ext), BF16),
+            shape((blocks + extra, width, ext), BF16),
+            shape((blocks + extra, width, ext), BF16),
+            shape((blocks, ext), F32),
+            shape((blocks, width, ext), F32),
+        ],
+        scratch_shapes=[
+            pltpu.VMEM((width, count), F32),
+            pltpu.VMEM((blocks, ext, ext), BF16),
+            pltpu.VMEM((2, MESSAGE, ext), BF16),
+            pltpu.SemaphoreType.DMA((5,)),
+        ],
         name="first_smoothing",
-        **params(8, count * ext, tile_bytes // 4),
-    )(res, fine_tiles)
-
-    odd = me % 2
-
-    def sides(value):
-        near, far = halo(value)
-        return (
-            jnp.where(odd == 1, near, far),
-            jnp.where(odd == 1, far, near),
-        )
-
-    left, right = sides(a16)
-    b32, b16 = pl.pallas_call(
+        **params(FIRST_LIMIT, count * ext, tile_bytes // 4),
+    )(place, res, fine_tiles, mid_tiles, owner, mid_rows)
+
+    near, far = halo(for_partner, for_other)
+    tiles = fine_tiles
+    hot_own = pl.pallas_call(
+        hot_kernel,
+        in_specs=[ANY, VM],
+        out_specs=VM,
+        out_shape=shape((ext, count), BF16),
+        name="one_hot_rows",
+        **params(4, count * ext, 4 * tile_bytes),
+    )(winv, owner)
+    basis_pieces = [basis.T] + from_columns(basis.T)
+
+    b32, b16, mine = pl.pallas_call(
         second_kernel,
-        in_specs=[SM, SM] + [VM] * 6,
-        out_specs=[VM, VM],
-        out_shape=[shape((blocks, width, ext), F32), shape((blocks, width, ext), BF16)],
+        in_specs=[SM, SM] + [VM] * 6 + [ANY] * 4,
+        out_specs=[VM] * 3,
+        out_shape=[
+            shape((blocks, width, ext), F32),
+            shape((blocks, width, ext), BF16),
+            shape((2, extra, width, ext), BF16),
+        ],
         scratch_shapes=[pltpu.VMEM((3 * blocks, width, ext), BF16)],
         name="second_smoothing",
-        **params(12, fine_flops, tile_bytes),
-    )(index, place, fine_tiles, left, a16, right, res, winv)
-
-    left, right = sides(b16)
+        **params(6, fine_flops, tile_bytes),
+    )(index, place, tiles, near, a16, far, res_blocks, winv, hot_own, *basis_pieces[1:])
+
+    near, far = halo(b16, b16)
+    from_left, from_right, hot_left, hot_right = pl.pallas_call(
+        sides_kernel,
+        in_specs=[SM] + [VM] * 4,
+        out_specs=[VM] * 4,
+        out_shape=[
+            shape((MESSAGE, ext), BF16),
+            shape((MESSAGE, ext), BF16),
+            shape((ext, count), BF16),
+            shape((ext, count), BF16),
+        ],
+        scratch_shapes=[pltpu.VMEM((2, 4, extra, width, ext), BF16)],
+        name="side_messages",
+        **params(4, count * ext, tile_bytes),
+    )(place, mine, *from_columns(mine))
+
     fres, u, bpart, send = pl.pallas_call(
         third_kernel,
         in_specs=[SM, SM] + [VM] * 11,
@@ -433,12 +525,11 @@
         scratch_shapes=[
             pltpu.VMEM((3 * blocks, width, ext), BF16),
             pltpu.VMEM((mids * width, count), BF16),
-            pltpu.VMEM((ext, count), BF16),
         ],
         name="residual_and_restriction",
-        **params(20, fine_flops, tile_bytes),
+        **params(10, fine_flops, tile_bytes),
     )(
-        index, place, fine_tiles, left, b16, right, res, b32, owner, mid_tiles, mid_rows,
+        index, place, tiles, near, b16, far, res_blocks, owner, hot_own, mid_tiles, mid_rows,
         from_left, from_right,
     )
 
@@ -449,7 +540,7 @@
         out_specs=[VM, VM],
         out_shape=[shape((width, ext), BF16), shape((mids, width, ext), F32)],
         name="coarse_product",
-        **params(16, 2 * width * coarse_inverse.size, coarse_inverse.size * 4),
+        **params(4, 2 * width * coarse_inverse.size, coarse_inverse.size * 4),
     )(place, got, coarse_inverse, mid_tiles, u, bpart, from_left, from_right)
 
     partner = lax.ppermute(fix, "rows", [(i, i ^ 1) for i in range(peers)])
@@ -463,18 +554,18 @@
             shape((peers, mids + 1, width, ext), BF16),
         ],
         name="mid_level",
-        **params(12, 2 * width * mid_tiles.size, mid_tiles.size * 2),
+        **params(4, 2 * width * mid_tiles.size, mid_tiles.size * 2),
     )(place, fix, partner, mid_tiles, mid_rows, u, mid_b)
 
     return finish(
-        place, index, fine_tiles, send, dpart, c_edges, mid_tiles, owner, from_left, from_right,
-        b32, fres, winv, all_basis,
+        place, index, tiles, send, dpart, c_edges, mid_tiles, owner, hot_own, from_left, hot_left,
+        from_right, hot_right, b32, fres, winv, basis_pieces,
     )
 
 
 def finish(
-    place, index, fine_tiles, send, dpart, c_edges, mid_tiles, owner, from_left, from_right, b32,
-    fres, winv, all_basis,
+    place, index, tiles, send, dpart, c_edges, mid_tiles, owner, hot_own, from_left, hot_left,
+    from_right, hot_right, b32, fres, winv, basis_pieces,
 ):
     peers = lax.axis_size("rows")
     blocks, width, ext = b32.shape
@@ -484,24 +575,32 @@
     got = lax.all_to_all(send, "rows", 0, 0)
     out, grams = pl.pallas_call(
         last_kernel,
-        in_specs=[SM, SM] + [VM] * 12,
+        in_specs=[SM, SM] + [VM] * 18,
         out_specs=[VM, VM],
         out_shape=[
             shape((width, count), F32),
-            shape((peers, width, all_basis.shape[0]), F32),
+            shape((peers, width, ext), F32),
         ],
         scratch_shapes=[
             pltpu.VMEM((3 * blocks, width, ext), BF16),
             pltpu.VMEM((blocks, width, ext), F32),
             pltpu.VMEM((width, count), BF16),
+            pltpu.VMEM((4, width, width), F32),
         ],
         name="prolongation_and_last_smoothing",
-        **params(16, 2 * fine_tiles.size * width, fine_tiles.size * 2),
+        **params(8, 2 * tiles.size * width, tiles.size * 2),
     )(
-        index, place, fine_tiles, got, dpart, c_edges, mid_tiles, owner, from_left, from_right,
-        b32, fres, winv, all_basis,
-    )
-    gram = jnp.sum(lax.all_to_all(grams, "rows", 0, 0), axis=0)
+        index, place, tiles, got, dpart, c_edges, mid_tiles, owner, hot_own, from_left, hot_left,
+        from_right, hot_right, b32, fres, winv, *basis_pieces,
+    )
+    gram = pl.pallas_call(
+        sum_kernel,
+        in_specs=[VM],
+        out_specs=VM,
+        out_shape=shape((width, 4 * width), F32),
+        name="gram_sum",
+        **params(4, 0, 0),
+    )(lax.all_to_all(grams, "rows", 0, 0))
     return out.T, gram.T
 
 

time: 115 us -> 97.3 us (0.85)
  local copies, waits for them, and re-layouts: 17 us -> 2.51 us
  between operations: 14.3 us -> 0.76 us
  waiting for transfers between devices: 9.93 us -> 22.9 us
  blocking collectives: 40.8 us -> 33.8 us
  Pallas kernels: 18 us -> 22.7 us
  other arithmetic: 1.56 us -> 0.08 us
    ppermute x6 -> x10, waiting for transfers between devices: 6.43 us -> 19.6 us  [the longest x6 16.7 us: from_columns(): lax.ppermute(value, 'cols', [(i, i ^ n) for i in range(peers)])]
    unnamed x26 -> x16, local copies, waits for them, and re-layouts: 12.7 us -> 2.51 us
    all_gather x1 -> x0, blocking collectives: 7.01 us -> none  [on_device(): lax.all_gather(jnp.stack([from_left, from_right]), 'cols', axis=1, tiled=...]
    pallas_call x3 -> x6, Pallas kernels: 10.8 us -> 15.4 us  [the longest x1 5.84 us: finish(): pl.pallas_call(last_kernel, in_specs=[SM, SM] + [VM] * 18, out_specs=[VM,...]
    gather x2 -> x0, local copies, waits for them, and re-layouts: 3.01 us -> none  [on_device(): diag = lambda b: jnp.diagonal(mid_tiles[b, 1])[None]]
    ppermute x6 -> x10, starting transfers between devices: 12.8 us -> 13.7 us  [the longest x2 8.61 us: halo(): near = lax.ppermute(for_partner, 'rows', swap(even))]
  transfers between devices with their start and end apart: 8 -> 11, of which waited for: 4 -> 6; matrix products, arithmetic and copies ran while one was open for 3% -> 0% of each run, Pallas kernels for 9% -> 2%
where the time goes in v2:
time: 97.3 us; the launch traced here: 96.9 us
  blocking collectives  33.8 us (35%)
  waiting for transfers between devices  22.9 us (24%)
  Pallas kernels  22.7 us (23%)
  starting transfers between devices  14.1 us (14%)
  local copies, waits for them, and re-layouts  2.51 us (3%)
    ppermute x6, waiting for transfers between devices, from_columns(): lax.ppermute(value, 'cols', [(i, i ^ n) for i in range(peers)])  16.7 us
    all_to_all x1, blocking collectives, on_device(): got = lax.all_to_all(send, 'rows', 0, 0)  13.2 us
    all_to_all x1, blocking collectives, finish(): got = lax.all_to_all(send, 'rows', 0, 0)  11.2 us
    all_to_all x1, blocking collectives, finish(): lax.all_to_all(grams, 'rows', 0, 0)  9.37 us
    ppermute x2, starting transfers between devices, halo(): near = lax.ppermute(for_partner, 'rows', swap(even))  8.61 us
    pallas_call x1, Pallas kernels, finish(): pl.pallas_call(last_kernel, in_specs=[SM, SM] + [VM] * 18, out_specs=[VM,...  5.84 us
    pallas_call x1, Pallas kernels, on_device(): pl.pallas_call(third_kernel, in_specs=[SM, SM] + [VM] * 11, out_specs=[VM...  5.47 us
    ppermute x6, starting transfers between devices, from_columns(): lax.ppermute(value, 'cols', [(i, i ^ n) for i in range(peers)])  3.79 us
  transfers between devices with their start and end apart: 11, of which 6 were waited for; matrix products, arithmetic and copies ran while one was open for 0% of the time, Pallas kernels for 2%

profile of v2, /device:TPU:0, one launch (start us, length us, event | category | flops | bytes accessed | tf_op | source)
XLA Modules:
  0.0 96.9 jit_solution(17001604175880620451)
XLA Ops:
  0.6 0.1 pad_add_fusion.place
  0.7 0.0 copy-start.2
  0.7 1.0 %copy-done.2 = f32[8192,16]{0,1:T(8,128)S(1)} copy-done((f32[8192,16]{0,1:T(8,128)S(1)}, f32[8192,16]{0,1:T(8,128)}, u32[]{:S(2)}) %copy-start.2) | copy-done | bytes 524312
  1.8 0.0 copy-start.4
  1.8 0.8 copy-done.4
  2.5 0.0 copy-start.6
  2.5 0.7 copy-done.6
  3.2 3.8 %first_smoothing.1 = (bf16[64,16,128]{2,1,0:T(8,128)(2,1)S(1)}, bf16[75,16,128]{2,1,0:T(8,128)(2,1)S(1)}, bf16[75,16,128]{2,1,0:T(8,128)(2,1)S(1)}, f32[64,128]{1,0:T(8,128)S(1)}, f32[64,16,128]{2,1,0:T(8,128)S(1)}) custom-call(s32[3]{0:T(128)S(1)} %pad_add_fusion.place, f32[16,8192]{1,0:T(8,128)S(1)} %bitcast.9, bf16[64,4,128,128]{3,2,1,0:T(8,128)(2,1)} %tiles.7, ...), custom_call_target="tpu_custom_call" | custom-call | flops 1048576 | bytes 2097152 | tf_op jit(solution)/shard_map/first_smoothing/pallas_call | solution.py:452
  7.0 0.0 copy-start.7
  7.0 3.0 %collective-permute-start = (bf16[75,16,128]{2,1,0:T(8,128)(2,1)S(1)}, bf16[75,16,128]{2,1,0:T(8,128)(2,1)S(1)}, u32[]{:S(2)}, u32[]{:S(2)}) collective-permute-start(bf16[75,16,128]{2,1,0:T(8,128)(2,1)S(1)} %get-tuple-element.25), channel_id=1, source_target_pairs={{0,4},{8,12},{16,20},{24,28},{4,0},{12,8},{20,16},{28,24},{1,5},{9... | collective-permute-start | bytes 921608 | tf_op jit(solution)/shard_map/ppermute | solution.py:421
  10.0 0.7 collective-permute-start.1
  10.7 0.0 copy-done.5
  10.7 0.7 collective-permute-start.4
  11.4 0.9 collective-permute-start.3
  12.4 0.3 collective-permute-start.2
  12.7 0.6 one_hot_rows.1.hot.hot_own
  13.2 6.1 %collective-permute-done.4.basis_d = bf16[16,8192]{1,0:T(8,128)(2,1)S(1)} collective-permute-done((bf16[16,8192]{1,0:T(8,128)(2,1)S(1)}, bf16[16,8192]{1,0:T(8,128)(2,1)S(1)}, u32[]{:S(2)}, u32[]{:S(2)}) %collective-permute-start.4) | collective-permute-done | bytes 262176 | tf_op jit(solution)/shard_map/ppermute | solution.py:429
  19.4 5.7 %collective-permute-done.3.basis_c = bf16[16,8192]{1,0:T(8,128)(2,1)S(1)} collective-permute-done((bf16[16,8192]{1,0:T(8,128)(2,1)S(1)}, bf16[16,8192]{1,0:T(8,128)(2,1)S(1)}, u32[]{:S(2)}, u32[]{:S(2)}) %collective-permute-start.3) | collective-permute-done | bytes 262176 | tf_op jit(solution)/shard_map/ppermute | solution.py:429
  25.0 0.0 collective-permute-done.2.basis_b
  25.0 0.0 collective-permute-done.near
  25.0 0.0 collective-permute-done.1.far
  25.0 0.0 copy-done
  25.0 0.0 copy-done.7
  25.1 0.0 copy-start.1
  25.1 2.9 %second_smoothing.1 = (f32[64,16,128]{2,1,0:T(8,128)S(1)}, bf16[64,16,128]{2,1,0:T(8,128)(2,1)S(1)}, bf16[2,11,16,128]{3,2,1,0:T(8,128)(2,1)S(1)}) custom-call(s32[4,64]{1,0:T(4,128)S(1)} %bitcast.21, s32[3]{0:T(128)S(1)} %pad_add_fusion.place, bf16[64,4,128,128]{3,2,1,0:T(8,128)(2,1)S(1)} %copy-done, bf16[75,16,128]{2,1,0:T(8,128)(2,1)S(1)} %collective-permute-done.near, ...), custom_call_target="tpu_custom_call" | custom-call | flops 134217728 | bytes 8388608 | tf_op jit(solution)/shard_map/second_smoothing/pallas_call | solution.py:485
  28.0 0.7 collective-permute-start.6
  28.7 5.6 %collective-permute-start.5 = (bf16[64,16,128]{2,1,0:T(8,128)(2,1)S(1)}, bf16[64,16,128]{2,1,0:T(8,128)(2,1)S(1)}, u32[]{:S(2)}, u32[]{:S(2)}) collective-permute-start(bf16[64,16,128]{2,1,0:T(8,128)(2,1)S(1)} %get-tuple-element.30.own), channel_id=1, source_target_pairs={{0,4},{8,12},{16,20},{24,28},{4,0},{12,8},{20,16},{28,24},{1,5},{9... | collective-permute-start | bytes 786440 | tf_op jit(solution)/shard_map/ppermute | solution.py:421
  34.2 0.2 collective-permute-start.9
  34.4 1.2 %collective-permute-start.8 = (bf16[2,11,16,128]{3,2,1,0:T(8,128)(2,1)S(1)}, bf16[2,11,16,128]{3,2,1,0:T(8,128)(2,1)S(1)}, u32[]{:S(2)}, u32[]{:S(2)}) collective-permute-start(bf16[2,11,16,128]{3,2,1,0:T(8,128)(2,1)S(1)} %get-tuple-element.31.a), channel_id=1, source_target_pairs={{0,2},{1,3},{2,0},{3,1},{4,6},{5,7},{6,4},{7,5},{8,10},{9,11},{10,... | collective-permute-start | bytes 270344 | tf_op jit(solution)/shard_map/ppermute | solution.py:429
  35.7 0.4 collective-permute-start.7
  36.1 3.1 %collective-permute-done.9.d = bf16[2,11,16,128]{3,2,1,0:T(8,128)(2,1)S(1)} collective-permute-done((bf16[2,11,16,128]{3,2,1,0:T(8,128)(2,1)S(1)}, bf16[2,11,16,128]{3,2,1,0:T(8,128)(2,1)S(1)}, u32[]{:S(2)}, u32[]{:S(2)}) %collective-permute-start.9) | collective-permute-done | bytes 90144 | tf_op jit(solution)/shard_map/ppermute | solution.py:429
  39.2 1.9 %collective-permute-done.8.c = bf16[2,11,16,128]{3,2,1,0:T(8,128)(2,1)S(1)} collective-permute-done((bf16[2,11,16,128]{3,2,1,0:T(8,128)(2,1)S(1)}, bf16[2,11,16,128]{3,2,1,0:T(8,128)(2,1)S(1)}, u32[]{:S(2)}, u32[]{:S(2)}) %collective-permute-start.8) | collective-permute-done | bytes 90144 | tf_op jit(solution)/shard_map/ppermute | solution.py:429
  41.0 0.0 collective-permute-done.7.b
  41.0 1.7 %side_messages.1 = (bf16[704,128]{1,0:T(8,128)(2,1)S(1)}, bf16[704,128]{1,0:T(8,128)(2,1)S(1)}, bf16[128,8192]{1,0:T(8,128)(2,1)S(1)}, bf16[128,8192]{1,0:T(8,128)(2,1)S(1)}) custom-call(s32[3]{0:T(128)S(1)} %pad_add_fusion.place, bf16[2,11,16,128]{3,2,1,0:T(8,128)(2,1)S(1)} %get-tuple-element.31.a, bf16[2,11,16,128]{3,2,1,0:T(8,128)(2,1)S(1)} %collective-permute-done.7.b, ...), custom_call_target="tpu_custom_call" | custom-call | flops 1048576 | bytes 8388608 | tf_op jit(solution)/shard_map/side_messages/pallas_call | solution.py:500
  42.7 0.0 collective-permute-done.6.far
  42.8 2.9 %collective-permute-done.5.near = bf16[64,16,128]{2,1,0:T(8,128)(2,1)S(1)} collective-permute-done((bf16[64,16,128]{2,1,0:T(8,128)(2,1)S(1)}, bf16[64,16,128]{2,1,0:T(8,128)(2,1)S(1)}, u32[]{:S(2)}, u32[]{:S(2)}) %collective-permute-start.5) | collective-permute-done | bytes 262176 | tf_op jit(solution)/shard_map/ppermute | solution.py:421
  45.6 0.0 copy-done.1
  45.7 5.5 %residual_and_restriction.1 = (f32[64,16,128]{2,1,0:T(8,128)S(1)}, f32[8,16,128]{2,1,0:T(8,128)S(1)}, f32[8,16,128]{2,1,0:T(8,128)S(1)}, bf16[8,5,16,128]{3,2,1,0:T(8,128)(2,1)S(1)}) custom-call(s32[4,64]{1,0:T(4,128)S(1)} %bitcast.22, s32[3]{0:T(128)S(1)} %pad_add_fusion.place, bf16[64,4,128,128]{3,2,1,0:T(8,128)(2,1)S(1)} %copy-done, ...), custom_call_target="tpu_custom_call" | custom-call | flops 134217728 | bytes 8388608 | tf_op jit(solution)/shard_map/residual_and_restriction/pallas_call | solution.py:515
  51.1 13.2 %all_to_all.15.got = bf16[8,5,16,128]{3,2,1,0:T(8,128)(2,1)S(1)} all-to-all(bf16[8,5,16,128]{3,2,1,0:T(8,128)(2,1)S(1)} %get-tuple-element.34), channel_id=1, replica_groups=mesh['rows'=8,'cols'=4] {'rows'}, dimensions={0} | all-to-all | bytes 327680 | tf_op jit(solution)/shard_map/all_to_all | solution.py:536
  64.4 0.0 copy-done.3
  64.4 0.7 coarse_product.1
  65.1 0.4 collective-permute-start.10
  65.5 3.3 %collective-permute-done.10.partner = bf16[16,128]{1,0:T(8,128)(2,1)S(1)} collective-permute-done((bf16[16,128]{1,0:T(8,128)(2,1)S(1)}, bf16[16,128]{1,0:T(8,128)(2,1)S(1)}, u32[]{:S(2)}, u32[]{:S(2)}) %collective-permute-start.10) | collective-permute-done | bytes 4128 | tf_op jit(solution)/shard_map/ppermute | solution.py:546
  68.8 1.0 %mid_level.1 = (f32[8,16,128]{2,1,0:T(8,128)S(1)}, bf16[2,16,128]{2,1,0:T(8,128)(2,1)S(1)}, bf16[8,9,16,128]{3,2,1,0:T(8,128)(2,1)S(1)}) custom-call(s32[3]{0:T(128)S(1)} %pad_add_fusion.place, bf16[16,128]{1,0:T(8,128)(2,1)S(1)} %get-tuple-element.37.fix, bf16[16,128]{1,0:T(8,128)(2,1)S(1)} %collective-permute-done.10.partner, ...), custom_call_target="tpu_custom_call" | custom-call | flops 12582912 | bytes 786432 | tf_op jit(solution)/shard_map/mid_level/pallas_call | solution.py:547
  69.8 11.2 %all_to_all.16.got = bf16[8,9,16,128]{3,2,1,0:T(8,128)(2,1)S(1)} all-to-all(bf16[8,9,16,128]{3,2,1,0:T(8,128)(2,1)S(1)} %get-tuple-element.39), channel_id=1, replica_groups=mesh['rows'=8,'cols'=4] {'rows'}, dimensions={0} | all-to-all | bytes 589824 | tf_op jit(solution)/shard_map/all_to_all | solution.py:575
  81.0 5.8 %prolongation_and_last_smoothing.1 = (f32[16,8192]{1,0:T(8,128)}, f32[8,16,128]{2,1,0:T(8,128)S(1)}) custom-call(s32[4,64]{1,0:T(4,128)S(1)} %bitcast.23, s32[3]{0:T(128)S(1)} %pad_add_fusion.place, bf16[64,4,128,128]{3,2,1,0:T(8,128)(2,1)S(1)} %copy-done, bf16[8,9,16,128]{3,2,1,0:T(8,128)(2,1)S(1)} %all_to_all.16.got, ...), custom_call_target="tpu_custom_call" | custom-call | flops 134217728 | bytes 8388608 | tf_op jit(solution)/shard_map/prolongation_and_last_smoothing/pallas_call | solution.py:576
  86.9 9.4 %all_to_all.17.got = f32[8,16,128]{2,1,0:T(8,128)S(1)} all-to-all(f32[8,16,128]{2,1,0:T(8,128)S(1)} %get-tuple-element.47), channel_id=1, replica_groups=mesh['rows'=8,'cols'=4] {'rows'}, dimensions={0} | all-to-all | bytes 131072 | tf_op jit(solution)/shard_map/all_to_all | solution.py:603
  96.3 0.6 gram_sum.1
  (3 shorter events, 0.0 us)
Async XLA Ops:
  0.7 1.0 %copy-start.2 = (f32[8192,16]{0,1:T(8,128)S(1)}, f32[8192,16]{0,1:T(8,128)}, u32[]{:S(2)}) copy-start(f32[8192,16]{0,1:T(8,128)} %param.8) | copy-start | bytes 1572868
  1.8 0.8 copy-start.4
  2.5 0.7 copy-start.6
  3.2 7.5 %copy-start.5 = (bf16[8192,16]{0,1:T(8,128)(2,1)S(1)}, bf16[8192,16]{0,1:T(8,128)(2,1)}, u32[]{:S(2)}) copy-start(bf16[8192,16]{0,1:T(8,128)(2,1)} %param.9) | copy-start | bytes 786436
  3.2 21.8 %copy-start = (bf16[64,4,128,128]{3,2,1,0:T(8,128)(2,1)S(1)}, bf16[64,4,128,128]{3,2,1,0:T(8,128)(2,1)}, u32[]{:S(2)}) copy-start(bf16[64,4,128,128]{3,2,1,0:T(8,128)(2,1)} %tiles.7) | copy-start | bytes 25165828
  7.0 18.0 %copy-start.7 = (s32[64,4]{0,1:T(4,128)S(1)}, s32[64,4]{0,1:T(4,128)}, u32[]{:S(2)}) copy-start(s32[64,4]{0,1:T(4,128)} %param.11) | copy-start | bytes 3076
  7.0 18.0 %collective-permute-start = (bf16[75,16,128]{2,1,0:T(8,128)(2,1)S(1)}, bf16[75,16,128]{2,1,0:T(8,128)(2,1)S(1)}, u32[]{:S(2)}, u32[]{:S(2)}) collective-permute-start(bf16[75,16,128]{2,1,0:T(8,128)(2,1)S(1)} %get-tuple-element.25), channel_id=1, source_target_pairs={{0,4},{8,12},{16,20},{24,28},{4,0},{12,8},{20,16},{28,24},{1,5},{9... | collective-permute-start | bytes 921608 | tf_op jit(solution)/shard_map/ppermute | solution.py:421
  10.0 15.0 %collective-permute-start.1 = (bf16[75,16,128]{2,1,0:T(8,128)(2,1)S(1)}, bf16[75,16,128]{2,1,0:T(8,128)(2,1)S(1)}, u32[]{:S(2)}, u32[]{:S(2)}) collective-permute-start(bf16[75,16,128]{2,1,0:T(8,128)(2,1)S(1)} %get-tuple-element.27), channel_id=1, source_target_pairs={{4,8},{12,16},{20,24},{8,4},{16,12},{24,20},{5,9},{13,17},{21,25},... | collective-permute-start | bytes 921608 | tf_op jit(solution)/shard_map/ppermute | solution.py:422
  10.7 8.6 %collective-permute-start.4 = (bf16[16,8192]{1,0:T(8,128)(2,1)S(1)}, bf16[16,8192]{1,0:T(8,128)(2,1)S(1)}, u32[]{:S(2)}, u32[]{:S(2)}) collective-permute-start(bf16[16,8192]{1,0:T(8,128)(2,1)S(1)} %bitcast.14), channel_id=1, source_target_pairs={{0,3},{1,2},{2,1},{3,0},{4,7},{5,6},{6,5},{7,4},{8,11},{9,10},{10,... | collective-permute-start | bytes 786440 | tf_op jit(solution)/shard_map/ppermute | solution.py:429
  11.4 13.6 %collective-permute-start.3 = (bf16[16,8192]{1,0:T(8,128)(2,1)S(1)}, bf16[16,8192]{1,0:T(8,128)(2,1)S(1)}, u32[]{:S(2)}, u32[]{:S(2)}) collective-permute-start(bf16[16,8192]{1,0:T(8,128)(2,1)S(1)} %bitcast.15), channel_id=1, source_target_pairs={{0,2},{1,3},{2,0},{3,1},{4,6},{5,7},{6,4},{7,5},{8,10},{9,11},{10,... | collective-permute-start | bytes 786440 | tf_op jit(solution)/shard_map/ppermute | solution.py:429
  12.4 12.7 %collective-permute-start.2 = (bf16[16,8192]{1,0:T(8,128)(2,1)S(1)}, bf16[16,8192]{1,0:T(8,128)(2,1)S(1)}, u32[]{:S(2)}, u32[]{:S(2)}) collective-permute-start(bf16[16,8192]{1,0:T(8,128)(2,1)S(1)} %bitcast.16), channel_id=1, source_target_pairs={{0,1},{1,0},{2,3},{3,2},{4,5},{5,4},{6,7},{7,6},{8,9},{9,8},{10,11... | collective-permute-start | bytes 786440 | tf_op jit(solution)/shard_map/ppermute | solution.py:429
  25.1 20.6 %copy-start.1 = (bf16[8,3,128,128]{3,2,1,0:T(8,128)(2,1)S(1)}, bf16[8,3,128,128]{3,2,1,0:T(8,128)(2,1)}, u32[]{:S(2)}) copy-start(bf16[8,3,128,128]{3,2,1,0:T(8,128)(2,1)} %mid_tiles.9) | copy-start | bytes 2359300
  28.0 14.8 %collective-permute-start.6 = (bf16[64,16,128]{2,1,0:T(8,128)(2,1)S(1)}, bf16[64,16,128]{2,1,0:T(8,128)(2,1)S(1)}, u32[]{:S(2)}, u32[]{:S(2)}) collective-permute-start(bf16[64,16,128]{2,1,0:T(8,128)(2,1)S(1)} %get-tuple-element.30.own), channel_id=1, source_target_pairs={{4,8},{12,16},{20,24},{8,4},{16,12},{24,20},{5,9},{13,17},{21,25},... | collective-permute-start | bytes 786440 | tf_op jit(solution)/shard_map/ppermute | solution.py:422
  28.7 17.0 %collective-permute-start.5 = (bf16[64,16,128]{2,1,0:T(8,128)(2,1)S(1)}, bf16[64,16,128]{2,1,0:T(8,128)(2,1)S(1)}, u32[]{:S(2)}, u32[]{:S(2)}) collective-permute-start(bf16[64,16,128]{2,1,0:T(8,128)(2,1)S(1)} %get-tuple-element.30.own), channel_id=1, source_target_pairs={{0,4},{8,12},{16,20},{24,28},{4,0},{12,8},{20,16},{28,24},{1,5},{9... | collective-permute-start | bytes 786440 | tf_op jit(solution)/shard_map/ppermute | solution.py:421
  34.2 4.9 %collective-permute-start.9 = (bf16[2,11,16,128]{3,2,1,0:T(8,128)(2,1)S(1)}, bf16[2,11,16,128]{3,2,1,0:T(8,128)(2,1)S(1)}, u32[]{:S(2)}, u32[]{:S(2)}) collective-permute-start(bf16[2,11,16,128]{3,2,1,0:T(8,128)(2,1)S(1)} %get-tuple-element.31.a), channel_id=1, source_target_pairs={{0,3},{1,2},{2,1},{3,0},{4,7},{5,6},{6,5},{7,4},{8,11},{9,10},{10,... | collective-permute-start | bytes 270344 | tf_op jit(solution)/shard_map/ppermute | solution.py:429
  34.4 6.6 %collective-permute-start.8 = (bf16[2,11,16,128]{3,2,1,0:T(8,128)(2,1)S(1)}, bf16[2,11,16,128]{3,2,1,0:T(8,128)(2,1)S(1)}, u32[]{:S(2)}, u32[]{:S(2)}) collective-permute-start(bf16[2,11,16,128]{3,2,1,0:T(8,128)(2,1)S(1)} %get-tuple-element.31.a), channel_id=1, source_target_pairs={{0,2},{1,3},{2,0},{3,1},{4,6},{5,7},{6,4},{7,5},{8,10},{9,11},{10,... | collective-permute-start | bytes 270344 | tf_op jit(solution)/shard_map/ppermute | solution.py:429
  35.7 5.4 %collective-permute-start.7 = (bf16[2,11,16,128]{3,2,1,0:T(8,128)(2,1)S(1)}, bf16[2,11,16,128]{3,2,1,0:T(8,128)(2,1)S(1)}, u32[]{:S(2)}, u32[]{:S(2)}) collective-permute-start(bf16[2,11,16,128]{3,2,1,0:T(8,128)(2,1)S(1)} %get-tuple-element.31.a), channel_id=1, source_target_pairs={{0,1},{1,0},{2,3},{3,2},{4,5},{5,4},{6,7},{7,6},{8,9},{9,8},{10,11... | collective-permute-start | bytes 270344 | tf_op jit(solution)/shard_map/ppermute | solution.py:429
  45.7 18.7 %copy-start.3 = (f32[128,1024]{1,0:T(8,128)S(1)}, f32[128,1024]{1,0:T(8,128)}, u32[]{:S(2)}) copy-start(f32[128,1024]{1,0:T(8,128)} %inverse_rows.1) | copy-start | bytes 1572868
  65.1 3.6 %collective-permute-start.10 = (bf16[16,128]{1,0:T(8,128)(2,1)S(1)}, bf16[16,128]{1,0:T(8,128)(2,1)S(1)}, u32[]{:S(2)}, u32[]{:S(2)}) collective-permute-start(bf16[16,128]{1,0:T(8,128)(2,1)S(1)} %get-tuple-element.37.fix), channel_id=1, source_target_pairs={{0,4},{4,0},{8,12},{12,8},{16,20},{20,16},{24,28},{28,24},{1,5},{5... | collective-permute-start | bytes 12296 | tf_op jit(solution)/shard_map/ppermute | solution.py:546

commit v3 on v2

--- a/solution.py
+++ b/solution.py
@@ -17,6 +17,7 @@
 HI_AT, LO_AT, MISC_AT = 512, 576, 640
 MESSAGE = 704
 FIRST_LIMIT = 52
+MID_LIMIT = 8
 
 
 def dot_nt(a, b):
@@ -39,8 +40,8 @@
 
 
 def first_kernel(
-    place, res, tiles, mid_tiles, owner, mid_owner, a_out, near_out, far_out, winv_out, res_out, flat,
-    held, message, sems,
+    place, res, tiles, mid_tiles, owner, mid_owner, inverse_rows, a_out, near_out, far_out, winv_out,
+    res_out, flat, held, message, owned, mid_owned, inverse_part, sems, side_sems,
 ):
     blocks, ext = held.shape[0], held.shape[1]
     width = a_out.shape[1]
@@ -52,37 +53,61 @@
         return pltpu.make_async_copy(tiles.at[rows, 0], held.at[rows], sems.at[part])
 
     whole = pltpu.make_async_copy(res, flat, sems.at[parts])
+    mids = mid_tiles.shape[0]
+    last = mids - 1
+    picks = (
+        [(last, 1), (last, 2), (last - 1, 2), (0, 0)],
+        [(0, 1), (0, 0), (1, 0), (last, 2)],
+    )
+    share = inverse_part.shape[0]
+    begin = pl.multiple_of(place[2] * share, share)
+    smalls = [
+        pltpu.make_async_copy(owner, owned, side_sems.at[0]),
+        pltpu.make_async_copy(mid_owner, mid_owned, side_sems.at[1]),
+        pltpu.make_async_copy(inverse_rows.at[pl.ds(begin, share)], inverse_part, side_sems.at[2]),
+    ]
+    for side in range(2):
+        for n, (b, k) in enumerate(picks[side]):
+            smalls.append(
+                pltpu.make_async_copy(
+                    mid_tiles.at[b, k],
+                    message.at[side, pl.ds(n * ext, ext)],
+                    side_sems.at[3 + 4 * side + n],
+                )
+            )
     whole.start()
-    for part in range(parts):
+    copy(0).start()
+    for small in smalls:
+        small.start()
+    for part in range(1, parts):
         copy(part).start()
     eye = eye_mask(ext)
-
-    mids = mid_tiles.shape[0]
-    last = mids - 1
-    lo, hi = split(owner[...] - place[0] * (mids * ext), ext)
-    mid_block, mid_hi = split(mid_owner[...], ext)
-    sides = (
-        ([(last, 1), (last, 2), (last - 1, 2), (0, 0)], last - 1, 0),
-        ([(0, 1), (0, 0), (1, 0), (last, 2)], 0, last),
-    )
-    for side, (picks, first, far) in enumerate(sides):
-        for n, (b, k) in enumerate(picks):
-            message[side, n * ext : (n + 1) * ext] = mid_tiles[b, k]
+    for small in smalls:
+        small.wait()
+    lo, hi = split(owned[...] - place[0] * (mids * ext), ext)
+    mid_block, mid_hi = split(mid_owned[...], ext)
+    for side, first in enumerate((last - 1, 0)):
         message[side, HI_AT : HI_AT + blocks] = hi.astype(F32).astype(BF16)
         message[side, LO_AT : LO_AT + blocks] = lo.astype(F32).astype(BF16)
         rows = [
             mid_hi[first : first + 2].astype(F32),
             mid_block[first : first + 2].astype(F32),
-            diag_row(mid_tiles[far, 1], eye),
+            diag_row(message[1 - side, 0:ext], eye),
             jnp.zeros((MESSAGE - MISC_AT - 5, ext), F32),
         ]
         message[side, MISC_AT:MESSAGE] = jnp.concatenate(rows, axis=0).astype(BF16)
-    extra = near_out.shape[0] - blocks
+    extra = far_out.shape[0] - blocks
     odd = place[0] % 2
     for n in range(extra):
         part = pl.ds(pl.multiple_of((place[2] * extra + n) * width, width), width)
         near_out[blocks + n] = message[odd, part]
         far_out[blocks + n] = message[1 - odd, part]
+    tall, wide = share // width, inverse_part.shape[1] // ext
+    for i in range(tall):
+        for k in range(wide):
+            near_out[blocks + extra + i * wide + k] = inverse_part[
+                i * width : (i + 1) * width, k * ext : (k + 1) * ext
+            ].astype(BF16)
 
     for part in range(parts):
         copy(part).wait()
@@ -107,17 +132,24 @@
         hot_out[:, g * ext : (g + 1) * ext] = one_hot(hi[g : g + 1, :], ext)
 
 
-def sides_kernel(place, a, b, c, d, left_out, right_out, hot_left, hot_right, buffer):
-    extra, width, ext = a.shape[1:]
+def sides_kernel(
+    place, a, b, c, d, left_out, right_out, inverse_out, hot_left, hot_right, buffer
+):
+    width, ext = a.shape[1:]
+    extra = left_out.shape[0] // (4 * width)
     for n, piece in enumerate((a, b, c, d)):
-        at = place[2] ^ n
-        buffer[0, at] = piece[0]
-        buffer[1, at] = piece[1]
+        buffer[place[2] ^ n] = piece[...]
+    share = inverse_out.shape[0] // 4
+    wide = inverse_out.shape[1] // ext
     for n in range(4):
         for k in range(extra):
             rows = slice((n * extra + k) * width, (n * extra + k + 1) * width)
-            left_out[rows] = buffer[0, n, k]
-            right_out[rows] = buffer[1, n, k]
+            left_out[rows] = buffer[n, k]
+            right_out[rows] = buffer[n, extra + k]
+        for i in range(share // width):
+            rows = slice(n * share + i * width, n * share + (i + 1) * width)
+            for k in range(wide):
+                inverse_out[rows, k * ext : (k + 1) * ext] = buffer[n, 2 * extra + i * wide + k]
     blocks = hot_left.shape[1] // ext
     for message, hot in ((left_out, hot_left), (right_out, hot_right)):
         hi = as_int(message[HI_AT : HI_AT + blocks, :])
@@ -143,7 +175,7 @@
 
 def second_kernel(
     index, place, tiles, near, own, far, res, winv, hot, basis_b, basis_c, basis_d, b_out, b16_out,
-    mine_out, window,
+    b16_too, mine_out, window,
 ):
     del hot, basis_b, basis_c, basis_d
     blocks, ext = own.shape[0], own.shape[2]
@@ -156,9 +188,14 @@
         b = w * r + w * (r - product)
         b_out[g] = b
         b16_out[g] = b.astype(BF16)
+        b16_too[g] = b.astype(BF16)
+    for n in range(blocks, b16_too.shape[0]):
+        b16_too[n] = jnp.zeros_like(b16_too[n])
     odd = place[0] % 2
-    mine_out[1 - odd] = near[blocks:]
-    mine_out[odd] = far[blocks:]
+    extra = far.shape[0] - blocks
+    mine_out[pl.ds((1 - odd) * extra, extra)] = near[blocks : blocks + extra]
+    mine_out[pl.ds(odd * extra, extra)] = far[blocks:]
+    mine_out[2 * extra :] = near[blocks + extra :]
 
 
 def split(row, ext):
@@ -269,11 +306,16 @@
         send[d, 4] = jnp.where(me + 1 == d, last, jnp.where(me - 1 == d, first, none))
 
 
-def coarse_kernel(place, got, inverse_rows, mid_tiles, u, bpart, from_left, from_right, fix_out, b_out):
+def mid_kernel(
+    place, got, inverse_rows, partner_rows, mid_tiles, mid_owner, u, bpart, from_left, from_right,
+    dpart_out, edges_out, near_out, far_out, next_out, beyond_out,
+):
     ext = mid_tiles.shape[2]
     mids = mid_tiles.shape[0]
     peers = got.shape[0]
+    width = got.shape[2]
     me = place[0]
+    odd = me % 2
     rhs = []
     for k in range(peers):
         terms = [
@@ -283,42 +325,29 @@
         ]
         rhs.append(sum(terms[1:], terms[0]))
     rhs16 = jnp.concatenate([r.astype(BF16) for r in rhs], axis=1)
-    fix_out[...] = dot_nt(rhs16, inverse_rows[...].astype(BF16)).astype(BF16)
+    mine = dot_nt(rhs16, inverse_rows[...].astype(BF16))
+    other = dot_nt(rhs16, partner_rows[...])
+    pair = jnp.concatenate(
+        [jnp.where(odd == 0, mine, other), jnp.where(odd == 0, other, mine)], axis=0
+    ).astype(BF16)
     eye = eye_mask(ext)
+    winv = mid_inverse(mid_tiles, eye)
     winv_left = inverse(diag_row(edge(from_left, 0), eye), me > 0)
     winv_right = inverse(diag_row(edge(from_right, 0), eye), me < peers - 1)
     before = got[lax.rem(me + peers - 1, peers), 4].astype(F32)
     after = got[lax.rem(me + 1, peers), 4].astype(F32)
     a_before = (winv_left * before).astype(BF16)
     a_after = (winv_right * after).astype(BF16)
+    c, c16 = {}, {}
     for b in range(mids):
         value = bpart[b]
-        if b == 0 or b == mids - 1:
-            winv = DAMPING * (1.0 / diag_row(mid_tiles[b, 1], eye))
-            if b == 0:
-                value = value - winv * dot_nt(a_before, mid_tiles[b, 0])
-            if b == mids - 1:
-                value = value - winv * dot_nt(a_after, mid_tiles[b, 2])
-        b_out[b] = value
-
-
-def mid_kernel(place, fix, partner, mid_tiles, mid_owner, u, b_in, dpart_out, edges_out, send):
-    ext = mid_tiles.shape[2]
-    width = fix.shape[0]
-    mids = mid_tiles.shape[0]
-    me = place[0]
-    odd = me % 2
-    mine, other = fix[...], partner[...]
-    pair = jnp.concatenate(
-        [jnp.where(odd == 0, mine, other), jnp.where(odd == 0, other, mine)], axis=0
-    )
-    eye = eye_mask(ext)
-    winv = mid_inverse(mid_tiles, eye)
-    c, c16 = {}, {}
-    for b in range(mids):
+        if b == 0:
+            value = value - winv[b] * dot_nt(a_before, mid_tiles[b, 0])
+        if b == mids - 1:
+            value = value - winv[b] * dot_nt(a_after, mid_tiles[b, 2])
         block, hi = split(mid_owner[b : b + 1, :], ext)
         both = jnp.dot(pair, one_hot(hi, ext), preferred_element_type=F32)
-        c[b] = b_in[b] + jnp.where(block - (me - odd) == 0, both[:width], both[width:])
+        c[b] = value + jnp.where(block - (me - odd) == 0, both[:width], both[width:])
         c16[b] = c[b].astype(BF16)
     d16 = []
     for b in range(mids):
@@ -327,13 +356,15 @@
         d16.append(d.astype(BF16))
     edges_out[0] = c16[0]
     edges_out[1] = c16[mids - 1]
-    none = jnp.zeros_like(c16[0])
-    for t in range(send.shape[0]):
-        for b in range(mids):
-            send[t, b] = d16[b]
-        ahead = jnp.logical_or(me + 1 == t, me + 2 == t)
-        behind = jnp.logical_or(me - 1 == t, me - 2 == t)
-        send[t, mids] = jnp.where(ahead, c16[mids - 1], jnp.where(behind, c16[0], none))
+    for b in range(mids):
+        near_out[b] = d16[b]
+        far_out[b] = d16[b]
+    first, last = c16[0], c16[mids - 1]
+    low = me % 4 < 2
+    near_out[mids] = jnp.where(odd == 0, last, first)
+    far_out[mids] = jnp.where(odd == 0, first, last)
+    next_out[...] = jnp.where(low, last, first)
+    beyond_out[...] = jnp.where(low, first, last)
 
 
 def prolong(values, hot, lo, width, mids):
@@ -345,51 +376,60 @@
 
 
 def last_kernel(
-    index, place, tiles, got, dpart, c_edges, mid_tiles, owner, hot_own, from_left, hot_left,
+    index, place, tiles, near, far, nexts, beyond, dpart, c_edges, mid_tiles, owner, hot_own, from_left, hot_left,
     from_right, hot_right, b_in, fres, winv, basis_a, basis_b, basis_c, basis_d, out, gram_out, window,
     added, rounded, grams,
 ):
     blocks, width, ext = b_in.shape
     mids = mid_tiles.shape[0]
-    peers = got.shape[0]
-    me = place[0]
-    at = lambda shift: lax.rem(me + shift + peers, peers)
+    me, peers = place[0], place[1]
+    odd = me % 2
+    low = me % 4 < 2
     eye = eye_mask(ext)
-    left, right, far_left, far_right = (at(k) for k in (-1, 1, -2, 2))
     has_left, has_right = me > 0, me < peers - 1
+    left = [jnp.where(odd == 1, near[b], far[b]) for b in range(mids + 1)]
+    right = [jnp.where(odd == 1, far[b], near[b]) for b in range(mids + 1)]
+    far_left = jnp.where(low, beyond[...], nexts[...])
+    far_right = jnp.where(low, nexts[...], beyond[...])
     minv = lambda b: DAMPING * (1.0 / diag_row(mid_tiles[b, 1], eye))
     own = [dpart[b] for b in range(mids)]
-    own[0] = own[0] - minv(0) * dot_nt(got[left, mids], mid_tiles[0, 0])
-    own[-1] = own[-1] - minv(mids - 1) * dot_nt(got[right, mids], mid_tiles[mids - 1, 2])
-    lefts = [got[left, b].astype(F32) for b in range(mids)]
+    own[0] = own[0] - minv(0) * dot_nt(left[mids], mid_tiles[0, 0])
+    own[-1] = own[-1] - minv(mids - 1) * dot_nt(right[mids], mid_tiles[mids - 1, 2])
+    lefts = [v.astype(F32) for v in left[:mids]]
     lefts[0] = lefts[0] - inverse(
         from_left[MISC_AT + 4 : MISC_AT + 5, :].astype(F32), has_left
-    ) * dot_nt(got[far_left, mids], edge(from_left, 384))
+    ) * dot_nt(far_left, edge(from_left, 384))
     lefts[-1] = lefts[-1] - inverse(diag_row(edge(from_left, 0), eye), has_left) * dot_nt(
         c_edges[0], edge(from_left, 128)
     )
-    rights = [got[right, b].astype(F32) for b in range(mids)]
+    rights = [v.astype(F32) for v in right[:mids]]
     rights[0] = rights[0] - inverse(diag_row(edge(from_right, 0), eye), has_right) * dot_nt(
         c_edges[1], edge(from_right, 128)
     )
     rights[-1] = rights[-1] - inverse(
         from_right[MISC_AT + 4 : MISC_AT + 5, :].astype(F32), has_right
-    ) * dot_nt(got[far_right, mids], edge(from_right, 384))
+    ) * dot_nt(far_right, edge(from_right, 384))
     own16, left16, right16 = (
         jnp.concatenate([v.astype(BF16) for v in side], axis=0) for side in (own, lefts, rights)
     )
-    for g in range(blocks):
-        cols = slice(g * ext, (g + 1) * ext)
-        lo, _ = split(owner[pl.ds(g, 1), :] - me * (mids * ext), ext)
-        value = prolong(own16, hot_own[:, cols], lo, width, mids)
-        added[g] = value
-        window[blocks + g] = value.astype(BF16)
-        for message, hot, values, base in (
-            (from_left, hot_left, left16, 0),
-            (from_right, hot_right, right16, 2 * blocks),
+    own_lo, _ = split(owner[...] - me * (mids * ext), ext)
+    left_lo, right_lo = (
+        as_int(message[LO_AT : LO_AT + blocks, :]) for message in (from_left, from_right)
+    )
+    for g in range(0, blocks, 2):
+        cols = slice(g * ext, (g + 2) * ext)
+        for lo, hot, values, base in (
+            (own_lo, hot_own, own16, blocks),
+            (left_lo, hot_left, left16, 0),
+            (right_lo, hot_right, right16, 2 * blocks),
         ):
-            lo = as_int(message[LO_AT + g : LO_AT + g + 1, :])
-            window[base + g] = prolong(values, hot[:, cols], lo, width, mids).astype(BF16)
+            row = jnp.concatenate([lo[g : g + 1], lo[g + 1 : g + 2]], axis=1)
+            value = prolong(values, hot[:, cols], row, width, mids)
+            for n in range(2):
+                half = value[:, n * ext : (n + 1) * ext]
+                if base == blocks:
+                    added[g + n] = half
+                window[base + g + n] = half.astype(BF16)
     offset = (me - 1) * blocks
     for g in range(blocks):
         product = fine_row(index, offset, tiles, window, g)
@@ -425,9 +465,9 @@
 
 def from_columns(value):
     peers = lax.axis_size("cols")
-    return [
-        lax.ppermute(value, "cols", [(i, i ^ n) for i in range(peers)]) for n in range(1, peers)
-    ]
+    swap = lambda v, n: lax.ppermute(v, "cols", [(i, i ^ n) for i in range(peers)])
+    across = swap(value, 2)
+    return [swap(value, 1), across, swap(across, 1)]
 
 
 def on_device(
@@ -449,13 +489,18 @@
     fine_flops = 2 * fine_tiles.size * width
     extra = MESSAGE // (lax.axis_size("cols") * width)
 
+    columns = lax.axis_size("cols")
+    share = coarse_inverse.shape[0] // columns
+    whole_row = coarse_inverse.shape[1]
+    quarter = (share // width) * (whole_row // ext)
+
     a16, for_partner, for_other, winv, res_blocks = pl.pallas_call(
         first_kernel,
-        in_specs=[SM, HBM, HBM, VM, VM, VM],
+        in_specs=[SM] + [HBM] * 6,
         out_specs=[VM] * 5,
         out_shape=[
             shape((blocks, width, ext), BF16),
-            shape((blocks + extra, width, ext), BF16),
+            shape((blocks + extra + quarter, width, ext), BF16),
             shape((blocks + extra, width, ext), BF16),
             shape((blocks, ext), F32),
             shape((blocks, width, ext), F32),
@@ -464,11 +509,15 @@
             pltpu.VMEM((width, count), F32),
             pltpu.VMEM((blocks, ext, ext), BF16),
             pltpu.VMEM((2, MESSAGE, ext), BF16),
+            pltpu.VMEM((blocks, ext), jnp.int32),
+            pltpu.VMEM((mids, ext), jnp.int32),
+            pltpu.VMEM((share, whole_row), F32),
             pltpu.SemaphoreType.DMA((5,)),
+            pltpu.SemaphoreType.DMA((11,)),
         ],
         name="first_smoothing",
         **params(FIRST_LIMIT, count * ext, tile_bytes // 4),
-    )(place, res, fine_tiles, mid_tiles, owner, mid_rows)
+    )(place, res, fine_tiles, mid_tiles, owner, mid_rows, coarse_inverse)
 
     near, far = halo(for_partner, for_other)
     tiles = fine_tiles
@@ -482,34 +531,36 @@
     )(winv, owner)
     basis_pieces = [basis.T] + from_columns(basis.T)
 
-    b32, b16, mine = pl.pallas_call(
+    b32, b16, b16_too, mine = pl.pallas_call(
         second_kernel,
         in_specs=[SM, SM] + [VM] * 6 + [ANY] * 4,
-        out_specs=[VM] * 3,
+        out_specs=[VM] * 4,
         out_shape=[
             shape((blocks, width, ext), F32),
             shape((blocks, width, ext), BF16),
-            shape((2, extra, width, ext), BF16),
+            shape((blocks + 1, width, ext), BF16),
+            shape((2 * extra + quarter, width, ext), BF16),
         ],
         scratch_shapes=[pltpu.VMEM((3 * blocks, width, ext), BF16)],
         name="second_smoothing",
         **params(6, fine_flops, tile_bytes),
     )(index, place, tiles, near, a16, far, res_blocks, winv, hot_own, *basis_pieces[1:])
 
-    near, far = halo(b16, b16)
-    from_left, from_right, hot_left, hot_right = pl.pallas_call(
+    near, far = halo(b16_too, b16)
+    from_left, from_right, partner_rows, hot_left, hot_right = pl.pallas_call(
         sides_kernel,
         in_specs=[SM] + [VM] * 4,
-        out_specs=[VM] * 4,
+        out_specs=[VM] * 5,
         out_shape=[
             shape((MESSAGE, ext), BF16),
             shape((MESSAGE, ext), BF16),
+            shape(coarse_inverse.shape, BF16),
             shape((ext, count), BF16),
             shape((ext, count), BF16),
         ],
-        scratch_shapes=[pltpu.VMEM((2, 4, extra, width, ext), BF16)],
+        scratch_shapes=[pltpu.VMEM((4, 2 * extra + quarter, width, ext), BF16)],
         name="side_messages",
-        **params(4, count * ext, tile_bytes),
+        **params(4, ext, ext),
     )(place, mine, *from_columns(mine))
 
     fres, u, bpart, send = pl.pallas_call(
@@ -534,37 +585,33 @@
     )
 
     got = lax.all_to_all(send, "rows", 0, 0)
-    fix, mid_b = pl.pallas_call(
-        coarse_kernel,
-        in_specs=[SM] + [VM] * 7,
-        out_specs=[VM, VM],
-        out_shape=[shape((width, ext), BF16), shape((mids, width, ext), F32)],
-        name="coarse_product",
-        **params(4, 2 * width * coarse_inverse.size, coarse_inverse.size * 4),
-    )(place, got, coarse_inverse, mid_tiles, u, bpart, from_left, from_right)
-
-    partner = lax.ppermute(fix, "rows", [(i, i ^ 1) for i in range(peers)])
-    dpart, c_edges, send = pl.pallas_call(
+    dpart, c_edges, *sends = pl.pallas_call(
         mid_kernel,
-        in_specs=[SM] + [VM] * 6,
-        out_specs=[VM] * 3,
+        in_specs=[SM] + [VM] * 9,
+        out_specs=[VM] * 6,
         out_shape=[
             shape((mids, width, ext), F32),
             shape((2, width, ext), BF16),
-            shape((peers, mids + 1, width, ext), BF16),
-        ],
-        name="mid_level",
-        **params(4, 2 * width * mid_tiles.size, mid_tiles.size * 2),
-    )(place, fix, partner, mid_tiles, mid_rows, u, mid_b)
+            shape((mids + 1, width, ext), BF16),
+            shape((mids + 1, width, ext), BF16),
+            shape((width, ext), BF16),
+            shape((width, ext), BF16),
+        ],
+        name="coarse_and_mid_level",
+        **params(MID_LIMIT, 4 * width * coarse_inverse.size, coarse_inverse.size * 4),
+    )(
+        place, got, coarse_inverse, partner_rows, mid_tiles, mid_rows, u, bpart, from_left,
+        from_right,
+    )
 
     return finish(
-        place, index, tiles, send, dpart, c_edges, mid_tiles, owner, hot_own, from_left, hot_left,
+        place, index, tiles, sends, dpart, c_edges, mid_tiles, owner, hot_own, from_left, hot_left,
         from_right, hot_right, b32, fres, winv, basis_pieces,
     )
 
 
 def finish(
-    place, index, tiles, send, dpart, c_edges, mid_tiles, owner, hot_own, from_left, hot_left,
+    place, index, tiles, sends, dpart, c_edges, mid_tiles, owner, hot_own, from_left, hot_left,
     from_right, hot_right, b32, fres, winv, basis_pieces,
 ):
     peers = lax.axis_size("rows")
@@ -572,10 +619,14 @@
     mids = mid_tiles.shape[0]
     count = blocks * ext
     shape = jax.ShapeDtypeStruct
-    got = lax.all_to_all(send, "rows", 0, 0)
+    near, far = halo(*sends[:2])
+    pairs = [(i, i + 2) for i in range(peers - 2) if i % 4 >= 2]
+    pairs += [(j, i) for i, j in pairs]
+    nexts = lax.ppermute(sends[2], "rows", [(i, i ^ 2) for i in range(peers)])
+    beyond = lax.ppermute(sends[3], "rows", pairs)
     out, grams = pl.pallas_call(
         last_kernel,
-        in_specs=[SM, SM] + [VM] * 18,
+        in_specs=[SM, SM] + [VM] * 21,
         out_specs=[VM, VM],
         out_shape=[
             shape((width, count), F32),
@@ -590,7 +641,7 @@
         name="prolongation_and_last_smoothing",
         **params(8, 2 * tiles.size * width, tiles.size * 2),
     )(
-        index, place, tiles, got, dpart, c_edges, mid_tiles, owner, hot_own, from_left, hot_left,
+        index, place, tiles, near, far, nexts, beyond, dpart, c_edges, mid_tiles, owner, hot_own, from_left, hot_left,
         from_right, hot_right, b32, fres, winv, *basis_pieces,
     )
     gram = pl.pallas_call(

time: 97.3 us -> 86.3 us (0.89)
  blocking collectives: 33.8 us -> 25.5 us
  waiting for transfers between devices: 22.9 us -> 20.9 us
  starting transfers between devices: 14.1 us -> 15.8 us
  Pallas kernels: 22.7 us -> 21.5 us
  local copies, waits for them, and re-layouts: 2.51 us -> 1.47 us
    ppermute x7 -> x8, waiting for transfers between devices: 20 us -> 4.53 us  [the longest x6 3.29 us: from_columns(): lax.ppermute(v, 'cols', [(i, i ^ n) for i in range(peers)])]
    ppermute x2 -> x3, waiting for transfers between devices: 2.9 us -> 16.4 us  [halo(): near = lax.ppermute(for_partner, 'rows', swap(even))]
    all_to_all x1 -> x0, blocking collectives: 11.2 us -> none  [finish(): got = lax.all_to_all(send, 'rows', 0, 0)]
    ppermute x7 -> x8, starting transfers between devices: 4.15 us -> 9.53 us  [the longest x1 4.68 us: finish(): nexts = lax.ppermute(sends[2], 'rows', [(i, i ^ 2) for i in range(peers)])]
    ppermute x2 -> x3, starting transfers between devices: 8.61 us -> 4.25 us  [halo(): near = lax.ppermute(for_partner, 'rows', swap(even))]
    all_to_all x1, blocking collectives: 9.37 us -> 12.3 us  [finish(): lax.all_to_all(grams, 'rows', 0, 0)]
    pallas_call x5 -> x4, Pallas kernels: 13.1 us -> 11.9 us  [the longest x1 5.83 us: finish(): pl.pallas_call(last_kernel, in_specs=[SM, SM] + [VM] * 21, out_specs=[VM,...]
    unnamed x16 -> x14, local copies, waits for them, and re-layouts: 2.51 us -> 1.47 us
  transfers between devices with their start and end apart: 11 -> 14, of which waited for: 6 -> 6; matrix products, arithmetic and copies ran while one was open for 0% -> 0% of each run, Pallas kernels for 2% -> 6%
where the time goes in v3:
time: 86.3 us; the launch traced here: 86 us
  blocking collectives  25.5 us (30%)
  Pallas kernels  21.5 us (25%)
  waiting for transfers between devices  20.9 us (24%)
  starting transfers between devices  15.8 us (18%)
  local copies, waits for them, and re-layouts  1.47 us (2%)
    ppermute x3, waiting for transfers between devices, halo(): near = lax.ppermute(for_partner, 'rows', swap(even))  16.4 us
    all_to_all x1, blocking collectives, on_device(): got = lax.all_to_all(send, 'rows', 0, 0)  13.2 us
    all_to_all x1, blocking collectives, finish(): lax.all_to_all(grams, 'rows', 0, 0)  12.3 us
    pallas_call x1, Pallas kernels, finish(): pl.pallas_call(last_kernel, in_specs=[SM, SM] + [VM] * 21, out_specs=[VM,...  5.83 us
    pallas_call x1, Pallas kernels, on_device(): pl.pallas_call(third_kernel, in_specs=[SM, SM] + [VM] * 11, out_specs=[VM...  5.46 us
    ppermute x1, starting transfers between devices, finish(): nexts = lax.ppermute(sends[2], 'rows', [(i, i ^ 2) for i in range(peers)])  4.68 us
    ppermute x3, starting transfers between devices, halo(): near = lax.ppermute(for_partner, 'rows', swap(even))  4.25 us
    ppermute x6, starting transfers between devices, from_columns(): lax.ppermute(v, 'cols', [(i, i ^ n) for i in range(peers)])  4.2 us
  transfers between devices with their start and end apart: 14, of which 6 were waited for; matrix products, arithmetic and copies ran while one was open for 0% of the time, Pallas kernels for 6%

profile of v3, /device:TPU:0, one launch (start us, length us, event | category | flops | bytes accessed | tf_op | source)
XLA Modules:
  0.0 86.0 jit_solution(16163604888991072010)
XLA Ops:
  0.6 3.0 %collective-permute-start.3 = (bf16[16,8192]{1,0:T(8,128)(2,1)}, bf16[16,8192]{1,0:T(8,128)(2,1)S(1)}, u32[]{:S(2)}, u32[]{:S(2)}) collective-permute-start(bf16[16,8192]{1,0:T(8,128)(2,1)} %bitcast.13), channel_id=1, source_target_pairs={{0,2},{1,3},{2,0},{3,1},{4,6},{5,7},{6,4},{7,5},{8,10},{9,11},{10,... | collective-permute-start | bytes 786440 | tf_op jit(solution)/shard_map/ppermute | solution.py:468
  3.6 0.1 pad_add_fusion.place
  3.7 0.0 copy-start.3
  3.7 0.8 copy-done.3
  4.5 0.7 copy-done.5
  5.2 3.1 %first_smoothing.1 = (bf16[64,16,128]{2,1,0:T(8,128)(2,1)S(1)}, bf16[91,16,128]{2,1,0:T(8,128)(2,1)S(1)}, bf16[75,16,128]{2,1,0:T(8,128)(2,1)S(1)}, f32[64,128]{1,0:T(8,128)S(1)}, f32[64,16,128]{2,1,0:T(8,128)S(1)}) custom-call(s32[3]{0:T(128)S(1)} %pad_add_fusion.place, f32[16,8192]{1,0:T(8,128)} %bitcast.22, bf16[64,4,128,128]{3,2,1,0:T(8,128)(2,1)} %tiles.7, ...), custom_call_target="tpu_custom_call" | custom-call | flops 1048576 | bytes 2097152 | tf_op jit(solution)/shard_map/first_smoothing/pallas_call | solution.py:497
  8.2 0.0 copy-start.6
  8.2 1.6 %collective-permute-start = (bf16[91,16,128]{2,1,0:T(8,128)(2,1)S(1)}, bf16[91,16,128]{2,1,0:T(8,128)(2,1)S(1)}, u32[]{:S(2)}, u32[]{:S(2)}) collective-permute-start(bf16[91,16,128]{2,1,0:T(8,128)(2,1)S(1)} %get-tuple-element.28), channel_id=1, source_target_pairs={{0,4},{8,12},{16,20},{24,28},{4,0},{12,8},{20,16},{28,24},{1,5},{9... | collective-permute-start | bytes 1118216 | tf_op jit(solution)/shard_map/ppermute | solution.py:461
  9.8 0.7 collective-permute-start.1
  10.5 0.0 copy-done.4
  10.5 0.1 collective-permute-start.2
  10.6 0.0 collective-permute-done.3.basis_c
  10.6 0.5 collective-permute-start.4
  11.1 0.6 one_hot_rows.1.hot.hot_own
  11.7 0.5 collective-permute-done.2.basis_b
  12.1 0.0 collective-permute-done.1.far
  12.1 11.9 %collective-permute-done.near = bf16[91,16,128]{2,1,0:T(8,128)(2,1)S(1)} collective-permute-done((bf16[91,16,128]{2,1,0:T(8,128)(2,1)S(1)}, bf16[91,16,128]{2,1,0:T(8,128)(2,1)S(1)}, u32[]{:S(2)}, u32[]{:S(2)}) %collective-permute-start) | collective-permute-done | bytes 372768 | tf_op jit(solution)/shard_map/ppermute | solution.py:461
  24.1 0.0 collective-permute-done.4.basis_d
  24.1 0.0 copy-done
  24.1 0.0 copy-done.6
  24.1 2.9 %second_smoothing.1 = (f32[64,16,128]{2,1,0:T(8,128)S(1)}, bf16[64,16,128]{2,1,0:T(8,128)(2,1)S(1)}, bf16[65,16,128]{2,1,0:T(8,128)(2,1)S(1)}, bf16[38,16,128]{2,1,0:T(8,128)(2,1)S(1)}) custom-call(s32[4,64]{1,0:T(4,128)S(1)} %bitcast.19, s32[3]{0:T(128)S(1)} %pad_add_fusion.place, bf16[64,4,128,128]{3,2,1,0:T(8,128)(2,1)S(1)} %copy-done, ...), custom_call_target="tpu_custom_call" | custom-call | flops 134217728 | bytes 8388608 | tf_op jit(solution)/shard_map/second_smoothing/pallas_call | solution.py:534
  27.0 0.6 collective-permute-start.8
  27.6 2.5 %collective-permute-start.5 = (bf16[65,16,128]{2,1,0:T(8,128)(2,1)S(1)}, bf16[65,16,128]{2,1,0:T(8,128)(2,1)S(1)}, u32[]{:S(2)}, u32[]{:S(2)}) collective-permute-start(bf16[65,16,128]{2,1,0:T(8,128)(2,1)S(1)} %get-tuple-element.33), channel_id=1, source_target_pairs={{0,4},{8,12},{16,20},{24,28},{4,0},{12,8},{20,16},{28,24},{1,5},{9... | collective-permute-start | bytes 798728 | tf_op jit(solution)/shard_map/ppermute | solution.py:461
  30.1 0.7 collective-permute-start.6
  30.7 0.1 collective-permute-start.7
  30.8 1.5 %collective-permute-done.8.c = bf16[38,16,128]{2,1,0:T(8,128)(2,1)S(1)} collective-permute-done((bf16[38,16,128]{2,1,0:T(8,128)(2,1)S(1)}, bf16[38,16,128]{2,1,0:T(8,128)(2,1)S(1)}, u32[]{:S(2)}, u32[]{:S(2)}) %collective-permute-start.8) | collective-permute-done | bytes 155680 | tf_op jit(solution)/shard_map/ppermute | solution.py:468
  32.3 0.0 collective-permute-start.9
  32.3 0.0 collective-permute-done.7.b
  32.3 1.4 %collective-permute-done.9.d = bf16[38,16,128]{2,1,0:T(8,128)(2,1)S(1)} collective-permute-done((bf16[38,16,128]{2,1,0:T(8,128)(2,1)S(1)}, bf16[38,16,128]{2,1,0:T(8,128)(2,1)S(1)}, u32[]{:S(2)}, u32[]{:S(2)}) %collective-permute-start.9) | collective-permute-done | bytes 155680 | tf_op jit(solution)/shard_map/ppermute | solution.py:468
  33.6 1.8 %side_messages.1 = (bf16[704,128]{1,0:T(8,128)(2,1)S(1)}, bf16[704,128]{1,0:T(8,128)(2,1)S(1)}, bf16[128,1024]{1,0:T(8,128)(2,1)S(1)}, bf16[128,8192]{1,0:T(8,128)(2,1)S(1)}, bf16[128,8192]{1,0:T(8,128)(2,1)S(1)}) custom-call(s32[3]{0:T(128)S(1)} %pad_add_fusion.place, bf16[38,16,128]{2,1,0:T(8,128)(2,1)S(1)} %get-tuple-element.35.a, ...), custom_call_target="tpu_custom_call" | custom-call | flops 128 | bytes 128 | tf_op jit(solution)/shard_map/side_messages/pallas_call | solution.py:550
  35.4 0.0 collective-permute-done.6.far
  35.4 4.4 %collective-permute-done.5.near = bf16[65,16,128]{2,1,0:T(8,128)(2,1)S(1)} collective-permute-done((bf16[65,16,128]{2,1,0:T(8,128)(2,1)S(1)}, bf16[65,16,128]{2,1,0:T(8,128)(2,1)S(1)}, u32[]{:S(2)}, u32[]{:S(2)}) %collective-permute-start.5) | collective-permute-done | bytes 266272 | tf_op jit(solution)/shard_map/ppermute | solution.py:461
  39.9 0.0 copy-done.1
  39.9 5.5 %residual_and_restriction.1 = (f32[64,16,128]{2,1,0:T(8,128)S(1)}, f32[8,16,128]{2,1,0:T(8,128)S(1)}, f32[8,16,128]{2,1,0:T(8,128)S(1)}, bf16[8,5,16,128]{3,2,1,0:T(8,128)(2,1)S(1)}) custom-call(s32[4,64]{1,0:T(4,128)S(1)} %bitcast.20, s32[3]{0:T(128)S(1)} %pad_add_fusion.place, bf16[64,4,128,128]{3,2,1,0:T(8,128)(2,1)S(1)} %copy-done, ...), custom_call_target="tpu_custom_call" | custom-call | flops 134217728 | bytes 8388608 | tf_op jit(solution)/shard_map/residual_and_restriction/pallas_call | solution.py:566
  45.3 13.2 %all_to_all.10.got = bf16[8,5,16,128]{3,2,1,0:T(8,128)(2,1)S(1)} all-to-all(bf16[8,5,16,128]{3,2,1,0:T(8,128)(2,1)S(1)} %get-tuple-element.38), channel_id=1, replica_groups=mesh['rows'=8,'cols'=4] {'rows'}, dimensions={0} | all-to-all | bytes 327680 | tf_op jit(solution)/shard_map/all_to_all | solution.py:587
  58.5 0.0 copy-done.2
  58.5 1.2 %coarse_and_mid_level.1 = (f32[8,16,128]{2,1,0:T(8,128)S(1)}, bf16[2,16,128]{2,1,0:T(8,128)(2,1)S(1)}, bf16[9,16,128]{2,1,0:T(8,128)(2,1)S(1)}, bf16[9,16,128]{2...) custom-call(s32[3]{0:T(128)S(1)} %pad_add_fusion.place, ...), custom_call_target="tpu_custom_call" | custom-call | flops 8388608 | bytes 524288 | tf_op jit(solution)/shard_map/coarse_and_mid_level/pallas_call | solution.py:588
  59.8 0.2 collective-permute-start.10
  60.0 0.7 collective-permute-start.11
  60.6 4.7 %collective-permute-start.12 = (bf16[16,128]{1,0:T(8,128)(2,1)S(1)}, bf16[16,128]{1,0:T(8,128)(2,1)S(1)}, u32[]{:S(2)}, u32[]{:S(2)}) collective-permute-start(bf16[16,128]{1,0:T(8,128)(2,1)S(1)} %get-tuple-element.44), channel_id=1, source_target_pairs={{0,8},{4,12},{8,0},{12,4},{16,24},{20,28},{24,16},{28,20},{1,9},{5... | collective-permute-start | bytes 12296 | tf_op jit(solution)/shard_map/ppermute | solution.py:625
  65.3 0.6 collective-permute-start.13
  66.0 1.2 %collective-permute-done.12.nexts = bf16[16,128]{1,0:T(8,128)(2,1)S(1)} collective-permute-done((bf16[16,128]{1,0:T(8,128)(2,1)S(1)}, bf16[16,128]{1,0:T(8,128)(2,1)S(1)}, u32[]{:S(2)}, u32[]{:S(2)}) %collective-permute-start.12) | collective-permute-done | bytes 4128 | tf_op jit(solution)/shard_map/ppermute | solution.py:625
  67.2 0.0 collective-permute-done.13.beyond
  67.2 0.0 collective-permute-done.10.near
  67.2 0.0 collective-permute-done.11.far
  67.2 5.8 %prolongation_and_last_smoothing.1 = (f32[16,8192]{1,0:T(8,128)}, f32[8,16,128]{2,1,0:T(8,128)S(1)}) custom-call(s32[4,64]{1,0:T(4,128)S(1)} %bitcast.21, s32[3]{0:T(128)S(1)} %pad_add_fusion.place, bf16[64,4,128,128]{3,2,1,0:T(8,128)(2,1)S(1)} %copy-done, bf16[9,16,128]{2,1,0:T(8,128)(2,1)S(1)} %collective-permute-done.10.near, ...), custom_call_target="tpu_custom_call" | custom-call | flops 134217728 | bytes 8388608 | tf_op jit(solution)/shard_map/prolongation_and_last_smoothing/pallas_call | solution.py:627
  73.0 12.3 %all_to_all.11.got = f32[8,16,128]{2,1,0:T(8,128)S(1)} all-to-all(f32[8,16,128]{2,1,0:T(8,128)S(1)} %get-tuple-element.53), channel_id=1, replica_groups=mesh['rows'=8,'cols'=4] {'rows'}, dimensions={0} | all-to-all | bytes 131072 | tf_op jit(solution)/shard_map/all_to_all | solution.py:654
  85.4 0.6 gram_sum.1
  (5 shorter events, 0.0 us)
Async XLA Ops:
  0.6 10.0 %collective-permute-start.3 = (bf16[16,8192]{1,0:T(8,128)(2,1)}, bf16[16,8192]{1,0:T(8,128)(2,1)S(1)}, u32[]{:S(2)}, u32[]{:S(2)}) collective-permute-start(bf16[16,8192]{1,0:T(8,128)(2,1)} %bitcast.13), channel_id=1, source_target_pairs={{0,2},{1,3},{2,0},{3,1},{4,6},{5,7},{6,4},{7,5},{8,10},{9,11},{10,... | collective-permute-start | bytes 786440 | tf_op jit(solution)/shard_map/ppermute | solution.py:468
  3.7 0.8 copy-start.3
  4.5 0.7 copy-start.5
  5.2 5.4 %copy-start.4 = (bf16[8192,16]{0,1:T(8,128)(2,1)S(1)}, bf16[8192,16]{0,1:T(8,128)(2,1)}, u32[]{:S(2)}) copy-start(bf16[8192,16]{0,1:T(8,128)(2,1)} %param.9) | copy-start | bytes 786436
  5.2 18.9 %copy-start = (bf16[64,4,128,128]{3,2,1,0:T(8,128)(2,1)S(1)}, bf16[64,4,128,128]{3,2,1,0:T(8,128)(2,1)}, u32[]{:S(2)}) copy-start(bf16[64,4,128,128]{3,2,1,0:T(8,128)(2,1)} %tiles.7) | copy-start | bytes 25165828
  8.2 15.8 %copy-start.6 = (s32[64,4]{0,1:T(4,128)S(1)}, s32[64,4]{0,1:T(4,128)}, u32[]{:S(2)}) copy-start(s32[64,4]{0,1:T(4,128)} %param.11) | copy-start | bytes 3076
  8.2 15.8 %collective-permute-start = (bf16[91,16,128]{2,1,0:T(8,128)(2,1)S(1)}, bf16[91,16,128]{2,1,0:T(8,128)(2,1)S(1)}, u32[]{:S(2)}, u32[]{:S(2)}) collective-permute-start(bf16[91,16,128]{2,1,0:T(8,128)(2,1)S(1)} %get-tuple-element.28), channel_id=1, source_target_pairs={{0,4},{8,12},{16,20},{24,28},{4,0},{12,8},{20,16},{28,24},{1,5},{9... | collective-permute-start | bytes 1118216 | tf_op jit(solution)/shard_map/ppermute | solution.py:461
  9.8 2.3 %collective-permute-start.1 = (bf16[75,16,128]{2,1,0:T(8,128)(2,1)S(1)}, bf16[75,16,128]{2,1,0:T(8,128)(2,1)S(1)}, u32[]{:S(2)}, u32[]{:S(2)}) collective-permute-start(bf16[75,16,128]{2,1,0:T(8,128)(2,1)S(1)} %get-tuple-element.30), channel_id=1, source_target_pairs={{4,8},{12,16},{20,24},{8,4},{16,12},{24,20},{5,9},{13,17},{21,25},... | collective-permute-start | bytes 921608 | tf_op jit(solution)/shard_map/ppermute | solution.py:462
  10.5 1.6 %collective-permute-start.2 = (bf16[16,8192]{1,0:T(8,128)(2,1)S(1)}, bf16[16,8192]{1,0:T(8,128)(2,1)S(1)}, u32[]{:S(2)}, u32[]{:S(2)}) collective-permute-start(bf16[16,8192]{1,0:T(8,128)(2,1)S(1)} %bitcast.14), channel_id=1, source_target_pairs={{0,1},{1,0},{2,3},{3,2},{4,5},{5,4},{6,7},{7,6},{8,9},{9,8},{10,11... | collective-permute-start | bytes 786440 | tf_op jit(solution)/shard_map/ppermute | solution.py:468
  10.6 13.5 %collective-permute-start.4 = (bf16[16,8192]{1,0:T(8,128)(2,1)S(1)}, bf16[16,8192]{1,0:T(8,128)(2,1)S(1)}, u32[]{:S(2)}, u32[]{:S(2)}) collective-permute-start(bf16[16,8192]{1,0:T(8,128)(2,1)S(1)} %collective-permute-done.3.basis_c), channel_id=1, source_target_pairs={{0,1},{1,0},{2,3},{3,2},{4,5},{5,4},{6,7},{7,6},{8,9},{9,8},{10,11... | collective-permute-start | bytes 786440 | tf_op jit(solution)/shard_map/ppermute | solution.py:468
  24.1 15.8 %copy-start.1 = (bf16[8,3,128,128]{3,2,1,0:T(8,128)(2,1)S(1)}, bf16[8,3,128,128]{3,2,1,0:T(8,128)(2,1)}, u32[]{:S(2)}) copy-start(bf16[8,3,128,128]{3,2,1,0:T(8,128)(2,1)} %mid_tiles.7) | copy-start | bytes 2359300
  27.0 5.3 %collective-permute-start.8 = (bf16[38,16,128]{2,1,0:T(8,128)(2,1)S(1)}, bf16[38,16,128]{2,1,0:T(8,128)(2,1)S(1)}, u32[]{:S(2)}, u32[]{:S(2)}) collective-permute-start(bf16[38,16,128]{2,1,0:T(8,128)(2,1)S(1)} %get-tuple-element.35.a), channel_id=1, source_target_pairs={{0,2},{1,3},{2,0},{3,1},{4,6},{5,7},{6,4},{7,5},{8,10},{9,11},{10,... | collective-permute-start | bytes 466952 | tf_op jit(solution)/shard_map/ppermute | solution.py:468
  27.6 12.3 %collective-permute-start.5 = (bf16[65,16,128]{2,1,0:T(8,128)(2,1)S(1)}, bf16[65,16,128]{2,1,0:T(8,128)(2,1)S(1)}, u32[]{:S(2)}, u32[]{:S(2)}) collective-permute-start(bf16[65,16,128]{2,1,0:T(8,128)(2,1)S(1)} %get-tuple-element.33), channel_id=1, source_target_pairs={{0,4},{8,12},{16,20},{24,28},{4,0},{12,8},{20,16},{28,24},{1,5},{9... | collective-permute-start | bytes 798728 | tf_op jit(solution)/shard_map/ppermute | solution.py:461
  30.1 5.4 %collective-permute-start.6 = (bf16[64,16,128]{2,1,0:T(8,128)(2,1)S(1)}, bf16[64,16,128]{2,1,0:T(8,128)(2,1)S(1)}, u32[]{:S(2)}, u32[]{:S(2)}) collective-permute-start(bf16[64,16,128]{2,1,0:T(8,128)(2,1)S(1)} %get-tuple-element.34.own), channel_id=1, source_target_pairs={{4,8},{12,16},{20,24},{8,4},{16,12},{24,20},{5,9},{13,17},{21,25},... | collective-permute-start | bytes 786440 | tf_op jit(solution)/shard_map/ppermute | solution.py:462
  30.7 1.5 %collective-permute-start.7 = (bf16[38,16,128]{2,1,0:T(8,128)(2,1)S(1)}, bf16[38,16,128]{2,1,0:T(8,128)(2,1)S(1)}, u32[]{:S(2)}, u32[]{:S(2)}) collective-permute-start(bf16[38,16,128]{2,1,0:T(8,128)(2,1)S(1)} %get-tuple-element.35.a), channel_id=1, source_target_pairs={{0,1},{1,0},{2,3},{3,2},{4,5},{5,4},{6,7},{7,6},{8,9},{9,8},{10,11... | collective-permute-start | bytes 466952 | tf_op jit(solution)/shard_map/ppermute | solution.py:468
  32.3 1.4 %collective-permute-start.9 = (bf16[38,16,128]{2,1,0:T(8,128)(2,1)S(1)}, bf16[38,16,128]{2,1,0:T(8,128)(2,1)S(1)}, u32[]{:S(2)}, u32[]{:S(2)}) collective-permute-start(bf16[38,16,128]{2,1,0:T(8,128)(2,1)S(1)} %collective-permute-done.8.c), channel_id=1, source_target_pairs={{0,1},{1,0},{2,3},{3,2},{4,5},{5,4},{6,7},{7,6},{8,9},{9,8},{10,11... | collective-permute-start | bytes 466952 | tf_op jit(solution)/shard_map/ppermute | solution.py:468
  39.9 18.7 %copy-start.2 = (f32[128,1024]{1,0:T(8,128)S(1)}, f32[128,1024]{1,0:T(8,128)}, u32[]{:S(2)}) copy-start(f32[128,1024]{1,0:T(8,128)} %inverse_rows.3) | copy-start | bytes 1572868
  59.8 7.4 %collective-permute-start.10 = (bf16[9,16,128]{2,1,0:T(8,128)(2,1)S(1)}, bf16[9,16,128]{2,1,0:T(8,128)(2,1)S(1)}, u32[]{:S(2)}, u32[]{:S(2)}) collective-permute-start(bf16[9,16,128]{2,1,0:T(8,128)(2,1)S(1)} %get-tuple-element.42), channel_id=1, source_target_pairs={{0,4},{8,12},{16,20},{24,28},{4,0},{12,8},{20,16},{28,24},{1,5},{9... | collective-permute-start | bytes 110600 | tf_op jit(solution)/shard_map/ppermute | solution.py:461
  60.0 7.2 %collective-permute-start.11 = (bf16[9,16,128]{2,1,0:T(8,128)(2,1)S(1)}, bf16[9,16,128]{2,1,0:T(8,128)(2,1)S(1)}, u32[]{:S(2)}, u32[]{:S(2)}) collective-permute-start(bf16[9,16,128]{2,1,0:T(8,128)(2,1)S(1)} %get-tuple-element.43), channel_id=1, source_target_pairs={{4,8},{12,16},{20,24},{8,4},{16,12},{24,20},{5,9},{13,17},{21,25},... | collective-permute-start | bytes 110600 | tf_op jit(solution)/shard_map/ppermute | solution.py:462
  60.6 6.6 %collective-permute-start.12 = (bf16[16,128]{1,0:T(8,128)(2,1)S(1)}, bf16[16,128]{1,0:T(8,128)(2,1)S(1)}, u32[]{:S(2)}, u32[]{:S(2)}) collective-permute-start(bf16[16,128]{1,0:T(8,128)(2,1)S(1)} %get-tuple-element.44), channel_id=1, source_target_pairs={{0,8},{4,12},{8,0},{12,4},{16,24},{20,28},{24,16},{28,20},{1,9},{5... | collective-permute-start | bytes 12296 | tf_op jit(solution)/shard_map/ppermute | solution.py:625
  65.3 1.9 %collective-permute-start.13 = (bf16[16,128]{1,0:T(8,128)(2,1)S(1)}, bf16[16,128]{1,0:T(8,128)(2,1)S(1)}, u32[]{:S(2)}, u32[]{:S(2)}) collective-permute-start(bf16[16,128]{1,0:T(8,128)(2,1)S(1)} %get-tuple-element.45), channel_id=1, source_target_pairs={{8,16},{12,20},{16,8},{20,12},{9,17},{13,21},{17,9},{21,13},{10,18... | collective-permute-start | bytes 12296 | tf_op jit(solution)/shard_map/ppermute | solution.py:626

commit v4 on v3

--- a/solution.py
+++ b/solution.py
@@ -18,6 +18,10 @@
 MESSAGE = 704
 FIRST_LIMIT = 52
 MID_LIMIT = 8
+
+
+def dot_nn(a, b):
+    return jnp.dot(a, b, preferred_element_type=F32)
 
 
 def dot_nt(a, b):
@@ -76,11 +80,10 @@
                 )
             )
     whole.start()
-    copy(0).start()
+    for part in range(parts):
+        copy(part).start()
     for small in smalls:
         small.start()
-    for part in range(1, parts):
-        copy(part).start()
     eye = eye_mask(ext)
     for small in smalls:
         small.wait()
@@ -124,16 +127,90 @@
             far_out[g] = value
 
 
-def hot_kernel(after, owner, hot_out):
+def plan_kernel(place, index, after, owner, hot_out, plan):
     del after
     blocks, ext = owner.shape
+    first = place[0] * blocks
+    zero = 3 * blocks
+
+    def row(g, most):
+        away, block = [], []
+        for s in range(1, 4):
+            at = index[s, g] - first
+            own = jnp.logical_and(at >= 0, at < blocks)
+            away.append(jnp.where(own, 0, 1))
+            block.append(at + blocks)
+        count = away[0] + away[1] + away[2]
+        one = jnp.where(away[0] == 1, 0, jnp.where(away[1] == 1, 1, 2))
+        two = jnp.where(away[0] + away[1] == 2, 1, 2)
+        pick = lambda k: jnp.where(k == 0, block[0], jnp.where(k == 1, block[1], block[2]))
+        plan[0, g] = one + 1
+        plan[1, g] = jnp.where(count >= 1, pick(one), zero)
+        plan[2, g] = two + 1
+        plan[3, g] = jnp.where(count >= 2, pick(two), zero)
+        plan[4, g] = 0
+        return jnp.maximum(most, count)
+
+    plan[4, 0] = lax.fori_loop(0, blocks, row, 0)
     _, hi = split(owner[...], ext)
     for g in range(blocks):
         hot_out[:, g * ext : (g + 1) * ext] = one_hot(hi[g : g + 1, :], ext)
 
 
+def own_rows(index, place, own, window, slots):
+    blocks = own.shape[0]
+    window[0:blocks] = own[...]
+    window[blocks] = jnp.zeros_like(window[blocks])
+    first = place[0] * blocks
+
+    def local(s, g):
+        at = index[s, g] - first
+        return jnp.where(jnp.logical_and(at >= 0, at < blocks), at, blocks)
+
+    def row(g):
+        picked = [window[g]] + [window[local(s, g)] for s in range(1, slots)]
+        return jnp.concatenate(picked, axis=1)
+
+    return row
+
+
+def own_first_kernel(index, place, tiles, own, out, turned_out, window):
+    blocks, slots = tiles.shape[:2]
+    row = own_rows(index, place, own, window, slots)
+    for g in range(blocks):
+        turned = [tiles[g, s].T for s in range(slots)]
+        for s in range(slots):
+            turned_out[g, s] = turned[s]
+        out[g] = dot_nn(row(g), jnp.concatenate(turned, axis=0))
+
+
+def own_kernel(index, place, turned, own, out, window):
+    blocks, slots = turned.shape[:2]
+    row = own_rows(index, place, own, window, slots)
+    for g in range(blocks):
+        out[g] = dot_nn(row(g), jnp.concatenate([turned[g, s] for s in range(slots)], axis=0))
+
+
+def for_rows(index, plan, offset, tiles, window, part, blocks, then):
+    window[3 * blocks] = jnp.zeros_like(window[3 * blocks])
+
+    @pl.when(plan[4, 0] <= 2)
+    def _():
+        for g in range(blocks):
+            picked = [window[plan[1, g]], window[plan[3, g]]]
+            matched = [tiles[g, plan[0, g]], tiles[g, plan[2, g]]]
+            added = dot_nn(jnp.concatenate(picked, axis=1), jnp.concatenate(matched, axis=0))
+            then(g, part[g] + added)
+
+    @pl.when(plan[4, 0] > 2)
+    def _():
+        @pl.loop(0, blocks)
+        def _(g):
+            then(g, fine_row(index, offset, tiles, window, g))
+
+
 def sides_kernel(
-    place, a, b, c, d, left_out, right_out, inverse_out, hot_left, hot_right, buffer
+    place, a, b, c, d, left_out, right_out, inverse_out, buffer
 ):
     width, ext = a.shape[1:]
     extra = left_out.shape[0] // (4 * width)
@@ -150,8 +227,13 @@
             rows = slice(n * share + i * width, n * share + (i + 1) * width)
             for k in range(wide):
                 inverse_out[rows, k * ext : (k + 1) * ext] = buffer[n, 2 * extra + i * wide + k]
+
+
+def side_hot_kernel(after, from_left, from_right, hot_left, hot_right):
+    del after
+    ext = hot_left.shape[0]
     blocks = hot_left.shape[1] // ext
-    for message, hot in ((left_out, hot_left), (right_out, hot_right)):
+    for message, hot in ((from_left, hot_left), (from_right, hot_right)):
         hi = as_int(message[HI_AT : HI_AT + blocks, :])
         for g in range(blocks):
             hot[:, g * ext : (g + 1) * ext] = one_hot(hi[g : g + 1, :], ext)
@@ -167,28 +249,30 @@
 def fine_row(index, offset, tiles, window, g):
     slots = tiles.shape[1]
     picked = [window[index[s, g] - offset] for s in range(slots)]
-    return dot_nt(
+    return dot_nn(
         jnp.concatenate(picked, axis=1),
-        jnp.concatenate([tiles[g, s] for s in range(slots)], axis=1),
+        jnp.concatenate([tiles[g, s] for s in range(slots)], axis=0),
     )
 
 
 def second_kernel(
-    index, place, tiles, near, own, far, res, winv, hot, basis_b, basis_c, basis_d, b_out, b16_out,
-    b16_too, mine_out, window,
+    index, plan, place, tiles, near, own, far, part, res, winv, hot, basis_b, basis_c, basis_d, b_out,
+    b16_out, b16_too, mine_out, window,
 ):
     del hot, basis_b, basis_c, basis_d
     blocks, ext = own.shape[0], own.shape[2]
     offset = (place[0] - 1) * blocks
     fill_window(window, near, own, far, place[0])
-    for g in range(blocks):
-        product = fine_row(index, offset, tiles, window, g)
+
+    def finish_row(g, product):
         w = winv[pl.ds(g, 1), :]
         r = res[g]
         b = w * r + w * (r - product)
         b_out[g] = b
         b16_out[g] = b.astype(BF16)
         b16_too[g] = b.astype(BF16)
+
+    for_rows(index, plan, offset, tiles, window, part, blocks, finish_row)
     for n in range(blocks, b16_too.shape[0]):
         b16_too[n] = jnp.zeros_like(b16_too[n])
     odd = place[0] % 2
@@ -242,7 +326,7 @@
 
 
 def third_kernel(
-    index, place, tiles, near, own, far, res, owner, hot, mid_tiles, mid_owner, from_left,
+    index, plan, place, tiles, near, own, far, part, res, owner, hot, mid_tiles, mid_owner, from_left,
     from_right, fres_out, u_out, bpart_out, send, window, spread_rows,
 ):
     blocks, ext = own.shape[0], own.shape[2]
@@ -252,13 +336,17 @@
     peers = place[1]
     offset = (me - 1) * blocks
     fill_window(window, near, own, far, place[0])
-    for g in range(blocks):
-        product = fine_row(index, offset, tiles, window, g)
+
+    def finish_row(g, product):
         r = res[g] - product
         fres_out[g] = r
         lo, _ = split(owner[pl.ds(g, 1), :] - me * (mids * ext), ext)
-        spread_rows[:, g * ext : (g + 1) * ext] = spread(r, lo, mids)
-    total = dot_nt(spread_rows[...], hot[...])
+        at = g * ext if isinstance(g, int) else pl.multiple_of(g * ext, ext)
+        spread_rows[:, pl.ds(at, ext)] = spread(r, lo, mids)
+
+    for_rows(index, plan, offset, tiles, window, part, blocks, finish_row)
+    quarters = [slice(n * blocks // 4 * ext, (n + 1) * blocks // 4 * ext) for n in range(4)]
+    total = sum(dot_nt(spread_rows[:, q], hot[:, q]) for q in quarters)
     u = [total[b * width : (b + 1) * width] for b in range(mids)]
     eye = eye_mask(ext)
     winv = mid_inverse(mid_tiles, eye)
@@ -269,14 +357,14 @@
     winv_right = inverse(diag_row(right_mid, eye), has_right)
     a = [winv[b] * u[b] for b in range(mids)]
     a16 = {b: a[b].astype(BF16) for b in range(mids)}
-    part = {}
+    mine = {}
     for b in range(mids):
-        part[b] = a[b] + winv[b] * (u[b] - mid_product(mid_tiles, a16, b))
+        mine[b] = a[b] + winv[b] * (u[b] - mid_product(mid_tiles, a16, b))
         u_out[b] = u[b]
-        bpart_out[b] = part[b]
-    part[-1] = -winv_left * dot_nt(a16[0], left_next)
-    part[mids] = -winv_right * dot_nt(a16[mids - 1], right_prev)
-    p16 = {b: v.astype(BF16) for b, v in part.items()}
+        bpart_out[b] = mine[b]
+    mine[-1] = -winv_left * dot_nt(a16[0], left_next)
+    mine[mids] = -winv_right * dot_nt(a16[mids - 1], right_prev)
+    p16 = {b: v.astype(BF16) for b, v in mine.items()}
     rest = {b: u[b] - mid_product(mid_tiles, p16, b) for b in range(mids)}
     rest[-1] = -(dot_nt(p16[-1], left_mid) + dot_nt(p16[0], left_next))
     rest[-2] = -dot_nt(p16[-1], left_far)
@@ -378,7 +466,7 @@
 def last_kernel(
     index, place, tiles, near, far, nexts, beyond, dpart, c_edges, mid_tiles, owner, hot_own, from_left, hot_left,
     from_right, hot_right, b_in, fres, winv, basis_a, basis_b, basis_c, basis_d, out, gram_out, window,
-    added, rounded, grams,
+    added, rounded, grams, result, sems,
 ):
     blocks, width, ext = b_in.shape
     mids = mid_tiles.shape[0]
@@ -431,12 +519,21 @@
                     added[g + n] = half
                 window[base + g + n] = half.astype(BF16)
     offset = (me - 1) * blocks
+    count = sems.shape[0]
+    per = blocks // count
+
+    def copy(part):
+        cols = pl.ds(part * per * ext, per * ext)
+        return pltpu.make_async_copy(result.at[:, cols], out.at[:, cols], sems.at[part])
+
     for g in range(blocks):
         product = fine_row(index, offset, tiles, window, g)
         value = b_in[g] + added[g] + winv[pl.ds(g, 1), :] * (fres[g] - product)
         cols = slice(g * ext, (g + 1) * ext)
-        out[:, cols] = value
+        result[:, cols] = value
         rounded[:, cols] = value.astype(BF16)
+        if (g + 1) % per == 0:
+            copy((g + 1) // per - 1).start()
     for n, piece in enumerate((basis_a, basis_b, basis_c, basis_d)):
         grams[place[2] ^ n] = dot_nt(rounded[...], piece[...])
     gram = jnp.concatenate(
@@ -444,6 +541,8 @@
     )
     for d in range(gram_out.shape[0]):
         gram_out[d] = gram
+    for part in range(count):
+        copy(part).wait()
 
 
 def sum_kernel(got, out):
@@ -520,20 +619,30 @@
     )(place, res, fine_tiles, mid_tiles, owner, mid_rows, coarse_inverse)
 
     near, far = halo(for_partner, for_other)
-    tiles = fine_tiles
-    hot_own = pl.pallas_call(
-        hot_kernel,
-        in_specs=[ANY, VM],
-        out_specs=VM,
-        out_shape=shape((ext, count), BF16),
+    hot_own, plan = pl.pallas_call(
+        plan_kernel,
+        in_specs=[SM, SM, ANY, VM],
+        out_specs=[VM, SM],
+        out_shape=[shape((ext, count), BF16), shape((5, blocks), jnp.int32)],
         name="one_hot_rows",
         **params(4, count * ext, 4 * tile_bytes),
-    )(winv, owner)
+    )(place, index, winv, owner)
+
+    part_shape = shape((blocks, width, ext), F32)
+    part, tiles = pl.pallas_call(
+        own_first_kernel,
+        in_specs=[SM, SM, VM, VM],
+        out_specs=[VM, VM],
+        out_shape=[part_shape, shape(fine_tiles.shape, BF16)],
+        scratch_shapes=[pltpu.VMEM((blocks + 1, width, ext), BF16)],
+        name="own_part_and_turned_tiles",
+        **params(4, ext, ext),
+    )(index, place, fine_tiles, a16)
     basis_pieces = [basis.T] + from_columns(basis.T)
 
     b32, b16, b16_too, mine = pl.pallas_call(
         second_kernel,
-        in_specs=[SM, SM] + [VM] * 6 + [ANY] * 4,
+        in_specs=[SM] * 3 + [VM] * 7 + [ANY] * 4,
         out_specs=[VM] * 4,
         out_shape=[
             shape((blocks, width, ext), F32),
@@ -541,22 +650,32 @@
             shape((blocks + 1, width, ext), BF16),
             shape((2 * extra + quarter, width, ext), BF16),
         ],
-        scratch_shapes=[pltpu.VMEM((3 * blocks, width, ext), BF16)],
+        scratch_shapes=[pltpu.VMEM((3 * blocks + 1, width, ext), BF16)],
         name="second_smoothing",
         **params(6, fine_flops, tile_bytes),
-    )(index, place, tiles, near, a16, far, res_blocks, winv, hot_own, *basis_pieces[1:])
+    )(
+        index, plan, place, tiles, near, a16, far, part, res_blocks, winv, hot_own,
+        *basis_pieces[1:],
+    )
 
     near, far = halo(b16_too, b16)
-    from_left, from_right, partner_rows, hot_left, hot_right = pl.pallas_call(
+    part = pl.pallas_call(
+        own_kernel,
+        in_specs=[SM, SM, VM, VM],
+        out_specs=VM,
+        out_shape=part_shape,
+        scratch_shapes=[pltpu.VMEM((blocks + 1, width, ext), BF16)],
+        name="own_part_of_residual",
+        **params(4, ext, ext),
+    )(index, place, tiles, b16)
+    from_left, from_right, partner_rows = pl.pallas_call(
         sides_kernel,
         in_specs=[SM] + [VM] * 4,
-        out_specs=[VM] * 5,
+        out_specs=[VM] * 3,
         out_shape=[
             shape((MESSAGE, ext), BF16),
             shape((MESSAGE, ext), BF16),
             shape(coarse_inverse.shape, BF16),
-            shape((ext, count), BF16),
-            shape((ext, count), BF16),
         ],
         scratch_shapes=[pltpu.VMEM((4, 2 * extra + quarter, width, ext), BF16)],
         name="side_messages",
@@ -565,7 +684,7 @@
 
     fres, u, bpart, send = pl.pallas_call(
         third_kernel,
-        in_specs=[SM, SM] + [VM] * 11,
+        in_specs=[SM] * 3 + [VM] * 12,
         out_specs=[VM] * 4,
         out_shape=[
             shape((blocks, width, ext), F32),
@@ -574,14 +693,14 @@
             shape((peers, 5, width, ext), BF16),
         ],
         scratch_shapes=[
-            pltpu.VMEM((3 * blocks, width, ext), BF16),
+            pltpu.VMEM((3 * blocks + 1, width, ext), BF16),
             pltpu.VMEM((mids * width, count), BF16),
         ],
         name="residual_and_restriction",
         **params(10, fine_flops, tile_bytes),
     )(
-        index, place, tiles, near, b16, far, res_blocks, owner, hot_own, mid_tiles, mid_rows,
-        from_left, from_right,
+        index, plan, place, tiles, near, b16, far, part, res_blocks, owner, hot_own, mid_tiles,
+        mid_rows, from_left, from_right,
     )
 
     got = lax.all_to_all(send, "rows", 0, 0)
@@ -605,14 +724,14 @@
     )
 
     return finish(
-        place, index, tiles, sends, dpart, c_edges, mid_tiles, owner, hot_own, from_left, hot_left,
-        from_right, hot_right, b32, fres, winv, basis_pieces,
+        place, index, tiles, sends, dpart, c_edges, mid_tiles, owner, hot_own, from_left, from_right,
+        b32, fres, winv, basis_pieces,
     )
 
 
 def finish(
-    place, index, tiles, sends, dpart, c_edges, mid_tiles, owner, hot_own, from_left, hot_left,
-    from_right, hot_right, b32, fres, winv, basis_pieces,
+    place, index, tiles, sends, dpart, c_edges, mid_tiles, owner, hot_own, from_left, from_right, b32,
+    fres, winv, basis_pieces,
 ):
     peers = lax.axis_size("rows")
     blocks, width, ext = b32.shape
@@ -624,10 +743,18 @@
     pairs += [(j, i) for i, j in pairs]
     nexts = lax.ppermute(sends[2], "rows", [(i, i ^ 2) for i in range(peers)])
     beyond = lax.ppermute(sends[3], "rows", pairs)
+    hot_left, hot_right = pl.pallas_call(
+        side_hot_kernel,
+        in_specs=[ANY, VM, VM],
+        out_specs=[VM] * 2,
+        out_shape=[shape((ext, count), BF16)] * 2,
+        name="side_one_hot_rows",
+        **params(4, ext, ext),
+    )(c_edges, from_left, from_right)
     out, grams = pl.pallas_call(
         last_kernel,
         in_specs=[SM, SM] + [VM] * 21,
-        out_specs=[VM, VM],
+        out_specs=[HBM, VM],
         out_shape=[
             shape((width, count), F32),
             shape((peers, width, ext), F32),
@@ -637,6 +764,8 @@
             pltpu.VMEM((blocks, width, ext), F32),
             pltpu.VMEM((width, count), BF16),
             pltpu.VMEM((4, width, width), F32),
+            pltpu.VMEM((width, count), F32),
+            pltpu.SemaphoreType.DMA((4,)),
         ],
         name="prolongation_and_last_smoothing",
         **params(8, 2 * tiles.size * width, tiles.size * 2),

time: 86.3 us -> 82.5 us (0.956)
  waiting for transfers between devices: 20.9 us -> 13.8 us
  Pallas kernels: 21.5 us -> 24.4 us
    ppermute x3, waiting for transfers between devices: 16.4 us -> 12.4 us  [halo(): near = lax.ppermute(for_partner, 'rows', swap(even))]
    pallas_call x5 -> x8, Pallas kernels: 16.5 us -> 19.3 us  [the longest x1 4.46 us: finish(): pl.pallas_call(last_kernel, in_specs=[SM, SM] + [VM] * 21, out_specs=[HBM...]
    ppermute x6, waiting for transfers between devices: 3.29 us -> 1.34 us  [from_columns(): lax.ppermute(v, 'cols', [(i, i ^ n) for i in range(peers)])]
    ppermute x1, waiting for transfers between devices: 1.23 us -> 0.01 us  [finish(): nexts = lax.ppermute(sends[2], 'rows', [(i, i ^ 2) for i in range(peers)])]
  transfers between devices with their start and end apart: 14 -> 14, of which waited for: 6 -> 3; matrix products, arithmetic and copies ran while one was open for 0% -> 0% of each run, Pallas kernels for 6% -> 15%
where the time goes in v4:
time: 82.5 us; the launch traced here: 82.2 us
  blocking collectives  25.4 us (31%)
  Pallas kernels  24.4 us (30%)
  starting transfers between devices  16.1 us (20%)
  waiting for transfers between devices  13.8 us (17%)
  local copies, waits for them, and re-layouts  1.47 us (2%)
  between operations  0.83 us (1%)
    all_to_all x1, blocking collectives, on_device(): got = lax.all_to_all(send, 'rows', 0, 0)  13.2 us
    ppermute x3, waiting for transfers between devices, halo(): near = lax.ppermute(for_partner, 'rows', swap(even))  12.4 us
    all_to_all x1, blocking collectives, finish(): lax.all_to_all(grams, 'rows', 0, 0)  12.2 us
    ppermute x1, starting transfers between devices, finish(): nexts = lax.ppermute(sends[2], 'rows', [(i, i ^ 2) for i in range(peers)])  4.68 us
    pallas_call x1, Pallas kernels, finish(): pl.pallas_call(last_kernel, in_specs=[SM, SM] + [VM] * 21, out_specs=[HBM...  4.46 us
    pallas_call x1, Pallas kernels, on_device(): pl.pallas_call(third_kernel, in_specs=[SM] * 3 + [VM] * 12, out_specs=[VM...  4.25 us
    ppermute x3, starting transfers between devices, halo(): near = lax.ppermute(for_partner, 'rows', swap(even))  4.25 us
    ppermute x6, starting transfers between devices, from_columns(): lax.ppermute(v, 'cols', [(i, i ^ n) for i in range(peers)])  4.24 us
  transfers between devices with their start and end apart: 14, of which 3 were waited for; matrix products, arithmetic and copies ran while one was open for 0% of the time, Pallas kernels for 15%

profile of v4, /device:TPU:0, one launch (start us, length us, event | category | flops | bytes accessed | tf_op | source)
XLA Modules:
  0.0 82.2 jit_solution(12706654658184603334)
XLA Ops:
  0.6 3.0 %collective-permute-start.3 = (bf16[16,8192]{1,0:T(8,128)(2,1)}, bf16[16,8192]{1,0:T(8,128)(2,1)S(1)}, u32[]{:S(2)}, u32[]{:S(2)}) collective-permute-start(bf16[16,8192]{1,0:T(8,128)(2,1)} %bitcast.13), channel_id=1, source_target_pairs={{0,2},{1,3},{2,0},{3,1},{4,6},{5,7},{6,4},{7,5},{8,10},{9,11},{10,... | collective-permute-start | bytes 786440 | tf_op jit(solution)/shard_map/ppermute | solution.py:567
  3.6 0.1 pad_add_fusion.place
  3.7 0.8 copy-done.3
  4.5 0.7 copy-done.6
  5.2 3.2 %first_smoothing.1 = (bf16[64,16,128]{2,1,0:T(8,128)(2,1)S(1)}, bf16[91,16,128]{2,1,0:T(8,128)(2,1)S(1)}, bf16[75,16,128]{2,1,0:T(8,128)(2,1)S(1)}, f32[64,128]{1,0:T(8,128)S(1)}, f32[64,16,128]{2,1,0:T(8,128)S(1)}) custom-call(s32[3]{0:T(128)S(1)} %pad_add_fusion.place, f32[16,8192]{1,0:T(8,128)} %bitcast.25, bf16[64,4,128,128]{3,2,1,0:T(8,128)(2,1)} %tiles.3, ...), custom_call_target="tpu_custom_call" | custom-call | flops 1048576 | bytes 2097152 | tf_op jit(solution)/shard_map/first_smoothing/pallas_call | solution.py:596
  8.4 1.6 %collective-permute-start = (bf16[91,16,128]{2,1,0:T(8,128)(2,1)S(1)}, bf16[91,16,128]{2,1,0:T(8,128)(2,1)S(1)}, u32[]{:S(2)}, u32[]{:S(2)}) collective-permute-start(bf16[91,16,128]{2,1,0:T(8,128)(2,1)S(1)} %get-tuple-element.36), channel_id=1, source_target_pairs={{0,4},{8,12},{16,20},{24,28},{4,0},{12,8},{20,16},{28,24},{1,5},{9... | collective-permute-start | bytes 1118216 | tf_op jit(solution)/shard_map/ppermute | solution.py:560
  10.0 0.7 collective-permute-start.1
  10.7 0.0 copy-done.4
  10.7 0.1 collective-permute-start.2
  10.8 0.0 collective-permute-done.3.basis_c
  10.8 0.5 collective-permute-start.4
  11.3 0.0 copy-done
  11.3 0.0 copy-done.5
  11.3 2.9 %own_part_and_turned_tiles.1 = (f32[64,16,128]{2,1,0:T(8,128)S(1)}, bf16[64,4,128,128]{3,2,1,0:T(8,128)(2,1)S(1)}) custom-call(s32[4,64]{1,0:T(4,128)S(1)} %bitcast.16, s32[3]{0:T(128)S(1)} %pad_add_fusion.place, bf16[64,4,128,128]{3,2,1,0:T(8,128)(2,1)S(1)} %copy-done, bf16[64,16,128]{2,1,0:T(8,128)(2,1)S(1)} %get-tuple-element.32.own), custom_call_target="tpu_custom_call" | custom-call | flops 128 | bytes 128 | tf_op jit(solution)/shard_map/own_part_and_turned_tiles/pallas_call | solution.py:632
  14.2 2.7 %one_hot_rows.1 = (bf16[128,8192]{1,0:T(8,128)(2,1)S(1)}, s32[5,64]{1,0:T(8,128)S(1)}) custom-call(s32[3]{0:T(128)S(1)} %pad_add_fusion.place, s32[4,64]{1,0:T(4,128)S(1)} %bitcast.17, f32[64,128]{1,0:T(8,128)S(1)} %get-tuple-element.34.after.winv, s32[64,128]{1,0:T(8,128)S(1)} %bitcast.10), custom_call_target="tpu_custom_call" | custom-call | flops 1048576 | bytes 33554432 | tf_op jit(solution)/shard_map/one_hot_rows/pallas_call | solution.py:622
  16.9 0.0 collective-permute-done.2.basis_b
  16.9 0.0 collective-permute-done.1.far
  16.9 7.3 %collective-permute-done.near = bf16[91,16,128]{2,1,0:T(8,128)(2,1)S(1)} collective-permute-done((bf16[91,16,128]{2,1,0:T(8,128)(2,1)S(1)}, bf16[91,16,128]{2,1,0:T(8,128)(2,1)S(1)}, u32[]{:S(2)}, u32[]{:S(2)}) %collective-permute-start) | collective-permute-done | bytes 372768 | tf_op jit(solution)/shard_map/ppermute | solution.py:560
  24.2 0.0 collective-permute-done.4.basis_d
  24.2 1.5 %second_smoothing.1 = (f32[64,16,128]{2,1,0:T(8,128)S(1)}, bf16[64,16,128]{2,1,0:T(8,128)(2,1)S(1)}, bf16[65,16,128]{2,1,0:T(8,128)(2,1)S(1)}, bf16[38,16,128]{2,1,0:T(8,128)(2,1)S(1)}) custom-call(s32[4,64]{1,0:T(4,128)S(1)} %bitcast.18, s32[5,64]{1,0:T(8,128)S(1)} %get-tuple-element.35.plan, s32[3]{0:T(128)S(1)} %pad_add_fusion.place, ...), custom_call_target="tpu_custom_call" | custom-call | flops 134217728 | bytes 8388608 | tf_op jit(solution)/shard_map/second_smoothing/pallas_call | solution.py:643
  25.7 0.6 collective-permute-start.8
  26.3 2.5 %collective-permute-start.5 = (bf16[65,16,128]{2,1,0:T(8,128)(2,1)S(1)}, bf16[65,16,128]{2,1,0:T(8,128)(2,1)S(1)}, u32[]{:S(2)}, u32[]{:S(2)}) collective-permute-start(bf16[65,16,128]{2,1,0:T(8,128)(2,1)S(1)} %get-tuple-element.41), channel_id=1, source_target_pairs={{0,4},{8,12},{16,20},{24,28},{4,0},{12,8},{20,16},{28,24},{1,5},{9... | collective-permute-start | bytes 798728 | tf_op jit(solution)/shard_map/ppermute | solution.py:560
  28.8 0.8 collective-permute-start.6
  29.6 0.1 collective-permute-start.7
  29.7 1.3 %collective-permute-done.8.c = bf16[38,16,128]{2,1,0:T(8,128)(2,1)S(1)} collective-permute-done((bf16[38,16,128]{2,1,0:T(8,128)(2,1)S(1)}, bf16[38,16,128]{2,1,0:T(8,128)(2,1)S(1)}, u32[]{:S(2)}, u32[]{:S(2)}) %collective-permute-start.8) | collective-permute-done | bytes 155680 | tf_op jit(solution)/shard_map/ppermute | solution.py:567
  31.0 0.0 collective-permute-start.9
  31.0 1.8 %own_part_of_residual.1.part = f32[64,16,128]{2,1,0:T(8,128)S(1)} custom-call(s32[4,64]{1,0:T(4,128)S(1)} %bitcast.19, s32[3]{0:T(128)S(1)} %pad_add_fusion.place, bf16[64,4,128,128]{3,2,1,0:T(8,128)(2,1)S(1)} %get-tuple-element.33.tiles.turned, bf16[64,16,128]{2,1,0:T(8,128)(2,1)S(1)} %get-tuple-element.42.own), custom_call_target="tpu_custom_call" | custom-call | flops 128 | bytes 128 | tf_op jit(solution)/shard_map/own_part_of_residual/pallas_call | solution.py:662
  32.8 0.0 collective-permute-done.7.b
  32.8 0.0 collective-permute-done.9.d
  32.8 0.7 side_messages.1
  33.5 0.0 collective-permute-done.6.far
  33.5 5.1 %collective-permute-done.5.near = bf16[65,16,128]{2,1,0:T(8,128)(2,1)S(1)} collective-permute-done((bf16[65,16,128]{2,1,0:T(8,128)(2,1)S(1)}, bf16[65,16,128]{2,1,0:T(8,128)(2,1)S(1)}, u32[]{:S(2)}, u32[]{:S(2)}) %collective-permute-start.5) | collective-permute-done | bytes 266272 | tf_op jit(solution)/shard_map/ppermute | solution.py:560
  38.6 0.0 copy-done.1
  38.6 4.3 %residual_and_restriction.1 = (f32[64,16,128]{2,1,0:T(8,128)S(1)}, f32[8,16,128]{2,1,0:T(8,128)S(1)}, f32[8,16,128]{2,1,0:T(8,128)S(1)}, bf16[8,5,16,128]{3,2,1,0:T(8,128)(2,1)S(1)}) custom-call(s32[4,64]{1,0:T(4,128)S(1)} %bitcast.20, s32[5,64]{1,0:T(8,128)S(1)} %get-tuple-element.35.plan, s32[3]{0:T(128)S(1)} %pad_add_fusion.place, ...), custom_call_target="tpu_custom_call" | custom-call | flops 134217728 | bytes 8388608 | tf_op jit(solution)/shard_map/residual_and_restriction/pallas_call | solution.py:685
  42.9 13.2 %all_to_all.10.got = bf16[8,5,16,128]{3,2,1,0:T(8,128)(2,1)S(1)} all-to-all(bf16[8,5,16,128]{3,2,1,0:T(8,128)(2,1)S(1)} %get-tuple-element.46), channel_id=1, replica_groups=mesh['rows'=8,'cols'=4] {'rows'}, dimensions={0} | all-to-all | bytes 327680 | tf_op jit(solution)/shard_map/all_to_all | solution.py:706
  56.1 1.2 %coarse_and_mid_level.1 = (f32[8,16,128]{2,1,0:T(8,128)S(1)}, bf16[2,16,128]{2,1,0:T(8,128)(2,1)S(1)}, bf16[9,16,128]{2,1,0:T(8,128)(2,1)S(1)}, bf16[9,16,128]{2...) custom-call(s32[3]{0:T(128)S(1)} %pad_add_fusion.place, ...), custom_call_target="tpu_custom_call" | custom-call | flops 8388608 | bytes 524288 | tf_op jit(solution)/shard_map/coarse_and_mid_level/pallas_call | solution.py:707
  57.3 0.2 collective-permute-start.10
  57.5 0.7 collective-permute-start.11
  58.2 4.7 %collective-permute-start.12 = (bf16[16,128]{1,0:T(8,128)(2,1)S(1)}, bf16[16,128]{1,0:T(8,128)(2,1)S(1)}, u32[]{:S(2)}, u32[]{:S(2)}) collective-permute-start(bf16[16,128]{1,0:T(8,128)(2,1)S(1)} %get-tuple-element.52), channel_id=1, source_target_pairs={{0,8},{4,12},{8,0},{12,4},{16,24},{20,28},{24,16},{28,20},{1,9},{5... | collective-permute-start | bytes 12296 | tf_op jit(solution)/shard_map/ppermute | solution.py:744
  62.9 0.8 %collective-permute-start.13 = (bf16[16,128]{1,0:T(8,128)(2,1)S(1)}, bf16[16,128]{1,0:T(8,128)(2,1)S(1)}, u32[]{:S(2)}, u32[]{:S(2)}) collective-permute-start(bf16[16,128]{1,0:T(8,128)(2,1)S(1)} %get-tuple-element.53), channel_id=1, source_target_pairs={{8,16},{12,20},{16,8},{20,12},{9,17},{13,21},{17,9},{21,13},{10,18... | collective-permute-start | bytes 12296 | tf_op jit(solution)/shard_map/ppermute | solution.py:745
  63.7 1.1 %side_one_hot_rows.1 = (bf16[128,8192]{1,0:T(8,128)(2,1)S(1)}, bf16[128,8192]{1,0:T(8,128)(2,1)S(1)}) custom-call(bf16[2,16,128]{2,1,0:T(8,128)(2,1)S(1)} %get-tuple-element.55.after.c_edges, bf16[704,128]{1,0:T(8,128)(2,1)S(1)} %get-tuple-element.44.from_left, bf16[704,128]{1,0:T(8,128)(2,1)S(1)} %get-tuple-element.45.from_right), custom_call_target="tpu_custom_call" | custom-call | flops 128 | bytes 128 | tf_op jit(solution)/shard_map/side_one_hot_rows/pallas_call | solution.py:746
  64.8 0.0 collective-permute-done.12.nexts
  64.8 0.0 collective-permute-done.13.beyond
  64.8 0.0 collective-permute-done.10.near
  64.9 0.0 collective-permute-done.11.far
  64.9 4.5 %prolongation_and_last_smoothing.1 = (f32[16,8192]{1,0:T(8,128)}, f32[8,16,128]{2,1,0:T(8,128)S(1)}) custom-call(s32[4,64]{1,0:T(4,128)S(1)} %bitcast.21, s32[3]{0:T(128)S(1)} %pad_add_fusion.place, bf16[64,4,128,128]{3,2,1,0:T(8,128)(2,1)S(1)} %get-tuple-element.33.tiles.turned, bf16[9,16,128]{2,1,0:T(8,128)(2,1)S(1)} %collective-permute-done.10.near, ...), custom_call_target="tpu_custom_call" | custom-call | flops 134217728 | bytes 8388608 | tf_op jit(solution)/shard_map/prolongation_and_last_smoothing/pallas_call | solution.py:754
  69.3 12.2 %all_to_all.11.got = f32[8,16,128]{2,1,0:T(8,128)S(1)} all-to-all(f32[8,16,128]{2,1,0:T(8,128)S(1)} %get-tuple-element.61), channel_id=1, replica_groups=mesh['rows'=8,'cols'=4] {'rows'}, dimensions={0} | all-to-all | bytes 131072 | tf_op jit(solution)/shard_map/all_to_all | solution.py:783
  81.6 0.6 gram_sum.1
  (10 shorter events, 0.0 us)
Async XLA Ops:
  0.6 10.1 %collective-permute-start.3 = (bf16[16,8192]{1,0:T(8,128)(2,1)}, bf16[16,8192]{1,0:T(8,128)(2,1)S(1)}, u32[]{:S(2)}, u32[]{:S(2)}) collective-permute-start(bf16[16,8192]{1,0:T(8,128)(2,1)} %bitcast.13), channel_id=1, source_target_pairs={{0,2},{1,3},{2,0},{3,1},{4,6},{5,7},{6,4},{7,5},{8,10},{9,11},{10,... | collective-permute-start | bytes 786440 | tf_op jit(solution)/shard_map/ppermute | solution.py:567
  3.7 0.8 copy-start.3
  4.5 0.7 copy-start.6
  5.2 5.5 %copy-start.4 = (bf16[8192,16]{0,1:T(8,128)(2,1)S(1)}, bf16[8192,16]{0,1:T(8,128)(2,1)}, u32[]{:S(2)}) copy-start(bf16[8192,16]{0,1:T(8,128)(2,1)} %param.9) | copy-start | bytes 786436
  5.2 6.1 %copy-start = (bf16[64,4,128,128]{3,2,1,0:T(8,128)(2,1)S(1)}, bf16[64,4,128,128]{3,2,1,0:T(8,128)(2,1)}, u32[]{:S(2)}) copy-start(bf16[64,4,128,128]{3,2,1,0:T(8,128)(2,1)} %tiles.3) | copy-start | bytes 25165828
  5.2 6.1 %copy-start.5 = (s32[64,4]{0,1:T(4,128)S(1)}, s32[64,4]{0,1:T(4,128)}, u32[]{:S(2)}) copy-start(s32[64,4]{0,1:T(4,128)} %param.11) | copy-start | bytes 3076
  8.4 15.8 %collective-permute-start = (bf16[91,16,128]{2,1,0:T(8,128)(2,1)S(1)}, bf16[91,16,128]{2,1,0:T(8,128)(2,1)S(1)}, u32[]{:S(2)}, u32[]{:S(2)}) collective-permute-start(bf16[91,16,128]{2,1,0:T(8,128)(2,1)S(1)} %get-tuple-element.36), channel_id=1, source_target_pairs={{0,4},{8,12},{16,20},{24,28},{4,0},{12,8},{20,16},{28,24},{1,5},{9... | collective-permute-start | bytes 1118216 | tf_op jit(solution)/shard_map/ppermute | solution.py:560
  10.0 6.9 %collective-permute-start.1 = (bf16[75,16,128]{2,1,0:T(8,128)(2,1)S(1)}, bf16[75,16,128]{2,1,0:T(8,128)(2,1)S(1)}, u32[]{:S(2)}, u32[]{:S(2)}) collective-permute-start(bf16[75,16,128]{2,1,0:T(8,128)(2,1)S(1)} %get-tuple-element.37), channel_id=1, source_target_pairs={{4,8},{12,16},{20,24},{8,4},{16,12},{24,20},{5,9},{13,17},{21,25},... | collective-permute-start | bytes 921608 | tf_op jit(solution)/shard_map/ppermute | solution.py:561
  10.7 6.2 %collective-permute-start.2 = (bf16[16,8192]{1,0:T(8,128)(2,1)S(1)}, bf16[16,8192]{1,0:T(8,128)(2,1)S(1)}, u32[]{:S(2)}, u32[]{:S(2)}) collective-permute-start(bf16[16,8192]{1,0:T(8,128)(2,1)S(1)} %bitcast.14), channel_id=1, source_target_pairs={{0,1},{1,0},{2,3},{3,2},{4,5},{5,4},{6,7},{7,6},{8,9},{9,8},{10,11... | collective-permute-start | bytes 786440 | tf_op jit(solution)/shard_map/ppermute | solution.py:567
  10.8 13.5 %collective-permute-start.4 = (bf16[16,8192]{1,0:T(8,128)(2,1)S(1)}, bf16[16,8192]{1,0:T(8,128)(2,1)S(1)}, u32[]{:S(2)}, u32[]{:S(2)}) collective-permute-start(bf16[16,8192]{1,0:T(8,128)(2,1)S(1)} %collective-permute-done.3.basis_c), channel_id=1, source_target_pairs={{0,1},{1,0},{2,3},{3,2},{4,5},{5,4},{6,7},{7,6},{8,9},{9,8},{10,11... | collective-permute-start | bytes 786440 | tf_op jit(solution)/shard_map/ppermute | solution.py:567
  25.7 5.3 %collective-permute-start.8 = (bf16[38,16,128]{2,1,0:T(8,128)(2,1)S(1)}, bf16[38,16,128]{2,1,0:T(8,128)(2,1)S(1)}, u32[]{:S(2)}, u32[]{:S(2)}) collective-permute-start(bf16[38,16,128]{2,1,0:T(8,128)(2,1)S(1)} %get-tuple-element.43.a), channel_id=1, source_target_pairs={{0,2},{1,3},{2,0},{3,1},{4,6},{5,7},{6,4},{7,5},{8,10},{9,11},{10,... | collective-permute-start | bytes 466952 | tf_op jit(solution)/shard_map/ppermute | solution.py:567
  26.3 12.3 %collective-permute-start.5 = (bf16[65,16,128]{2,1,0:T(8,128)(2,1)S(1)}, bf16[65,16,128]{2,1,0:T(8,128)(2,1)S(1)}, u32[]{:S(2)}, u32[]{:S(2)}) collective-permute-start(bf16[65,16,128]{2,1,0:T(8,128)(2,1)S(1)} %get-tuple-element.41), channel_id=1, source_target_pairs={{0,4},{8,12},{16,20},{24,28},{4,0},{12,8},{20,16},{28,24},{1,5},{9... | collective-permute-start | bytes 798728 | tf_op jit(solution)/shard_map/ppermute | solution.py:560
  28.8 9.8 %copy-start.1 = (bf16[8,3,128,128]{3,2,1,0:T(8,128)(2,1)S(1)}, bf16[8,3,128,128]{3,2,1,0:T(8,128)(2,1)}, u32[]{:S(2)}) copy-start(bf16[8,3,128,128]{3,2,1,0:T(8,128)(2,1)} %mid_tiles.7) | copy-start | bytes 2359300
  28.8 9.8 %copy-start.7 = (s32[1024]{0:T(1024)S(1)}, s32[1024]{0:T(1024)}, u32[]{:S(2)}) copy-start(s32[1024]{0:T(1024)} %param.14) | copy-start | bytes 12292
  28.8 4.7 %collective-permute-start.6 = (bf16[64,16,128]{2,1,0:T(8,128)(2,1)S(1)}, bf16[64,16,128]{2,1,0:T(8,128)(2,1)S(1)}, u32[]{:S(2)}, u32[]{:S(2)}) collective-permute-start(bf16[64,16,128]{2,1,0:T(8,128)(2,1)S(1)} %get-tuple-element.42.own), channel_id=1, source_target_pairs={{4,8},{12,16},{20,24},{8,4},{16,12},{24,20},{5,9},{13,17},{21,25},... | collective-permute-start | bytes 786440 | tf_op jit(solution)/shard_map/ppermute | solution.py:561
  29.6 3.2 %collective-permute-start.7 = (bf16[38,16,128]{2,1,0:T(8,128)(2,1)S(1)}, bf16[38,16,128]{2,1,0:T(8,128)(2,1)S(1)}, u32[]{:S(2)}, u32[]{:S(2)}) collective-permute-start(bf16[38,16,128]{2,1,0:T(8,128)(2,1)S(1)} %get-tuple-element.43.a), channel_id=1, source_target_pairs={{0,1},{1,0},{2,3},{3,2},{4,5},{5,4},{6,7},{7,6},{8,9},{9,8},{10,11... | collective-permute-start | bytes 466952 | tf_op jit(solution)/shard_map/ppermute | solution.py:567
  31.0 1.8 %collective-permute-start.9 = (bf16[38,16,128]{2,1,0:T(8,128)(2,1)S(1)}, bf16[38,16,128]{2,1,0:T(8,128)(2,1)S(1)}, u32[]{:S(2)}, u32[]{:S(2)}) collective-permute-start(bf16[38,16,128]{2,1,0:T(8,128)(2,1)S(1)} %collective-permute-done.8.c), channel_id=1, source_target_pairs={{0,1},{1,0},{2,3},{3,2},{4,5},{5,4},{6,7},{7,6},{8,9},{9,8},{10,11... | collective-permute-start | bytes 466952 | tf_op jit(solution)/shard_map/ppermute | solution.py:567
  38.6 17.5 %copy-start.2 = (f32[128,1024]{1,0:T(8,128)S(1)}, f32[128,1024]{1,0:T(8,128)}, u32[]{:S(2)}) copy-start(f32[128,1024]{1,0:T(8,128)} %inverse_rows.3) | copy-start | bytes 1572868
  57.3 7.5 %collective-permute-start.10 = (bf16[9,16,128]{2,1,0:T(8,128)(2,1)S(1)}, bf16[9,16,128]{2,1,0:T(8,128)(2,1)S(1)}, u32[]{:S(2)}, u32[]{:S(2)}) collective-permute-start(bf16[9,16,128]{2,1,0:T(8,128)(2,1)S(1)} %get-tuple-element.50), channel_id=1, source_target_pairs={{0,4},{8,12},{16,20},{24,28},{4,0},{12,8},{20,16},{28,24},{1,5},{9... | collective-permute-start | bytes 110600 | tf_op jit(solution)/shard_map/ppermute | solution.py:560
  57.5 7.3 %collective-permute-start.11 = (bf16[9,16,128]{2,1,0:T(8,128)(2,1)S(1)}, bf16[9,16,128]{2,1,0:T(8,128)(2,1)S(1)}, u32[]{:S(2)}, u32[]{:S(2)}) collective-permute-start(bf16[9,16,128]{2,1,0:T(8,128)(2,1)S(1)} %get-tuple-element.51), channel_id=1, source_target_pairs={{4,8},{12,16},{20,24},{8,4},{16,12},{24,20},{5,9},{13,17},{21,25},... | collective-permute-start | bytes 110600 | tf_op jit(solution)/shard_map/ppermute | solution.py:561
  58.2 6.6 %collective-permute-start.12 = (bf16[16,128]{1,0:T(8,128)(2,1)S(1)}, bf16[16,128]{1,0:T(8,128)(2,1)S(1)}, u32[]{:S(2)}, u32[]{:S(2)}) collective-permute-start(bf16[16,128]{1,0:T(8,128)(2,1)S(1)} %get-tuple-element.52), channel_id=1, source_target_pairs={{0,8},{4,12},{8,0},{12,4},{16,24},{20,28},{24,16},{28,20},{1,9},{5... | collective-permute-start | bytes 12296 | tf_op jit(solution)/shard_map/ppermute | solution.py:744
  62.9 2.0 %collective-permute-start.13 = (bf16[16,128]{1,0:T(8,128)(2,1)S(1)}, bf16[16,128]{1,0:T(8,128)(2,1)S(1)}, u32[]{:S(2)}, u32[]{:S(2)}) collective-permute-start(bf16[16,128]{1,0:T(8,128)(2,1)S(1)} %get-tuple-element.53), channel_id=1, source_target_pairs={{8,16},{12,20},{16,8},{20,12},{9,17},{13,21},{17,9},{21,13},{10,18... | collective-permute-start | bytes 12296 | tf_op jit(solution)/shard_map/ppermute | solution.py:745

commit v5 on v4

--- a/solution.py
+++ b/solution.py
@@ -15,7 +15,7 @@
 HBM = pl.BlockSpec(memory_space=pltpu.HBM)
 
 HI_AT, LO_AT, MISC_AT = 512, 576, 640
-MESSAGE = 704
+MESSAGE = 656
 FIRST_LIMIT = 52
 MID_LIMIT = 8
 
@@ -44,8 +44,8 @@
 
 
 def first_kernel(
-    place, res, tiles, mid_tiles, owner, mid_owner, inverse_rows, a_out, near_out, far_out, winv_out,
-    res_out, flat, held, message, owned, mid_owned, inverse_part, sems, side_sems,
+    place, res, tiles, mid_tiles, owner, inverse_rows, a_out, near_out, far_out, winv_out,
+    res_out, flat, held, picked, inverse_part, sems, side_sems,
 ):
     blocks, ext = held.shape[0], held.shape[1]
     width = a_out.shape[1]
@@ -59,52 +59,63 @@
     whole = pltpu.make_async_copy(res, flat, sems.at[parts])
     mids = mid_tiles.shape[0]
     last = mids - 1
-    picks = (
-        [(last, 1), (last, 2), (last - 1, 2), (0, 0)],
-        [(0, 1), (0, 0), (1, 0), (last, 2)],
-    )
+    column = place[2]
+    odd = place[0] % 2
+    choose = lambda *values: jnp.where(
+        column < 2,
+        jnp.where(column == 0, values[0], values[1]),
+        jnp.where(column == 2, values[2], values[3]),
+    )
+    up = choose(last, last, last - 1, 0), choose(1, 2, 2, 0)
+    down = choose(0, 0, 1, last), choose(1, 0, 0, 2)
+    tiles_at = [
+        [jnp.where(odd == side, one, two) for one, two in zip(up, down)] for side in range(2)
+    ] + [(0, 1), (last, 1)]
     share = inverse_part.shape[0]
-    begin = pl.multiple_of(place[2] * share, share)
+    begin = pl.multiple_of(column * share, share)
     smalls = [
-        pltpu.make_async_copy(owner, owned, side_sems.at[0]),
-        pltpu.make_async_copy(mid_owner, mid_owned, side_sems.at[1]),
-        pltpu.make_async_copy(inverse_rows.at[pl.ds(begin, share)], inverse_part, side_sems.at[2]),
+        pltpu.make_async_copy(inverse_rows.at[pl.ds(begin, share)], inverse_part, side_sems.at[4])
+    ] + [
+        pltpu.make_async_copy(mid_tiles.at[b, k], picked.at[n], side_sems.at[n])
+        for n, (b, k) in enumerate(tiles_at)
     ]
-    for side in range(2):
-        for n, (b, k) in enumerate(picks[side]):
-            smalls.append(
-                pltpu.make_async_copy(
-                    mid_tiles.at[b, k],
-                    message.at[side, pl.ds(n * ext, ext)],
-                    side_sems.at[3 + 4 * side + n],
-                )
-            )
     whole.start()
     for part in range(parts):
         copy(part).start()
     for small in smalls:
         small.start()
     eye = eye_mask(ext)
+    quarter = blocks // 4
+    rows = pl.ds(pl.multiple_of(column * quarter, quarter), quarter)
+    lo, hi = split(owner[rows] - place[0] * (mids * ext), ext)
+    mid_block, mid_hi = split(owner[blocks:], ext)
     for small in smalls:
         small.wait()
-    lo, hi = split(owned[...] - place[0] * (mids * ext), ext)
-    mid_block, mid_hi = split(mid_owned[...], ext)
-    for side, first in enumerate((last - 1, 0)):
-        message[side, HI_AT : HI_AT + blocks] = hi.astype(F32).astype(BF16)
-        message[side, LO_AT : LO_AT + blocks] = lo.astype(F32).astype(BF16)
-        rows = [
-            mid_hi[first : first + 2].astype(F32),
-            mid_block[first : first + 2].astype(F32),
-            diag_row(message[1 - side, 0:ext], eye),
-            jnp.zeros((MESSAGE - MISC_AT - 5, ext), F32),
-        ]
-        message[side, MISC_AT:MESSAGE] = jnp.concatenate(rows, axis=0).astype(BF16)
     extra = far_out.shape[0] - blocks
-    odd = place[0] % 2
-    for n in range(extra):
-        part = pl.ds(pl.multiple_of((place[2] * extra + n) * width, width), width)
-        near_out[blocks + n] = message[odd, part]
-        far_out[blocks + n] = message[1 - odd, part]
+    singles = [
+        jnp.concatenate(
+            [
+                mid_hi[first : first + 2].astype(F32),
+                mid_block[first : first + 2].astype(F32),
+                diag_row(picked[2 + side], eye),
+                jnp.zeros((width - 5, ext), F32),
+            ],
+            axis=0,
+        )
+        for side, first in enumerate((last - 1, 0))
+    ]
+    tile_blocks = ext // width
+    for n, (to, single) in enumerate(
+        (
+            (near_out, jnp.where(odd == 0, singles[0], singles[1])),
+            (far_out, jnp.where(odd == 0, singles[1], singles[0])),
+        )
+    ):
+        for k in range(tile_blocks):
+            to[blocks + k] = picked[n, k * width : (k + 1) * width]
+        to[blocks + tile_blocks] = hi.astype(F32).astype(BF16)
+        to[blocks + tile_blocks + 1] = lo.astype(F32).astype(BF16)
+        to[blocks + tile_blocks + 2] = single.astype(BF16)
     tall, wide = share // width, inverse_part.shape[1] // ext
     for i in range(tall):
         for k in range(wide):
@@ -129,7 +140,7 @@
 
 def plan_kernel(place, index, after, owner, hot_out, plan):
     del after
-    blocks, ext = owner.shape
+    blocks, ext = index.shape[1], owner.shape[1]
     first = place[0] * blocks
     zero = 3 * blocks
 
@@ -151,8 +162,8 @@
         plan[4, g] = 0
         return jnp.maximum(most, count)
 
-    plan[4, 0] = lax.fori_loop(0, blocks, row, 0)
-    _, hi = split(owner[...], ext)
+    plan[4, 0] = lax.fori_loop(0, blocks, row, 0, unroll=8)
+    _, hi = split(owner[0:blocks], ext)
     for g in range(blocks):
         hot_out[:, g * ext : (g + 1) * ext] = one_hot(hi[g : g + 1, :], ext)
 
@@ -210,23 +221,51 @@
 
 
 def sides_kernel(
-    place, a, b, c, d, left_out, right_out, inverse_out, buffer
+    place, a, b, c, d, mid_tiles, owner, left_out, right_out, inverse_out, scale_out, mid_hot,
+    mid_block, buffer,
 ):
     width, ext = a.shape[1:]
-    extra = left_out.shape[0] // (4 * width)
+    tile_blocks = ext // width
+    extra = tile_blocks + 3
     for n, piece in enumerate((a, b, c, d)):
         buffer[place[2] ^ n] = piece[...]
     share = inverse_out.shape[0] // 4
     wide = inverse_out.shape[1] // ext
+    for out, first in ((left_out, 0), (right_out, extra)):
+        for n in range(4):
+            for k in range(tile_blocks):
+                at = n * ext + k * width
+                out[at : at + width] = buffer[n, first + k]
+            out[HI_AT + n * width : HI_AT + (n + 1) * width] = buffer[n, first + tile_blocks]
+            out[LO_AT + n * width : LO_AT + (n + 1) * width] = buffer[n, first + tile_blocks + 1]
+        out[MISC_AT:MESSAGE] = buffer[0, first + tile_blocks + 2]
     for n in range(4):
-        for k in range(extra):
-            rows = slice((n * extra + k) * width, (n * extra + k + 1) * width)
-            left_out[rows] = buffer[n, k]
-            right_out[rows] = buffer[n, extra + k]
         for i in range(share // width):
             rows = slice(n * share + i * width, n * share + (i + 1) * width)
             for k in range(wide):
                 inverse_out[rows, k * ext : (k + 1) * ext] = buffer[n, 2 * extra + i * wide + k]
+    mids = mid_tiles.shape[0]
+    eye = eye_mask(ext)
+    has_left, has_right = place[0] > 0, place[0] < place[1] - 1
+    left_single, right_single = (m[MISC_AT:MESSAGE].astype(F32) for m in (left_out, right_out))
+    scales = [DAMPING * (1.0 / diag_row(mid_tiles[b, 1], eye)) for b in range(mids)] + [
+        inverse(diag_row(left_out[0:ext], eye), has_left),
+        inverse(diag_row(right_out[0:ext], eye), has_right),
+        inverse(left_single[4:5], has_left),
+        inverse(right_single[4:5], has_right),
+    ]
+    scale_out[...] = jnp.concatenate(
+        scales + [jnp.zeros((scale_out.shape[0] - len(scales), ext), F32)], axis=0
+    )
+    blocks = owner.shape[0] - mids
+    own_block, own_hi = split(owner[blocks:], ext)
+    block = [left_single[2:4].astype(jnp.int32), own_block, right_single[2:4].astype(jnp.int32)]
+    hi = [left_single[0:2].astype(jnp.int32), own_hi, right_single[0:2].astype(jnp.int32)]
+    hi = jnp.concatenate(hi, axis=0)
+    start = place[0] - 2 + place[0] % 2
+    mid_block[0 : mids + 4] = jnp.concatenate(block, axis=0) - start
+    for b in range(mids + 4):
+        mid_hot[:, b * ext : (b + 1) * ext] = one_hot(hi[b : b + 1], ext)
 
 
 def side_hot_kernel(after, from_left, from_right, hot_left, hot_right):
@@ -309,12 +348,6 @@
     return DAMPING * (1.0 / jnp.where(present, row, 1.0))
 
 
-def mid_inverse(mid_tiles, eye):
-    return [
-        DAMPING * (1.0 / diag_row(mid_tiles[b, 1], eye)) for b in range(mid_tiles.shape[0])
-    ]
-
-
 def mid_product(mid_tiles, v, b):
     ext = mid_tiles.shape[2]
     count = mid_tiles.shape[0]
@@ -326,14 +359,13 @@
 
 
 def third_kernel(
-    index, plan, place, tiles, near, own, far, part, res, owner, hot, mid_tiles, mid_owner, from_left,
-    from_right, fres_out, u_out, bpart_out, send, window, spread_rows,
+    index, plan, place, tiles, near, own, far, part, res, owner, hot, mid_tiles, from_left,
+    from_right, scale, mid_hot, mid_block, fres_out, u_out, bpart_out, send, window, spread_rows,
 ):
     blocks, ext = own.shape[0], own.shape[2]
     width = own.shape[1]
     mids = mid_tiles.shape[0]
     me = place[0]
-    peers = place[1]
     offset = (me - 1) * blocks
     fill_window(window, near, own, far, place[0])
 
@@ -348,13 +380,10 @@
     quarters = [slice(n * blocks // 4 * ext, (n + 1) * blocks // 4 * ext) for n in range(4)]
     total = sum(dot_nt(spread_rows[:, q], hot[:, q]) for q in quarters)
     u = [total[b * width : (b + 1) * width] for b in range(mids)]
-    eye = eye_mask(ext)
-    winv = mid_inverse(mid_tiles, eye)
-    has_left, has_right = me > 0, me < peers - 1
+    winv = [scale[b : b + 1, :] for b in range(mids)]
+    winv_left, winv_right = scale[mids : mids + 1, :], scale[mids + 1 : mids + 2, :]
     left_mid, left_next, left_far = (edge(from_left, 128 * k) for k in range(3))
     right_mid, right_prev, right_far = (edge(from_right, 128 * k) for k in range(3))
-    winv_left = inverse(diag_row(left_mid, eye), has_left)
-    winv_right = inverse(diag_row(right_mid, eye), has_right)
     a = [winv[b] * u[b] for b in range(mids)]
     a16 = {b: a[b].astype(BF16) for b in range(mids)}
     mine = {}
@@ -370,21 +399,10 @@
     rest[-2] = -dot_nt(p16[-1], left_far)
     rest[mids] = -(dot_nt(p16[mids], right_mid) + dot_nt(p16[mids - 1], right_prev))
     rest[mids + 1] = -dot_nt(p16[mids], right_far)
-    start = me - 2 + me % 2
-    order = list(range(-2, mids + 2))
-    spreads, hots = [], []
-    for b in order:
-        if b < 0:
-            at = MISC_AT + 2 + b
-            hi, block = as_int(from_left[at : at + 1, :]), as_int(from_left[at + 2 : at + 3, :])
-        elif b >= mids:
-            at = MISC_AT + b - mids
-            hi, block = as_int(from_right[at : at + 1, :]), as_int(from_right[at + 2 : at + 3, :])
-        else:
-            block, hi = split(mid_owner[b : b + 1, :], ext)
-        spreads.append(spread(rest[b], block - start, 4))
-        hots.append(one_hot(hi, ext))
-    coarse = dot_nt(jnp.concatenate(spreads, axis=1), jnp.concatenate(hots, axis=1))
+    spreads = [
+        spread(rest[b], mid_block[b + 2 : b + 3, :], 4) for b in range(-2, mids + 2)
+    ]
+    coarse = dot_nt(jnp.concatenate(spreads, axis=1), mid_hot[...])
     coarse16 = coarse.astype(BF16)
     first, last = u[0].astype(BF16), u[mids - 1].astype(BF16)
     none = jnp.zeros_like(first)
@@ -395,7 +413,7 @@
 
 
 def mid_kernel(
-    place, got, inverse_rows, partner_rows, mid_tiles, mid_owner, u, bpart, from_left, from_right,
+    place, got, inverse_rows, partner_rows, mid_tiles, scale, mid_hot, mid_block, u, bpart,
     dpart_out, edges_out, near_out, far_out, next_out, beyond_out,
 ):
     ext = mid_tiles.shape[2]
@@ -418,10 +436,8 @@
     pair = jnp.concatenate(
         [jnp.where(odd == 0, mine, other), jnp.where(odd == 0, other, mine)], axis=0
     ).astype(BF16)
-    eye = eye_mask(ext)
-    winv = mid_inverse(mid_tiles, eye)
-    winv_left = inverse(diag_row(edge(from_left, 0), eye), me > 0)
-    winv_right = inverse(diag_row(edge(from_right, 0), eye), me < peers - 1)
+    winv = [scale[b : b + 1, :] for b in range(mids)]
+    winv_left, winv_right = scale[mids : mids + 1, :], scale[mids + 1 : mids + 2, :]
     before = got[lax.rem(me + peers - 1, peers), 4].astype(F32)
     after = got[lax.rem(me + 1, peers), 4].astype(F32)
     a_before = (winv_left * before).astype(BF16)
@@ -433,9 +449,10 @@
             value = value - winv[b] * dot_nt(a_before, mid_tiles[b, 0])
         if b == mids - 1:
             value = value - winv[b] * dot_nt(a_after, mid_tiles[b, 2])
-        block, hi = split(mid_owner[b : b + 1, :], ext)
-        both = jnp.dot(pair, one_hot(hi, ext), preferred_element_type=F32)
-        c[b] = value + jnp.where(block - (me - odd) == 0, both[:width], both[width:])
+        hot = mid_hot[:, (b + 2) * ext : (b + 3) * ext]
+        both = jnp.dot(pair, hot, preferred_element_type=F32)
+        second = mid_block[b + 2 : b + 3, :] == 3 - 2 * odd
+        c[b] = value + jnp.where(second, both[width:], both[:width])
         c16[b] = c[b].astype(BF16)
     d16 = []
     for b in range(mids):
@@ -464,7 +481,7 @@
 
 
 def last_kernel(
-    index, place, tiles, near, far, nexts, beyond, dpart, c_edges, mid_tiles, owner, hot_own, from_left, hot_left,
+    index, place, tiles, near, far, other, nexts, beyond, dpart, c_edges, mid_tiles, scale, owner, hot_own, from_left, hot_left,
     from_right, hot_right, b_in, fres, winv, basis_a, basis_b, basis_c, basis_d, out, gram_out, window,
     added, rounded, grams, result, sems,
 ):
@@ -473,34 +490,31 @@
     me, peers = place[0], place[1]
     odd = me % 2
     low = me % 4 < 2
-    eye = eye_mask(ext)
-    has_left, has_right = me > 0, me < peers - 1
-    left = [jnp.where(odd == 1, near[b], far[b]) for b in range(mids + 1)]
-    right = [jnp.where(odd == 1, far[b], near[b]) for b in range(mids + 1)]
-    far_left = jnp.where(low, beyond[...], nexts[...])
-    far_right = jnp.where(low, nexts[...], beyond[...])
-    minv = lambda b: DAMPING * (1.0 / diag_row(mid_tiles[b, 1], eye))
+    middle = jnp.logical_or(me % 4 == 1, me % 4 == 2)
+    present = jnp.logical_and(me > 0, me < peers - 1)
+    none = jnp.zeros_like(nexts[...])
+    away = [
+        jnp.where(middle, other[b], jnp.where(present, far[b], none)) for b in range(mids + 1)
+    ]
+    left = [jnp.where(odd == 1, near[b], away[b]) for b in range(mids + 1)]
+    right = [jnp.where(odd == 1, away[b], near[b]) for b in range(mids + 1)]
+    outer = jnp.where(jnp.logical_and(me > 1, me < peers - 2), beyond[...], none)
+    far_left = jnp.where(low, outer, nexts[...])
+    far_right = jnp.where(low, nexts[...], outer)
+    row = lambda n: scale[n : n + 1, :]
     own = [dpart[b] for b in range(mids)]
-    own[0] = own[0] - minv(0) * dot_nt(left[mids], mid_tiles[0, 0])
-    own[-1] = own[-1] - minv(mids - 1) * dot_nt(right[mids], mid_tiles[mids - 1, 2])
+    own[0] = own[0] - row(0) * dot_nt(left[mids], mid_tiles[0, 0])
+    own[-1] = own[-1] - row(mids - 1) * dot_nt(right[mids], mid_tiles[mids - 1, 2])
     lefts = [v.astype(F32) for v in left[:mids]]
-    lefts[0] = lefts[0] - inverse(
-        from_left[MISC_AT + 4 : MISC_AT + 5, :].astype(F32), has_left
-    ) * dot_nt(far_left, edge(from_left, 384))
-    lefts[-1] = lefts[-1] - inverse(diag_row(edge(from_left, 0), eye), has_left) * dot_nt(
-        c_edges[0], edge(from_left, 128)
-    )
+    lefts[0] = lefts[0] - row(mids + 2) * dot_nt(far_left, edge(from_left, 384))
+    lefts[-1] = lefts[-1] - row(mids) * dot_nt(c_edges[0], edge(from_left, 128))
     rights = [v.astype(F32) for v in right[:mids]]
-    rights[0] = rights[0] - inverse(diag_row(edge(from_right, 0), eye), has_right) * dot_nt(
-        c_edges[1], edge(from_right, 128)
-    )
-    rights[-1] = rights[-1] - inverse(
-        from_right[MISC_AT + 4 : MISC_AT + 5, :].astype(F32), has_right
-    ) * dot_nt(far_right, edge(from_right, 384))
+    rights[0] = rights[0] - row(mids + 1) * dot_nt(c_edges[1], edge(from_right, 128))
+    rights[-1] = rights[-1] - row(mids + 3) * dot_nt(far_right, edge(from_right, 384))
     own16, left16, right16 = (
         jnp.concatenate([v.astype(BF16) for v in side], axis=0) for side in (own, lefts, rights)
     )
-    own_lo, _ = split(owner[...] - me * (mids * ext), ext)
+    own_lo, _ = split(owner[0:blocks] - me * (mids * ext), ext)
     left_lo, right_lo = (
         as_int(message[LO_AT : LO_AT + blocks, :]) for message in (from_left, from_right)
     )
@@ -536,9 +550,8 @@
             copy((g + 1) // per - 1).start()
     for n, piece in enumerate((basis_a, basis_b, basis_c, basis_d)):
         grams[place[2] ^ n] = dot_nt(rounded[...], piece[...])
-    gram = jnp.concatenate(
-        [grams[n] for n in range(4)] + [jnp.zeros((width, ext - 4 * width), F32)], axis=1
-    )
+    gram = jnp.concatenate([grams[n] for n in range(4)], axis=1)
+    gram = jnp.concatenate([gram[: width // 2], gram[width // 2 :]], axis=1)
     for d in range(gram_out.shape[0]):
         gram_out[d] = gram
     for part in range(count):
@@ -549,7 +562,9 @@
     total = got[0]
     for s in range(1, got.shape[0]):
         total = total + got[s]
-    out[...] = total[:, : out.shape[1]]
+    half, wide = out.shape[0] // 2, out.shape[1]
+    out[0:half] = total[:, :wide]
+    out[half:] = total[:, wide:]
 
 
 def halo(for_partner, for_other):
@@ -581,12 +596,11 @@
     res = residual_block.T
     index = fine_index.T
     place = jnp.stack([me, jnp.int32(peers), lax.axis_index("cols")])
-    owner = fine_owner.reshape(blocks, ext)
-    mid_rows = mid_owner.reshape(mids, ext)
+    owner = jnp.concatenate([fine_owner, mid_owner]).reshape(blocks + mids, ext)
     shape = jax.ShapeDtypeStruct
     tile_bytes = fine_tiles.size * 2
     fine_flops = 2 * fine_tiles.size * width
-    extra = MESSAGE // (lax.axis_size("cols") * width)
+    extra = ext // width + 3
 
     columns = lax.axis_size("cols")
     share = coarse_inverse.shape[0] // columns
@@ -595,7 +609,7 @@
 
     a16, for_partner, for_other, winv, res_blocks = pl.pallas_call(
         first_kernel,
-        in_specs=[SM] + [HBM] * 6,
+        in_specs=[SM] + [HBM] * 3 + [VM, HBM],
         out_specs=[VM] * 5,
         out_shape=[
             shape((blocks, width, ext), BF16),
@@ -607,16 +621,14 @@
         scratch_shapes=[
             pltpu.VMEM((width, count), F32),
             pltpu.VMEM((blocks, ext, ext), BF16),
-            pltpu.VMEM((2, MESSAGE, ext), BF16),
-            pltpu.VMEM((blocks, ext), jnp.int32),
-            pltpu.VMEM((mids, ext), jnp.int32),
+            pltpu.VMEM((4, ext, ext), BF16),
             pltpu.VMEM((share, whole_row), F32),
             pltpu.SemaphoreType.DMA((5,)),
-            pltpu.SemaphoreType.DMA((11,)),
+            pltpu.SemaphoreType.DMA((5,)),
         ],
         name="first_smoothing",
         **params(FIRST_LIMIT, count * ext, tile_bytes // 4),
-    )(place, res, fine_tiles, mid_tiles, owner, mid_rows, coarse_inverse)
+    )(place, res, fine_tiles, mid_tiles, owner, coarse_inverse)
 
     near, far = halo(for_partner, for_other)
     hot_own, plan = pl.pallas_call(
@@ -668,23 +680,26 @@
         name="own_part_of_residual",
         **params(4, ext, ext),
     )(index, place, tiles, b16)
-    from_left, from_right, partner_rows = pl.pallas_call(
+    from_left, from_right, partner_rows, scale, mid_hot, mid_block = pl.pallas_call(
         sides_kernel,
-        in_specs=[SM] + [VM] * 4,
-        out_specs=[VM] * 3,
+        in_specs=[SM] + [VM] * 6,
+        out_specs=[VM] * 6,
         out_shape=[
             shape((MESSAGE, ext), BF16),
             shape((MESSAGE, ext), BF16),
             shape(coarse_inverse.shape, BF16),
+            shape((16, ext), F32),
+            shape((ext, (mids + 4) * ext), BF16),
+            shape((16, ext), jnp.int32),
         ],
         scratch_shapes=[pltpu.VMEM((4, 2 * extra + quarter, width, ext), BF16)],
         name="side_messages",
         **params(4, ext, ext),
-    )(place, mine, *from_columns(mine))
+    )(place, mine, *from_columns(mine), mid_tiles, owner)
 
     fres, u, bpart, send = pl.pallas_call(
         third_kernel,
-        in_specs=[SM] * 3 + [VM] * 12,
+        in_specs=[SM] * 3 + [VM] * 14,
         out_specs=[VM] * 4,
         out_shape=[
             shape((blocks, width, ext), F32),
@@ -700,7 +715,7 @@
         **params(10, fine_flops, tile_bytes),
     )(
         index, plan, place, tiles, near, b16, far, part, res_blocks, owner, hot_own, mid_tiles,
-        mid_rows, from_left, from_right,
+        from_left, from_right, scale, mid_hot, mid_block,
     )
 
     got = lax.all_to_all(send, "rows", 0, 0)
@@ -719,18 +734,17 @@
         name="coarse_and_mid_level",
         **params(MID_LIMIT, 4 * width * coarse_inverse.size, coarse_inverse.size * 4),
     )(
-        place, got, coarse_inverse, partner_rows, mid_tiles, mid_rows, u, bpart, from_left,
-        from_right,
+        place, got, coarse_inverse, partner_rows, mid_tiles, scale, mid_hot, mid_block, u, bpart,
     )
 
     return finish(
-        place, index, tiles, sends, dpart, c_edges, mid_tiles, owner, hot_own, from_left, from_right,
+        place, index, tiles, sends, dpart, c_edges, mid_tiles, scale, owner, hot_own, from_left, from_right,
         b32, fres, winv, basis_pieces,
     )
 
 
 def finish(
-    place, index, tiles, sends, dpart, c_edges, mid_tiles, owner, hot_own, from_left, from_right, b32,
+    place, index, tiles, sends, dpart, c_edges, mid_tiles, scale, owner, hot_own, from_left, from_right, b32,
     fres, winv, basis_pieces,
 ):
     peers = lax.axis_size("rows")
@@ -738,11 +752,15 @@
     mids = mid_tiles.shape[0]
     count = blocks * ext
     shape = jax.ShapeDtypeStruct
-    near, far = halo(*sends[:2])
-    pairs = [(i, i + 2) for i in range(peers - 2) if i % 4 >= 2]
-    pairs += [(j, i) for i, j in pairs]
-    nexts = lax.ppermute(sends[2], "rows", [(i, i ^ 2) for i in range(peers)])
-    beyond = lax.ppermute(sends[3], "rows", pairs)
+    swap = lambda v, pairs: lax.ppermute(v, "rows", pairs + [(j, i) for i, j in pairs])
+    flip = lambda v, n: lax.ppermute(v, "rows", [(i, i ^ n) for i in range(peers)])
+    ends = [(0, 1), (peers - 2, peers - 1)] if peers > 4 else [(0, 1), (2, 3)]
+    inner = range(2, peers - 4, 4)
+    far = swap(sends[1], [(i + 1, i + 2) for i in inner] + [(i, i + 3) for i in inner] + ends)
+    beyond = swap(sends[3], [(i + n, i + 2 + n) for i in inner for n in range(2)] + ends)
+    near = flip(sends[0], 1)
+    other = flip(sends[1], 3)
+    nexts = flip(sends[2], 2)
     hot_left, hot_right = pl.pallas_call(
         side_hot_kernel,
         in_specs=[ANY, VM, VM],
@@ -753,11 +771,11 @@
     )(c_edges, from_left, from_right)
     out, grams = pl.pallas_call(
         last_kernel,
-        in_specs=[SM, SM] + [VM] * 21,
+        in_specs=[SM, SM] + [VM] * 23,
         out_specs=[HBM, VM],
         out_shape=[
             shape((width, count), F32),
-            shape((peers, width, ext), F32),
+            shape((peers, width // 2, 8 * width), F32),
         ],
         scratch_shapes=[
             pltpu.VMEM((3 * blocks, width, ext), BF16),
@@ -770,7 +788,7 @@
         name="prolongation_and_last_smoothing",
         **params(8, 2 * tiles.size * width, tiles.size * 2),
     )(
-        index, place, tiles, near, far, nexts, beyond, dpart, c_edges, mid_tiles, owner, hot_own, from_left, hot_left,
+        index, place, tiles, near, far, other, nexts, beyond, dpart, c_edges, mid_tiles, scale, owner, hot_own, from_left, hot_left,
         from_right, hot_right, b32, fres, winv, *basis_pieces,
     )
     gram = pl.pallas_call(

time: 82.5 us -> 80.9 us (0.981)
  waiting for transfers between devices: 13.8 us -> 15.7 us
  starting transfers between devices: 16.1 us -> 14.3 us
  local copies, waits for them, and re-layouts: 1.47 us -> 0.02 us
  blocking collectives: 25.4 us -> 24.5 us
    ppermute x2 -> x5, waiting for transfers between devices: 0.01 us -> 1.68 us  [the longest x2 1 us: finish(): lax.ppermute(v, 'rows', pairs + [(j, i) for i, j in pairs])]
    unnamed x16 -> x10, local copies, waits for them, and re-layouts: 1.47 us -> 0.02 us
    all_to_all x1, blocking collectives: 12.2 us -> 11.3 us  [finish(): lax.all_to_all(grams, 'rows', 0, 0)]
    ppermute x2 -> x5, starting transfers between devices: 5.51 us -> 4.66 us  [the longest x3 2.39 us: finish(): lax.ppermute(v, 'rows', [(i, i ^ n) for i in range(peers)])]
    ppermute x3 -> x2, starting transfers between devices: 2.12 us -> 1.47 us  [halo(): far = lax.ppermute(for_other, 'rows', swap(odd))]
    ppermute x3 -> x2, starting transfers between devices: 4.25 us -> 4.07 us  [halo(): near = lax.ppermute(for_partner, 'rows', swap(even))]
    ppermute x3 -> x2, waiting for transfers between devices: 12.4 us -> 12.5 us  [halo(): near = lax.ppermute(for_partner, 'rows', swap(even))]
  transfers between devices with their start and end apart: 14 -> 15, of which waited for: 3 -> 6; matrix products, arithmetic and copies ran while one was open for 0% -> 1% of each run, Pallas kernels for 15% -> 15%
where the time goes in v5:
time: 80.9 us; the launch traced here: 80.6 us
  Pallas kernels  24.6 us (30%)
  blocking collectives  24.5 us (30%)
  waiting for transfers between devices  15.7 us (19%)
  starting transfers between devices  14.3 us (18%)
  other arithmetic  0.85 us (1%)
    all_to_all x1, blocking collectives, on_device(): got = lax.all_to_all(send, 'rows', 0, 0)  13.2 us
    ppermute x2, waiting for transfers between devices, halo(): near = lax.ppermute(for_partner, 'rows', swap(even))  12.5 us
    all_to_all x1, blocking collectives, finish(): lax.all_to_all(grams, 'rows', 0, 0)  11.3 us
    pallas_call x1, Pallas kernels, finish(): pl.pallas_call(last_kernel, in_specs=[SM, SM] + [VM] * 23, out_specs=[HBM...  4.71 us
    pallas_call x1, Pallas kernels, on_device(): pl.pallas_call(third_kernel, in_specs=[SM] * 3 + [VM] * 14, out_specs=[VM...  4.24 us
    ppermute x2, starting transfers between devices, halo(): near = lax.ppermute(for_partner, 'rows', swap(even))  4.07 us
    ppermute x6, starting transfers between devices, from_columns(): lax.ppermute(v, 'cols', [(i, i ^ n) for i in range(peers)])  4.06 us
    pallas_call x1, Pallas kernels, on_device(): pl.pallas_call(first_kernel, in_specs=[SM] + [HBM] * 3 + [VM, HBM], out_s...  3.11 us
  transfers between devices with their start and end apart: 15, of which 6 were waited for; matrix products, arithmetic and copies ran while one was open for 1% of the time, Pallas kernels for 15%

profile of v5, /device:TPU:0, one launch (start us, length us, event | category | flops | bytes accessed | tf_op | source)
XLA Modules:
  0.0 80.6 jit_solution(5723418707914918681)
XLA Ops:
  0.6 3.0 %collective-permute-start.3 = (bf16[16,8192]{1,0:T(8,128)(2,1)}, bf16[16,8192]{1,0:T(8,128)(2,1)S(1)}, u32[]{:S(2)}, u32[]{:S(2)}) collective-permute-start(bf16[16,8192]{1,0:T(8,128)(2,1)} %bitcast.9), channel_id=1, source_target_pairs={{0,2},{1,3},{2,0},{3,1},{4,6},{5,7},{6,4},{7,5},{8,10},{9,11},{10,... | collective-permute-start | bytes 786440 | tf_op jit(solution)/shard_map/ppermute | solution.py:582
  3.6 0.1 pad_add_fusion.place
  3.7 0.8 add_bitcast_fusion.owner
  4.5 3.1 %first_smoothing.1 = (bf16[64,16,128]{2,1,0:T(8,128)(2,1)S(1)}, bf16[91,16,128]{2,1,0:T(8,128)(2,1)S(1)}, bf16[75,16,128]{2,1,0:T(8,128)(2,1)S(1)}, f32[64,128]{1,0:T(8,128)S(1)}, f32[64,16,128]{2,1,0:T(8,128)S(1)}) custom-call(s32[3]{0:T(128)S(1)} %pad_add_fusion.place, f32[16,8192]{1,0:T(8,128)} %bitcast.18, bf16[64,4,128,128]{3,2,1,0:T(8,128)(2,1)} %tiles.3, ...), custom_call_target="tpu_custom_call" | custom-call | flops 1048576 | bytes 2097152 | tf_op jit(solution)/shard_map/first_smoothing/pallas_call | solution.py:610
  7.6 1.6 %collective-permute-start = (bf16[91,16,128]{2,1,0:T(8,128)(2,1)S(1)}, bf16[91,16,128]{2,1,0:T(8,128)(2,1)S(1)}, u32[]{:S(2)}, u32[]{:S(2)}) collective-permute-start(bf16[91,16,128]{2,1,0:T(8,128)(2,1)S(1)} %get-tuple-element.39), channel_id=1, source_target_pairs={{0,4},{8,12},{16,20},{24,28},{4,0},{12,8},{20,16},{28,24},{1,5},{9... | collective-permute-start | bytes 1118216 | tf_op jit(solution)/shard_map/ppermute | solution.py:575
  9.2 0.7 collective-permute-start.1
  9.9 0.0 copy-done.3
  9.9 0.1 collective-permute-start.2
  10.0 0.2 collective-permute-done.3.basis_c
  10.2 0.3 collective-permute-start.4
  10.5 0.0 copy-done
  10.5 0.0 copy-done.4
  10.5 2.9 %own_part_and_turned_tiles.1 = (f32[64,16,128]{2,1,0:T(8,128)S(1)}, bf16[64,4,128,128]{3,2,1,0:T(8,128)(2,1)S(1)}) custom-call(s32[4,64]{1,0:T(4,128)S(1)} %bitcast.12, s32[3]{0:T(128)S(1)} %pad_add_fusion.place, bf16[64,4,128,128]{3,2,1,0:T(8,128)(2,1)S(1)} %copy-done, bf16[64,16,128]{2,1,0:T(8,128)(2,1)S(1)} %get-tuple-element.35.own), custom_call_target="tpu_custom_call" | custom-call | flops 128 | bytes 128 | tf_op jit(solution)/shard_map/own_part_and_turned_tiles/pallas_call | solution.py:644
  13.4 2.5 %one_hot_rows.1 = (bf16[128,8192]{1,0:T(8,128)(2,1)S(1)}, s32[5,64]{1,0:T(8,128)S(1)}) custom-call(s32[3]{0:T(128)S(1)} %pad_add_fusion.place, s32[4,64]{1,0:T(4,128)S(1)} %bitcast.13, f32[64,128]{1,0:T(8,128)S(1)} %get-tuple-element.37.after.winv, s32[72,128]{1,0:T(8,128)S(1)} %add_bitcast_fusion.owner), custom_call_target="tpu_custom_call" | custom-call | flops 1048576 | bytes 33554432 | tf_op jit(solution)/shard_map/one_hot_rows/pallas_call | solution.py:634
  15.9 0.0 collective-permute-done.2.basis_b
  15.9 0.0 collective-permute-done.1.far
  15.9 7.6 %collective-permute-done.near = bf16[91,16,128]{2,1,0:T(8,128)(2,1)S(1)} collective-permute-done((bf16[91,16,128]{2,1,0:T(8,128)(2,1)S(1)}, bf16[91,16,128]{2,1,0:T(8,128)(2,1)S(1)}, u32[]{:S(2)}, u32[]{:S(2)}) %collective-permute-start) | collective-permute-done | bytes 372768 | tf_op jit(solution)/shard_map/ppermute | solution.py:575
  23.4 0.0 collective-permute-done.4.basis_d
  23.4 1.5 %second_smoothing.1 = (f32[64,16,128]{2,1,0:T(8,128)S(1)}, bf16[64,16,128]{2,1,0:T(8,128)(2,1)S(1)}, bf16[65,16,128]{2,1,0:T(8,128)(2,1)S(1)}, bf16[38,16,128]{2,1,0:T(8,128)(2,1)S(1)}) custom-call(s32[4,64]{1,0:T(4,128)S(1)} %bitcast.14, s32[5,64]{1,0:T(8,128)S(1)} %get-tuple-element.38.plan, s32[3]{0:T(128)S(1)} %pad_add_fusion.place, ...), custom_call_target="tpu_custom_call" | custom-call | flops 134217728 | bytes 8388608 | tf_op jit(solution)/shard_map/second_smoothing/pallas_call | solution.py:655
  24.9 0.6 collective-permute-start.8
  25.5 2.5 %collective-permute-start.5 = (bf16[65,16,128]{2,1,0:T(8,128)(2,1)S(1)}, bf16[65,16,128]{2,1,0:T(8,128)(2,1)S(1)}, u32[]{:S(2)}, u32[]{:S(2)}) collective-permute-start(bf16[65,16,128]{2,1,0:T(8,128)(2,1)S(1)} %get-tuple-element.44), channel_id=1, source_target_pairs={{0,4},{8,12},{16,20},{24,28},{4,0},{12,8},{20,16},{28,24},{1,5},{9... | collective-permute-start | bytes 798728 | tf_op jit(solution)/shard_map/ppermute | solution.py:575
  28.0 0.8 collective-permute-start.6
  28.8 0.1 collective-permute-start.7
  28.9 1.3 %collective-permute-done.8.c = bf16[38,16,128]{2,1,0:T(8,128)(2,1)S(1)} collective-permute-done((bf16[38,16,128]{2,1,0:T(8,128)(2,1)S(1)}, bf16[38,16,128]{2,1,0:T(8,128)(2,1)S(1)}, u32[]{:S(2)}, u32[]{:S(2)}) %collective-permute-start.8) | collective-permute-done | bytes 155680 | tf_op jit(solution)/shard_map/ppermute | solution.py:582
  30.2 0.0 collective-permute-start.9
  30.2 1.8 %own_part_of_residual.1.part = f32[64,16,128]{2,1,0:T(8,128)S(1)} custom-call(s32[4,64]{1,0:T(4,128)S(1)} %bitcast.15, s32[3]{0:T(128)S(1)} %pad_add_fusion.place, bf16[64,4,128,128]{3,2,1,0:T(8,128)(2,1)S(1)} %get-tuple-element.36.tiles.turned, bf16[64,16,128]{2,1,0:T(8,128)(2,1)S(1)} %get-tuple-element.45.own), custom_call_target="tpu_custom_call" | custom-call | flops 128 | bytes 128 | tf_op jit(solution)/shard_map/own_part_of_residual/pallas_call | solution.py:674
  32.0 0.0 collective-permute-done.7.b
  32.0 0.0 collective-permute-done.9.d
  32.1 0.8 %side_messages.1 = (bf16[656,128]{1,0:T(8,128)(2,1)S(1)}, bf16[656,128]{1,0:T(8,128)(2,1)S(1)}, bf16[128,1024]{1,0:T(8,128)(2,1)S(1)}, f32[16,128]{1,0:T(8,128)S...) custom-call(s32[3]{0:T(128)S(1)} %pad_add_fusion.place, bf16[38,16,128]{2,1,0:T(8,128)(2,1)S(1)} %get-tuple-element.46.a, ...), custom_call_target="tpu_custom_call" | custom-call | flops 128 | bytes 128 | tf_op jit(solution)/shard_map/side_messages/pallas_call | solution.py:683
  32.9 0.0 collective-permute-done.6.far
  32.9 4.9 %collective-permute-done.5.near = bf16[65,16,128]{2,1,0:T(8,128)(2,1)S(1)} collective-permute-done((bf16[65,16,128]{2,1,0:T(8,128)(2,1)S(1)}, bf16[65,16,128]{2,1,0:T(8,128)(2,1)S(1)}, u32[]{:S(2)}, u32[]{:S(2)}) %collective-permute-start.5) | collective-permute-done | bytes 266272 | tf_op jit(solution)/shard_map/ppermute | solution.py:575
  37.8 4.2 %residual_and_restriction.1 = (f32[64,16,128]{2,1,0:T(8,128)S(1)}, f32[8,16,128]{2,1,0:T(8,128)S(1)}, f32[8,16,128]{2,1,0:T(8,128)S(1)}, bf16[8,5,16,128]{3,2,1,0:T(8,128)(2,1)S(1)}) custom-call(s32[4,64]{1,0:T(4,128)S(1)} %bitcast.16, s32[5,64]{1,0:T(8,128)S(1)} %get-tuple-element.38.plan, s32[3]{0:T(128)S(1)} %pad_add_fusion.place, ...), custom_call_target="tpu_custom_call" | custom-call | flops 134217728 | bytes 8388608 | tf_op jit(solution)/shard_map/residual_and_restriction/pallas_call | solution.py:700
  42.1 13.2 %all_to_all.10.got = bf16[8,5,16,128]{3,2,1,0:T(8,128)(2,1)S(1)} all-to-all(bf16[8,5,16,128]{3,2,1,0:T(8,128)(2,1)S(1)} %get-tuple-element.52), channel_id=1, replica_groups=mesh['rows'=8,'cols'=4] {'rows'}, dimensions={0} | all-to-all | bytes 327680 | tf_op jit(solution)/shard_map/all_to_all | solution.py:721
  55.3 1.2 %coarse_and_mid_level.1 = (f32[8,16,128]{2,1,0:T(8,128)S(1)}, bf16[2,16,128]{2,1,0:T(8,128)(2,1)S(1)}, bf16[9,16,128]{2,1,0:T(8,128)(2,1)S(1)}, bf16[9,16,128]{2...) custom-call(s32[3]{0:T(128)S(1)} %pad_add_fusion.place, ...), custom_call_target="tpu_custom_call" | custom-call | flops 8388608 | bytes 524288 | tf_op jit(solution)/shard_map/coarse_and_mid_level/pallas_call | solution.py:722
  56.5 0.2 collective-permute-start.10
  56.7 1.2 %collective-permute-start.12 = (bf16[9,16,128]{2,1,0:T(8,128)(2,1)S(1)}, bf16[9,16,128]{2,1,0:T(8,128)(2,1)S(1)}, u32[]{:S(2)}, u32[]{:S(2)}) collective-permute-start(bf16[9,16,128]{2,1,0:T(8,128)(2,1)S(1)} %get-tuple-element.57), channel_id=1, source_target_pairs={{0,12},{4,8},{8,4},{12,0},{16,28},{20,24},{24,20},{28,16},{1,13},{... | collective-permute-start | bytes 110600 | tf_op jit(solution)/shard_map/ppermute | solution.py:756
  57.9 1.5 %collective-permute-start.11 = (bf16[9,16,128]{2,1,0:T(8,128)(2,1)S(1)}, bf16[9,16,128]{2,1,0:T(8,128)(2,1)S(1)}, u32[]{:S(2)}, u32[]{:S(2)}) collective-permute-start(bf16[9,16,128]{2,1,0:T(8,128)(2,1)S(1)} %get-tuple-element.57), channel_id=1, source_target_pairs={{12,16},{8,20},{0,4},{24,28},{16,12},{20,8},{4,0},{28,24},{13,17},... | collective-permute-start | bytes 110600 | tf_op jit(solution)/shard_map/ppermute | solution.py:755
  59.4 1.0 %collective-permute-start.13 = (bf16[16,128]{1,0:T(8,128)(2,1)S(1)}, bf16[16,128]{1,0:T(8,128)(2,1)S(1)}, u32[]{:S(2)}, u32[]{:S(2)}) collective-permute-start(bf16[16,128]{1,0:T(8,128)(2,1)S(1)} %get-tuple-element.58), channel_id=1, source_target_pairs={{0,8},{4,12},{8,0},{12,4},{16,24},{20,28},{24,16},{28,20},{1,9},{5... | collective-permute-start | bytes 12296 | tf_op jit(solution)/shard_map/ppermute | solution.py:756
  60.4 0.8 %collective-permute-start.14 = (bf16[16,128]{1,0:T(8,128)(2,1)S(1)}, bf16[16,128]{1,0:T(8,128)(2,1)S(1)}, u32[]{:S(2)}, u32[]{:S(2)}) collective-permute-start(bf16[16,128]{1,0:T(8,128)(2,1)S(1)} %get-tuple-element.59), channel_id=1, source_target_pairs={{8,16},{12,20},{0,4},{24,28},{16,8},{20,12},{4,0},{28,24},{9,17},{... | collective-permute-start | bytes 12296 | tf_op jit(solution)/shard_map/ppermute | solution.py:755
  61.2 1.1 %side_one_hot_rows.1 = (bf16[128,8192]{1,0:T(8,128)(2,1)S(1)}, bf16[128,8192]{1,0:T(8,128)(2,1)S(1)}) custom-call(bf16[2,16,128]{2,1,0:T(8,128)(2,1)S(1)} %get-tuple-element.61.after.c_edges, bf16[656,128]{1,0:T(8,128)(2,1)S(1)} %get-tuple-element.47.from_left, bf16[656,128]{1,0:T(8,128)(2,1)S(1)} %get-tuple-element.48.from_right), custom_call_target="tpu_custom_call" | custom-call | flops 128 | bytes 128 | tf_op jit(solution)/shard_map/side_one_hot_rows/pallas_call | solution.py:764
  62.3 0.7 collective-permute-done.13.nexts
  63.0 1.0 %collective-permute-done.14.beyond = bf16[16,128]{1,0:T(8,128)(2,1)S(1)} collective-permute-done((bf16[16,128]{1,0:T(8,128)(2,1)S(1)}, bf16[16,128]{1,0:T(8,128)(2,1)S(1)}, u32[]{:S(2)}, u32[]{:S(2)}) %collective-permute-start.14) | collective-permute-done | bytes 4128 | tf_op jit(solution)/shard_map/ppermute | solution.py:755
  64.0 0.0 collective-permute-done.10.near
  64.0 0.0 collective-permute-done.12.other
  64.0 0.0 collective-permute-done.11.far
  64.0 4.7 %prolongation_and_last_smoothing.1 = (f32[16,8192]{1,0:T(8,128)}, f32[8,8,128]{2,1,0:T(8,128)S(1)}) custom-call(s32[4,64]{1,0:T(4,128)S(1)} %bitcast.17, s32[3]{0:T(128)S(1)} %pad_add_fusion.place, bf16[64,4,128,128]{3,2,1,0:T(8,128)(2,1)S(1)} %get-tuple-element.36.tiles.turned, bf16[9,16,128]{2,1,0:T(8,128)(2,1)S(1)} %collective-permute-done.10.near, ...), custom_call_target="tpu_custom_call" | custom-call | flops 134217728 | bytes 8388608 | tf_op jit(solution)/shard_map/prolongation_and_last_smoothing/pallas_call | solution.py:772
  68.7 11.3 %all_to_all.11.got = f32[8,8,128]{2,1,0:T(8,128)S(1)} all-to-all(f32[8,8,128]{2,1,0:T(8,128)S(1)} %get-tuple-element.67), channel_id=1, replica_groups=mesh['rows'=8,'cols'=4] {'rows'}, dimensions={0} | all-to-all | bytes 65536 | tf_op jit(solution)/shard_map/all_to_all | solution.py:801
  80.0 0.7 gram_sum.1
  (7 shorter events, 0.0 us)
Async XLA Ops:
  0.6 9.5 %collective-permute-start.3 = (bf16[16,8192]{1,0:T(8,128)(2,1)}, bf16[16,8192]{1,0:T(8,128)(2,1)S(1)}, u32[]{:S(2)}, u32[]{:S(2)}) collective-permute-start(bf16[16,8192]{1,0:T(8,128)(2,1)} %bitcast.9), channel_id=1, source_target_pairs={{0,2},{1,3},{2,0},{3,1},{4,6},{5,7},{6,4},{7,5},{8,10},{9,11},{10,... | collective-permute-start | bytes 786440 | tf_op jit(solution)/shard_map/ppermute | solution.py:582
  4.5 5.4 %copy-start.3 = (bf16[8192,16]{0,1:T(8,128)(2,1)S(1)}, bf16[8192,16]{0,1:T(8,128)(2,1)}, u32[]{:S(2)}) copy-start(bf16[8192,16]{0,1:T(8,128)(2,1)} %param.9) | copy-start | bytes 786436
  4.5 6.0 %copy-start = (bf16[64,4,128,128]{3,2,1,0:T(8,128)(2,1)S(1)}, bf16[64,4,128,128]{3,2,1,0:T(8,128)(2,1)}, u32[]{:S(2)}) copy-start(bf16[64,4,128,128]{3,2,1,0:T(8,128)(2,1)} %tiles.3) | copy-start | bytes 25165828
  4.5 6.0 %copy-start.4 = (s32[64,4]{0,1:T(4,128)S(1)}, s32[64,4]{0,1:T(4,128)}, u32[]{:S(2)}) copy-start(s32[64,4]{0,1:T(4,128)} %param.11) | copy-start | bytes 3076
  7.6 15.8 %collective-permute-start = (bf16[91,16,128]{2,1,0:T(8,128)(2,1)S(1)}, bf16[91,16,128]{2,1,0:T(8,128)(2,1)S(1)}, u32[]{:S(2)}, u32[]{:S(2)}) collective-permute-start(bf16[91,16,128]{2,1,0:T(8,128)(2,1)S(1)} %get-tuple-element.39), channel_id=1, source_target_pairs={{0,4},{8,12},{16,20},{24,28},{4,0},{12,8},{20,16},{28,24},{1,5},{9... | collective-permute-start | bytes 1118216 | tf_op jit(solution)/shard_map/ppermute | solution.py:575
  9.2 6.7 %collective-permute-start.1 = (bf16[75,16,128]{2,1,0:T(8,128)(2,1)S(1)}, bf16[75,16,128]{2,1,0:T(8,128)(2,1)S(1)}, u32[]{:S(2)}, u32[]{:S(2)}) collective-permute-start(bf16[75,16,128]{2,1,0:T(8,128)(2,1)S(1)} %get-tuple-element.40), channel_id=1, source_target_pairs={{4,8},{12,16},{20,24},{8,4},{16,12},{24,20},{5,9},{13,17},{21,25},... | collective-permute-start | bytes 921608 | tf_op jit(solution)/shard_map/ppermute | solution.py:576
  9.9 6.0 %collective-permute-start.2 = (bf16[16,8192]{1,0:T(8,128)(2,1)S(1)}, bf16[16,8192]{1,0:T(8,128)(2,1)S(1)}, u32[]{:S(2)}, u32[]{:S(2)}) collective-permute-start(bf16[16,8192]{1,0:T(8,128)(2,1)S(1)} %bitcast.10), channel_id=1, source_target_pairs={{0,1},{1,0},{2,3},{3,2},{4,5},{5,4},{6,7},{7,6},{8,9},{9,8},{10,11... | collective-permute-start | bytes 786440 | tf_op jit(solution)/shard_map/ppermute | solution.py:582
  10.2 13.3 %collective-permute-start.4 = (bf16[16,8192]{1,0:T(8,128)(2,1)S(1)}, bf16[16,8192]{1,0:T(8,128)(2,1)S(1)}, u32[]{:S(2)}, u32[]{:S(2)}) collective-permute-start(bf16[16,8192]{1,0:T(8,128)(2,1)S(1)} %collective-permute-done.3.basis_c), channel_id=1, source_target_pairs={{0,1},{1,0},{2,3},{3,2},{4,5},{5,4},{6,7},{7,6},{8,9},{9,8},{10,11... | collective-permute-start | bytes 786440 | tf_op jit(solution)/shard_map/ppermute | solution.py:582
  24.9 5.3 %collective-permute-start.8 = (bf16[38,16,128]{2,1,0:T(8,128)(2,1)S(1)}, bf16[38,16,128]{2,1,0:T(8,128)(2,1)S(1)}, u32[]{:S(2)}, u32[]{:S(2)}) collective-permute-start(bf16[38,16,128]{2,1,0:T(8,128)(2,1)S(1)} %get-tuple-element.46.a), channel_id=1, source_target_pairs={{0,2},{1,3},{2,0},{3,1},{4,6},{5,7},{6,4},{7,5},{8,10},{9,11},{10,... | collective-permute-start | bytes 466952 | tf_op jit(solution)/shard_map/ppermute | solution.py:582
  25.5 12.3 %collective-permute-start.5 = (bf16[65,16,128]{2,1,0:T(8,128)(2,1)S(1)}, bf16[65,16,128]{2,1,0:T(8,128)(2,1)S(1)}, u32[]{:S(2)}, u32[]{:S(2)}) collective-permute-start(bf16[65,16,128]{2,1,0:T(8,128)(2,1)S(1)} %get-tuple-element.44), channel_id=1, source_target_pairs={{0,4},{8,12},{16,20},{24,28},{4,0},{12,8},{20,16},{28,24},{1,5},{9... | collective-permute-start | bytes 798728 | tf_op jit(solution)/shard_map/ppermute | solution.py:575
  28.0 4.0 %copy-start.1 = (bf16[8,3,128,128]{3,2,1,0:T(8,128)(2,1)S(1)}, bf16[8,3,128,128]{3,2,1,0:T(8,128)(2,1)}, u32[]{:S(2)}) copy-start(bf16[8,3,128,128]{3,2,1,0:T(8,128)(2,1)} %mid_tiles.9) | copy-start | bytes 2359300
  28.0 4.9 %collective-permute-start.6 = (bf16[64,16,128]{2,1,0:T(8,128)(2,1)S(1)}, bf16[64,16,128]{2,1,0:T(8,128)(2,1)S(1)}, u32[]{:S(2)}, u32[]{:S(2)}) collective-permute-start(bf16[64,16,128]{2,1,0:T(8,128)(2,1)S(1)} %get-tuple-element.45.own), channel_id=1, source_target_pairs={{4,8},{12,16},{20,24},{8,4},{16,12},{24,20},{5,9},{13,17},{21,25},... | collective-permute-start | bytes 786440 | tf_op jit(solution)/shard_map/ppermute | solution.py:576
  28.8 3.2 %collective-permute-start.7 = (bf16[38,16,128]{2,1,0:T(8,128)(2,1)S(1)}, bf16[38,16,128]{2,1,0:T(8,128)(2,1)S(1)}, u32[]{:S(2)}, u32[]{:S(2)}) collective-permute-start(bf16[38,16,128]{2,1,0:T(8,128)(2,1)S(1)} %get-tuple-element.46.a), channel_id=1, source_target_pairs={{0,1},{1,0},{2,3},{3,2},{4,5},{5,4},{6,7},{7,6},{8,9},{9,8},{10,11... | collective-permute-start | bytes 466952 | tf_op jit(solution)/shard_map/ppermute | solution.py:582
  30.2 1.8 %collective-permute-start.9 = (bf16[38,16,128]{2,1,0:T(8,128)(2,1)S(1)}, bf16[38,16,128]{2,1,0:T(8,128)(2,1)S(1)}, u32[]{:S(2)}, u32[]{:S(2)}) collective-permute-start(bf16[38,16,128]{2,1,0:T(8,128)(2,1)S(1)} %collective-permute-done.8.c), channel_id=1, source_target_pairs={{0,1},{1,0},{2,3},{3,2},{4,5},{5,4},{6,7},{7,6},{8,9},{9,8},{10,11... | collective-permute-start | bytes 466952 | tf_op jit(solution)/shard_map/ppermute | solution.py:582
  37.8 17.5 %copy-start.2 = (f32[128,1024]{1,0:T(8,128)S(1)}, f32[128,1024]{1,0:T(8,128)}, u32[]{:S(2)}) copy-start(f32[128,1024]{1,0:T(8,128)} %inverse_rows.3) | copy-start | bytes 1572868
  56.5 7.5 %collective-permute-start.10 = (bf16[9,16,128]{2,1,0:T(8,128)(2,1)S(1)}, bf16[9,16,128]{2,1,0:T(8,128)(2,1)S(1)}, u32[]{:S(2)}, u32[]{:S(2)}) collective-permute-start(bf16[9,16,128]{2,1,0:T(8,128)(2,1)S(1)} %get-tuple-element.56), channel_id=1, source_target_pairs={{0,4},{4,0},{8,12},{12,8},{16,20},{20,16},{24,28},{28,24},{1,5},{5... | collective-permute-start | bytes 110600 | tf_op jit(solution)/shard_map/ppermute | solution.py:756
  56.7 7.3 %collective-permute-start.12 = (bf16[9,16,128]{2,1,0:T(8,128)(2,1)S(1)}, bf16[9,16,128]{2,1,0:T(8,128)(2,1)S(1)}, u32[]{:S(2)}, u32[]{:S(2)}) collective-permute-start(bf16[9,16,128]{2,1,0:T(8,128)(2,1)S(1)} %get-tuple-element.57), channel_id=1, source_target_pairs={{0,12},{4,8},{8,4},{12,0},{16,28},{20,24},{24,20},{28,16},{1,13},{... | collective-permute-start | bytes 110600 | tf_op jit(solution)/shard_map/ppermute | solution.py:756
  57.9 6.1 %collective-permute-start.11 = (bf16[9,16,128]{2,1,0:T(8,128)(2,1)S(1)}, bf16[9,16,128]{2,1,0:T(8,128)(2,1)S(1)}, u32[]{:S(2)}, u32[]{:S(2)}) collective-permute-start(bf16[9,16,128]{2,1,0:T(8,128)(2,1)S(1)} %get-tuple-element.57), channel_id=1, source_target_pairs={{12,16},{8,20},{0,4},{24,28},{16,12},{20,8},{4,0},{28,24},{13,17},... | collective-permute-start | bytes 110600 | tf_op jit(solution)/shard_map/ppermute | solution.py:755
  59.4 3.6 %collective-permute-start.13 = (bf16[16,128]{1,0:T(8,128)(2,1)S(1)}, bf16[16,128]{1,0:T(8,128)(2,1)S(1)}, u32[]{:S(2)}, u32[]{:S(2)}) collective-permute-start(bf16[16,128]{1,0:T(8,128)(2,1)S(1)} %get-tuple-element.58), channel_id=1, source_target_pairs={{0,8},{4,12},{8,0},{12,4},{16,24},{20,28},{24,16},{28,20},{1,9},{5... | collective-permute-start | bytes 12296 | tf_op jit(solution)/shard_map/ppermute | solution.py:756
  60.4 3.6 %collective-permute-start.14 = (bf16[16,128]{1,0:T(8,128)(2,1)S(1)}, bf16[16,128]{1,0:T(8,128)(2,1)S(1)}, u32[]{:S(2)}, u32[]{:S(2)}) collective-permute-start(bf16[16,128]{1,0:T(8,128)(2,1)S(1)} %get-tuple-element.59), channel_id=1, source_target_pairs={{8,16},{12,20},{0,4},{24,28},{16,8},{20,12},{4,0},{28,24},{9,17},{... | collective-permute-start | bytes 12296 | tf_op jit(solution)/shard_map/ppermute | solution.py:755

commit v6 on v5

--- a/solution.py
+++ b/solution.py
@@ -185,7 +185,8 @@
     return row
 
 
-def own_first_kernel(index, place, tiles, own, out, turned_out, window):
+def own_first_kernel(index, place, plan, tiles, own, out, turned_out, window):
+    del plan
     blocks, slots = tiles.shape[:2]
     row = own_rows(index, place, own, window, slots)
     for g in range(blocks):
@@ -221,14 +222,16 @@
 
 
 def sides_kernel(
-    place, a, b, c, d, mid_tiles, owner, left_out, right_out, inverse_out, scale_out, mid_hot,
-    mid_block, buffer,
+    place, a, b, c, d, rows_a, rows_b, rows_c, rows_d, mid_tiles, owner, left_out, right_out,
+    inverse_out, scale_out, mid_hot, mid_block, buffer, rows_buffer,
 ):
     width, ext = a.shape[1:]
     tile_blocks = ext // width
     extra = tile_blocks + 3
     for n, piece in enumerate((a, b, c, d)):
         buffer[place[2] ^ n] = piece[...]
+    for n, piece in enumerate((rows_a, rows_b, rows_c, rows_d)):
+        rows_buffer[place[2] ^ n] = piece[...]
     share = inverse_out.shape[0] // 4
     wide = inverse_out.shape[1] // ext
     for out, first in ((left_out, 0), (right_out, extra)):
@@ -243,7 +246,7 @@
         for i in range(share // width):
             rows = slice(n * share + i * width, n * share + (i + 1) * width)
             for k in range(wide):
-                inverse_out[rows, k * ext : (k + 1) * ext] = buffer[n, 2 * extra + i * wide + k]
+                inverse_out[rows, k * ext : (k + 1) * ext] = rows_buffer[n, i * wide + k]
     mids = mid_tiles.shape[0]
     eye = eye_mask(ext)
     has_left, has_right = place[0] > 0, place[0] < place[1] - 1
@@ -296,7 +299,7 @@
 
 def second_kernel(
     index, plan, place, tiles, near, own, far, part, res, winv, hot, basis_b, basis_c, basis_d, b_out,
-    b16_out, b16_too, mine_out, window,
+    b16_out, b16_too, mine_out, rows_out, window,
 ):
     del hot, basis_b, basis_c, basis_d
     blocks, ext = own.shape[0], own.shape[2]
@@ -318,7 +321,7 @@
     extra = far.shape[0] - blocks
     mine_out[pl.ds((1 - odd) * extra, extra)] = near[blocks : blocks + extra]
     mine_out[pl.ds(odd * extra, extra)] = far[blocks:]
-    mine_out[2 * extra :] = near[blocks + extra :]
+    rows_out[...] = near[blocks + extra :]
 
 
 def split(row, ext):
@@ -577,11 +580,16 @@
     return near, far
 
 
-def from_columns(value):
+def relay_kernel(value, after, out):
+    del after
+    out[...] = value[...]
+
+
+def from_columns(value, relay=lambda v: v):
     peers = lax.axis_size("cols")
     swap = lambda v, n: lax.ppermute(v, "cols", [(i, i ^ n) for i in range(peers)])
     across = swap(value, 2)
-    return [swap(value, 1), across, swap(across, 1)]
+    return [swap(value, 1), across, swap(relay(across), 1)]
 
 
 def on_device(
@@ -643,24 +651,25 @@
     part_shape = shape((blocks, width, ext), F32)
     part, tiles = pl.pallas_call(
         own_first_kernel,
-        in_specs=[SM, SM, VM, VM],
+        in_specs=[SM, SM, SM, VM, VM],
         out_specs=[VM, VM],
         out_shape=[part_shape, shape(fine_tiles.shape, BF16)],
         scratch_shapes=[pltpu.VMEM((blocks + 1, width, ext), BF16)],
         name="own_part_and_turned_tiles",
         **params(4, ext, ext),
-    )(index, place, fine_tiles, a16)
+    )(index, place, plan, fine_tiles, a16)
     basis_pieces = [basis.T] + from_columns(basis.T)
 
-    b32, b16, b16_too, mine = pl.pallas_call(
+    b32, b16, b16_too, mine, mine_rows = pl.pallas_call(
         second_kernel,
         in_specs=[SM] * 3 + [VM] * 7 + [ANY] * 4,
-        out_specs=[VM] * 4,
+        out_specs=[VM] * 5,
         out_shape=[
             shape((blocks, width, ext), F32),
             shape((blocks, width, ext), BF16),
             shape((blocks + 1, width, ext), BF16),
-            shape((2 * extra + quarter, width, ext), BF16),
+            shape((2 * extra, width, ext), BF16),
+            shape((quarter, width, ext), BF16),
         ],
         scratch_shapes=[pltpu.VMEM((3 * blocks + 1, width, ext), BF16)],
         name="second_smoothing",
@@ -680,9 +689,19 @@
         name="own_part_of_residual",
         **params(4, ext, ext),
     )(index, place, tiles, b16)
+    def relay(value):
+        return pl.pallas_call(
+            relay_kernel,
+            in_specs=[VM, ANY],
+            out_specs=VM,
+            out_shape=shape(value.shape, value.dtype),
+            name="relay",
+            **params(4, ext, ext),
+        )(value, part)
+
     from_left, from_right, partner_rows, scale, mid_hot, mid_block = pl.pallas_call(
         sides_kernel,
-        in_specs=[SM] + [VM] * 6,
+        in_specs=[SM] + [VM] * 10,
         out_specs=[VM] * 6,
         out_shape=[
             shape((MESSAGE, ext), BF16),
@@ -692,10 +711,15 @@
             shape((ext, (mids + 4) * ext), BF16),
             shape((16, ext), jnp.int32),
         ],
-        scratch_shapes=[pltpu.VMEM((4, 2 * extra + quarter, width, ext), BF16)],
+        scratch_shapes=[
+            pltpu.VMEM((4, 2 * extra, width, ext), BF16),
+            pltpu.VMEM((4, quarter, width, ext), BF16),
+        ],
         name="side_messages",
         **params(4, ext, ext),
-    )(place, mine, *from_columns(mine), mid_tiles, owner)
+    )(
+        place, mine, *from_columns(mine, relay), mine_rows, *from_columns(mine_rows, relay), mid_tiles, owner,
+    )
 
     fres, u, bpart, send = pl.pallas_call(
         third_kernel,
@@ -783,7 +807,7 @@
             pltpu.VMEM((width, count), BF16),
             pltpu.VMEM((4, width, width), F32),
             pltpu.VMEM((width, count), F32),
-            pltpu.SemaphoreType.DMA((4,)),
+            pltpu.SemaphoreType.DMA((2,)),
         ],
         name="prolongation_and_last_smoothing",
         **params(8, 2 * tiles.size * width, tiles.size * 2),

time: 80.9 us -> 80.6 us (level)
  waiting for transfers between devices: 15.7 us -> 13.4 us
  starting transfers between devices: 14.3 us -> 16.2 us
    ppermute x2, waiting for transfers between devices: 12.5 us -> 9.26 us  [halo(): near = lax.ppermute(for_partner, 'rows', swap(even))]
    ppermute x6 -> x9, starting transfers between devices: 4.06 us -> 6.07 us  [from_columns(): lax.ppermute(v, 'cols', [(i, i ^ n) for i in range(peers)])]
    ppermute x6 -> x9, waiting for transfers between devices: 1.53 us -> 2.48 us  [from_columns(): lax.ppermute(v, 'cols', [(i, i ^ n) for i in range(peers)])]
    pallas_call x2 -> x4, Pallas kernels: 3.73 us -> 3.82 us  [the longest x1 2.97 us: on_device(): pl.pallas_call(own_first_kernel, in_specs=[SM, SM, SM, VM, VM], out_specs...]
  transfers between devices with their start and end apart: 15 -> 18, of which waited for: 6 -> 8; matrix products, arithmetic and copies ran while one was open for 1% -> 1% of each run, Pallas kernels for 15% -> 15%
where the time goes in v6:
time: 80.6 us; the launch traced here: 80.3 us
  Pallas kernels  24.6 us (31%)
  blocking collectives  24.5 us (30%)
  starting transfers between devices  16.2 us (20%)
  waiting for transfers between devices  13.4 us (17%)
  other arithmetic  0.85 us (1%)
    all_to_all x1, blocking collectives, on_device(): got = lax.all_to_all(send, 'rows', 0, 0)  13.2 us
    all_to_all x1, blocking collectives, finish(): lax.all_to_all(grams, 'rows', 0, 0)  11.3 us
    ppermute x2, waiting for transfers between devices, halo(): near = lax.ppermute(for_partner, 'rows', swap(even))  9.26 us
    ppermute x9, starting transfers between devices, from_columns(): lax.ppermute(v, 'cols', [(i, i ^ n) for i in range(peers)])  6.07 us
    pallas_call x1, Pallas kernels, finish(): pl.pallas_call(last_kernel, in_specs=[SM, SM] + [VM] * 23, out_specs=[HBM...  4.61 us
    pallas_call x1, Pallas kernels, on_device(): pl.pallas_call(third_kernel, in_specs=[SM] * 3 + [VM] * 14, out_specs=[VM...  4.24 us
    ppermute x2, starting transfers between devices, halo(): near = lax.ppermute(for_partner, 'rows', swap(even))  4.13 us
    pallas_call x1, Pallas kernels, on_device(): pl.pallas_call(first_kernel, in_specs=[SM] + [HBM] * 3 + [VM, HBM], out_s...  3.13 us
  transfers between devices with their start and end apart: 18, of which 8 were waited for; matrix products, arithmetic and copies ran while one was open for 1% of the time, Pallas kernels for 15%

profile of v6, /device:TPU:0, one launch (start us, length us, event | category | flops | bytes accessed | tf_op | source)
XLA Modules:
  0.0 80.3 jit_solution(17170127241345170728)
XLA Ops:
  0.6 3.0 %collective-permute-start.3 = (bf16[16,8192]{1,0:T(8,128)(2,1)}, bf16[16,8192]{1,0:T(8,128)(2,1)S(1)}, u32[]{:S(2)}, u32[]{:S(2)}) collective-permute-start(bf16[16,8192]{1,0:T(8,128)(2,1)} %bitcast.9), channel_id=1, source_target_pairs={{0,2},{1,3},{2,0},{3,1},{4,6},{5,7},{6,4},{7,5},{8,10},{9,11},{10,... | collective-permute-start | bytes 786440 | tf_op jit(solution)/shard_map/ppermute | solution.py:590
  3.6 0.1 pad_add_fusion.place
  3.7 0.8 add_bitcast_fusion.owner
  4.5 3.1 %first_smoothing.1 = (bf16[64,16,128]{2,1,0:T(8,128)(2,1)S(1)}, bf16[91,16,128]{2,1,0:T(8,128)(2,1)S(1)}, bf16[75,16,128]{2,1,0:T(8,128)(2,1)S(1)}, f32[64,128]{1,0:T(8,128)S(1)}, f32[64,16,128]{2,1,0:T(8,128)S(1)}) custom-call(s32[3]{0:T(128)S(1)} %pad_add_fusion.place, f32[16,8192]{1,0:T(8,128)} %bitcast.18, bf16[64,4,128,128]{3,2,1,0:T(8,128)(2,1)} %tiles.3, ...), custom_call_target="tpu_custom_call" | custom-call | flops 1048576 | bytes 2097152 | tf_op jit(solution)/shard_map/first_smoothing/pallas_call | solution.py:618
  7.6 1.6 %collective-permute-start = (bf16[91,16,128]{2,1,0:T(8,128)(2,1)S(1)}, bf16[91,16,128]{2,1,0:T(8,128)(2,1)S(1)}, u32[]{:S(2)}, u32[]{:S(2)}) collective-permute-start(bf16[91,16,128]{2,1,0:T(8,128)(2,1)S(1)} %get-tuple-element.40), channel_id=1, source_target_pairs={{0,4},{8,12},{16,20},{24,28},{4,0},{12,8},{20,16},{28,24},{1,5},{9... | collective-permute-start | bytes 1118216 | tf_op jit(solution)/shard_map/ppermute | solution.py:578
  9.2 0.7 collective-permute-start.1
  9.9 0.1 collective-permute-start.2
  10.0 0.2 collective-permute-done.3.basis_c
  10.2 0.3 collective-permute-start.4
  10.5 2.5 %one_hot_rows.1 = (bf16[128,8192]{1,0:T(8,128)(2,1)S(1)}, s32[5,64]{1,0:T(8,128)S(1)}) custom-call(s32[3]{0:T(128)S(1)} %pad_add_fusion.place, s32[4,64]{1,0:T(4,128)S(1)} %bitcast.12, f32[64,128]{1,0:T(8,128)S(1)} %get-tuple-element.36.after.winv, s32[72,128]{1,0:T(8,128)S(1)} %add_bitcast_fusion.owner), custom_call_target="tpu_custom_call" | custom-call | flops 1048576 | bytes 33554432 | tf_op jit(solution)/shard_map/one_hot_rows/pallas_call | solution.py:642
  13.0 3.0 %own_part_and_turned_tiles.1 = (f32[64,16,128]{2,1,0:T(8,128)S(1)}, bf16[64,4,128,128]{3,2,1,0:T(8,128)(2,1)S(1)}) custom-call(s32[4,64]{1,0:T(4,128)S(1)} %bitcast.13, s32[3]{0:T(128)S(1)} %pad_add_fusion.place, s32[5,64]{1,0:T(8,128)S(1)} %get-tuple-element.37.plan, bf16[64,4,128,128]{3,2,1,0:T(8,128)(2,1)S(1)} %copy-done, ...), custom_call_target="tpu_custom_call" | custom-call | flops 128 | bytes 128 | tf_op jit(solution)/shard_map/own_part_and_turned_tiles/pallas_call | solution.py:652
  15.9 0.0 collective-permute-done.2.basis_b
  15.9 0.0 collective-permute-done.1.far
  16.0 7.5 %collective-permute-done.near = bf16[91,16,128]{2,1,0:T(8,128)(2,1)S(1)} collective-permute-done((bf16[91,16,128]{2,1,0:T(8,128)(2,1)S(1)}, bf16[91,16,128]{2,1,0:T(8,128)(2,1)S(1)}, u32[]{:S(2)}, u32[]{:S(2)}) %collective-permute-start) | collective-permute-done | bytes 372768 | tf_op jit(solution)/shard_map/ppermute | solution.py:578
  23.5 0.0 collective-permute-done.4.basis_d
  23.5 1.5 %second_smoothing.1 = (f32[64,16,128]{2,1,0:T(8,128)S(1)}, bf16[64,16,128]{2,1,0:T(8,128)(2,1)S(1)}, bf16[65,16,128]{2,1,0:T(8,128)(2,1)S(1)}, bf16[22,16,128]{2,1,0:T(8,128)(2,1)S(1)}, bf16[16,16,128]{2,1,0:T(8,128)(2,1)S(1)}) custom-call(s32[4,64]{1,0:T(4,128)S(1)} %bitcast.14, s32[5,64]{1,0:T(8,128)S(1)} %get-tuple-element.37.plan, ...), custom_call_target="tpu_custom_call" | custom-call | flops 134217728 | bytes 8388608 | tf_op jit(solution)/shard_map/second_smoothing/pallas_call | solution.py:663
  24.9 2.5 %collective-permute-start.5 = (bf16[65,16,128]{2,1,0:T(8,128)(2,1)S(1)}, bf16[65,16,128]{2,1,0:T(8,128)(2,1)S(1)}, u32[]{:S(2)}, u32[]{:S(2)}) collective-permute-start(bf16[65,16,128]{2,1,0:T(8,128)(2,1)S(1)} %get-tuple-element.45), channel_id=1, source_target_pairs={{0,4},{8,12},{16,20},{24,28},{4,0},{12,8},{20,16},{28,24},{1,5},{9... | collective-permute-start | bytes 798728 | tf_op jit(solution)/shard_map/ppermute | solution.py:578
  27.5 0.7 collective-permute-start.6
  28.2 0.6 collective-permute-start.8
  28.8 1.5 %collective-permute-start.11 = (bf16[16,16,128]{2,1,0:T(8,128)(2,1)S(1)}, bf16[16,16,128]{2,1,0:T(8,128)(2,1)S(1)}, u32[]{:S(2)}, u32[]{:S(2)}) collective-permute-start(bf16[16,16,128]{2,1,0:T(8,128)(2,1)S(1)} %get-tuple-element.48.rows_a), channel_id=1, source_target_pairs={{0,2},{1,3},{2,0},{3,1},{4,6},{5,7},{6,4},{7,5},{8,10},{9,11},{10,... | collective-permute-start | bytes 196616 | tf_op jit(solution)/shard_map/ppermute | solution.py:590
  30.3 0.0 collective-permute-start.10
  30.3 1.8 %own_part_of_residual.1.after.part = f32[64,16,128]{2,1,0:T(8,128)S(1)} custom-call(s32[4,64]{1,0:T(4,128)S(1)} %bitcast.15, s32[3]{0:T(128)S(1)} %pad_add_fusion.place, bf16[64,4,128,128]{3,2,1,0:T(8,128)(2,1)S(1)} %get-tuple-element.39.tiles.turned, bf16[64,16,128]{2,1,0:T(8,128)(2,1)S(1)} %get-tuple-element.46.own), custom_call_target="tpu_custom_call" | custom-call | flops 128 | bytes 128 | tf_op jit(solution)/shard_map/own_part_of_residual/pallas_call | solution.py:683
  32.1 0.7 collective-permute-done.8.value.c
  32.8 0.0 collective-permute-start.7
  32.8 0.7 collective-permute-done.11.value.rows_c
  33.5 0.0 collective-permute-start.9
  33.5 0.6 collective-permute-start.12
  34.1 0.0 collective-permute-done.7.b
  34.1 0.9 %collective-permute-done.12.rows_d = bf16[16,16,128]{2,1,0:T(8,128)(2,1)S(1)} collective-permute-done((bf16[16,16,128]{2,1,0:T(8,128)(2,1)S(1)}, bf16[16,16,128]{2,1,0:T(8,128)(2,1)S(1)}, u32[]{:S(2)}, u32[]{:S(2)}) %collective-permute-start.12) | collective-permute-done | bytes 65568 | tf_op jit(solution)/shard_map/ppermute | solution.py:590
  35.0 0.8 %side_messages.1 = (bf16[656,128]{1,0:T(8,128)(2,1)S(1)}, bf16[656,128]{1,0:T(8,128)(2,1)S(1)}, bf16[128,1024]{1,0:T(8,128)(2,1)S(1)}, f32[16,128]{1,0:T(8,128)S...) custom-call(s32[3]{0:T(128)S(1)} %pad_add_fusion.place, bf16[22,16,128]{2,1,0:T(8,128)(2,1)S(1)} %get-tuple-element.47.a, ...), custom_call_target="tpu_custom_call" | custom-call | flops 128 | bytes 128 | tf_op jit(solution)/shard_map/side_messages/pallas_call | solution.py:702
  35.8 1.8 %collective-permute-done.5.near = bf16[65,16,128]{2,1,0:T(8,128)(2,1)S(1)} collective-permute-done((bf16[65,16,128]{2,1,0:T(8,128)(2,1)S(1)}, bf16[65,16,128]{2,1,0:T(8,128)(2,1)S(1)}, u32[]{:S(2)}, u32[]{:S(2)}) %collective-permute-start.5) | collective-permute-done | bytes 266272 | tf_op jit(solution)/shard_map/ppermute | solution.py:578
  37.6 4.2 %residual_and_restriction.1 = (f32[64,16,128]{2,1,0:T(8,128)S(1)}, f32[8,16,128]{2,1,0:T(8,128)S(1)}, f32[8,16,128]{2,1,0:T(8,128)S(1)}, bf16[8,5,16,128]{3,2,1,0:T(8,128)(2,1)S(1)}) custom-call(s32[4,64]{1,0:T(4,128)S(1)} %bitcast.16, s32[5,64]{1,0:T(8,128)S(1)} %get-tuple-element.37.plan, s32[3]{0:T(128)S(1)} %pad_add_fusion.place, ...), custom_call_target="tpu_custom_call" | custom-call | flops 134217728 | bytes 8388608 | tf_op jit(solution)/shard_map/residual_and_restriction/pallas_call | solution.py:724
  41.8 13.2 %all_to_all.10.got = bf16[8,5,16,128]{3,2,1,0:T(8,128)(2,1)S(1)} all-to-all(bf16[8,5,16,128]{3,2,1,0:T(8,128)(2,1)S(1)} %get-tuple-element.54), channel_id=1, replica_groups=mesh['rows'=8,'cols'=4] {'rows'}, dimensions={0} | all-to-all | bytes 327680 | tf_op jit(solution)/shard_map/all_to_all | solution.py:745
  55.0 1.2 %coarse_and_mid_level.1 = (f32[8,16,128]{2,1,0:T(8,128)S(1)}, bf16[2,16,128]{2,1,0:T(8,128)(2,1)S(1)}, bf16[9,16,128]{2,1,0:T(8,128)(2,1)S(1)}, bf16[9,16,128]{2...) custom-call(s32[3]{0:T(128)S(1)} %pad_add_fusion.place, ...), custom_call_target="tpu_custom_call" | custom-call | flops 8388608 | bytes 524288 | tf_op jit(solution)/shard_map/coarse_and_mid_level/pallas_call | solution.py:746
  56.3 0.2 collective-permute-start.13
  56.5 1.2 %collective-permute-start.15 = (bf16[9,16,128]{2,1,0:T(8,128)(2,1)S(1)}, bf16[9,16,128]{2,1,0:T(8,128)(2,1)S(1)}, u32[]{:S(2)}, u32[]{:S(2)}) collective-permute-start(bf16[9,16,128]{2,1,0:T(8,128)(2,1)S(1)} %get-tuple-element.59), channel_id=1, source_target_pairs={{0,12},{4,8},{8,4},{12,0},{16,28},{20,24},{24,20},{28,16},{1,13},{... | collective-permute-start | bytes 110600 | tf_op jit(solution)/shard_map/ppermute | solution.py:780
  57.7 1.5 %collective-permute-start.14 = (bf16[9,16,128]{2,1,0:T(8,128)(2,1)S(1)}, bf16[9,16,128]{2,1,0:T(8,128)(2,1)S(1)}, u32[]{:S(2)}, u32[]{:S(2)}) collective-permute-start(bf16[9,16,128]{2,1,0:T(8,128)(2,1)S(1)} %get-tuple-element.59), channel_id=1, source_target_pairs={{12,16},{8,20},{0,4},{24,28},{16,12},{20,8},{4,0},{28,24},{13,17},... | collective-permute-start | bytes 110600 | tf_op jit(solution)/shard_map/ppermute | solution.py:779
  59.1 1.0 %collective-permute-start.16 = (bf16[16,128]{1,0:T(8,128)(2,1)S(1)}, bf16[16,128]{1,0:T(8,128)(2,1)S(1)}, u32[]{:S(2)}, u32[]{:S(2)}) collective-permute-start(bf16[16,128]{1,0:T(8,128)(2,1)S(1)} %get-tuple-element.60), channel_id=1, source_target_pairs={{0,8},{4,12},{8,0},{12,4},{16,24},{20,28},{24,16},{28,20},{1,9},{5... | collective-permute-start | bytes 12296 | tf_op jit(solution)/shard_map/ppermute | solution.py:780
  60.1 0.8 %collective-permute-start.17 = (bf16[16,128]{1,0:T(8,128)(2,1)S(1)}, bf16[16,128]{1,0:T(8,128)(2,1)S(1)}, u32[]{:S(2)}, u32[]{:S(2)}) collective-permute-start(bf16[16,128]{1,0:T(8,128)(2,1)S(1)} %get-tuple-element.61), channel_id=1, source_target_pairs={{8,16},{12,20},{0,4},{24,28},{16,8},{20,12},{4,0},{28,24},{9,17},{... | collective-permute-start | bytes 12296 | tf_op jit(solution)/shard_map/ppermute | solution.py:779
  61.0 1.1 %side_one_hot_rows.1 = (bf16[128,8192]{1,0:T(8,128)(2,1)S(1)}, bf16[128,8192]{1,0:T(8,128)(2,1)S(1)}) custom-call(bf16[2,16,128]{2,1,0:T(8,128)(2,1)S(1)} %get-tuple-element.63.after.c_edges, bf16[656,128]{1,0:T(8,128)(2,1)S(1)} %get-tuple-element.49.from_left, bf16[656,128]{1,0:T(8,128)(2,1)S(1)} %get-tuple-element.50.from_right), custom_call_target="tpu_custom_call" | custom-call | flops 128 | bytes 128 | tf_op jit(solution)/shard_map/side_one_hot_rows/pallas_call | solution.py:788
  62.1 0.7 collective-permute-done.16.nexts
  62.7 1.0 %collective-permute-done.17.beyond = bf16[16,128]{1,0:T(8,128)(2,1)S(1)} collective-permute-done((bf16[16,128]{1,0:T(8,128)(2,1)S(1)}, bf16[16,128]{1,0:T(8,128)(2,1)S(1)}, u32[]{:S(2)}, u32[]{:S(2)}) %collective-permute-start.17) | collective-permute-done | bytes 4128 | tf_op jit(solution)/shard_map/ppermute | solution.py:779
  63.7 0.0 collective-permute-done.13.near
  63.7 0.0 collective-permute-done.15.other
  63.7 0.0 collective-permute-done.14.far
  63.7 4.6 %prolongation_and_last_smoothing.1 = (f32[16,8192]{1,0:T(8,128)}, f32[8,8,128]{2,1,0:T(8,128)S(1)}) custom-call(s32[4,64]{1,0:T(4,128)S(1)} %bitcast.17, s32[3]{0:T(128)S(1)} %pad_add_fusion.place, bf16[64,4,128,128]{3,2,1,0:T(8,128)(2,1)S(1)} %get-tuple-element.39.tiles.turned, bf16[9,16,128]{2,1,0:T(8,128)(2,1)S(1)} %collective-permute-done.13.near, ...), custom_call_target="tpu_custom_call" | custom-call | flops 134217728 | bytes 8388608 | tf_op jit(solution)/shard_map/prolongation_and_last_smoothing/pallas_call | solution.py:796
  68.4 11.3 %all_to_all.11.got = f32[8,8,128]{2,1,0:T(8,128)S(1)} all-to-all(f32[8,8,128]{2,1,0:T(8,128)S(1)} %get-tuple-element.69), channel_id=1, replica_groups=mesh['rows'=8,'cols'=4] {'rows'}, dimensions={0} | all-to-all | bytes 65536 | tf_op jit(solution)/shard_map/all_to_all | solution.py:825
  79.6 0.7 gram_sum.1
  (15 shorter events, 0.0 us)
Async XLA Ops:
  0.6 9.5 %collective-permute-start.3 = (bf16[16,8192]{1,0:T(8,128)(2,1)}, bf16[16,8192]{1,0:T(8,128)(2,1)S(1)}, u32[]{:S(2)}, u32[]{:S(2)}) collective-permute-start(bf16[16,8192]{1,0:T(8,128)(2,1)} %bitcast.9), channel_id=1, source_target_pairs={{0,2},{1,3},{2,0},{3,1},{4,6},{5,7},{6,4},{7,5},{8,10},{9,11},{10,... | collective-permute-start | bytes 786440 | tf_op jit(solution)/shard_map/ppermute | solution.py:590
  4.5 5.4 %copy-start.3 = (bf16[8192,16]{0,1:T(8,128)(2,1)S(1)}, bf16[8192,16]{0,1:T(8,128)(2,1)}, u32[]{:S(2)}) copy-start(bf16[8192,16]{0,1:T(8,128)(2,1)} %param.9) | copy-start | bytes 786436
  4.5 6.0 %copy-start.4 = (s32[64,4]{0,1:T(4,128)S(1)}, s32[64,4]{0,1:T(4,128)}, u32[]{:S(2)}) copy-start(s32[64,4]{0,1:T(4,128)} %param.11) | copy-start | bytes 3076
  4.5 8.5 %copy-start = (bf16[64,4,128,128]{3,2,1,0:T(8,128)(2,1)S(1)}, bf16[64,4,128,128]{3,2,1,0:T(8,128)(2,1)}, u32[]{:S(2)}) copy-start(bf16[64,4,128,128]{3,2,1,0:T(8,128)(2,1)} %tiles.3) | copy-start | bytes 25165828
  7.6 15.8 %collective-permute-start = (bf16[91,16,128]{2,1,0:T(8,128)(2,1)S(1)}, bf16[91,16,128]{2,1,0:T(8,128)(2,1)S(1)}, u32[]{:S(2)}, u32[]{:S(2)}) collective-permute-start(bf16[91,16,128]{2,1,0:T(8,128)(2,1)S(1)} %get-tuple-element.40), channel_id=1, source_target_pairs={{0,4},{8,12},{16,20},{24,28},{4,0},{12,8},{20,16},{28,24},{1,5},{9... | collective-permute-start | bytes 1118216 | tf_op jit(solution)/shard_map/ppermute | solution.py:578
  9.2 6.7 %collective-permute-start.1 = (bf16[75,16,128]{2,1,0:T(8,128)(2,1)S(1)}, bf16[75,16,128]{2,1,0:T(8,128)(2,1)S(1)}, u32[]{:S(2)}, u32[]{:S(2)}) collective-permute-start(bf16[75,16,128]{2,1,0:T(8,128)(2,1)S(1)} %get-tuple-element.41), channel_id=1, source_target_pairs={{4,8},{12,16},{20,24},{8,4},{16,12},{24,20},{5,9},{13,17},{21,25},... | collective-permute-start | bytes 921608 | tf_op jit(solution)/shard_map/ppermute | solution.py:579
  9.9 6.0 %collective-permute-start.2 = (bf16[16,8192]{1,0:T(8,128)(2,1)S(1)}, bf16[16,8192]{1,0:T(8,128)(2,1)S(1)}, u32[]{:S(2)}, u32[]{:S(2)}) collective-permute-start(bf16[16,8192]{1,0:T(8,128)(2,1)S(1)} %bitcast.10), channel_id=1, source_target_pairs={{0,1},{1,0},{2,3},{3,2},{4,5},{5,4},{6,7},{7,6},{8,9},{9,8},{10,11... | collective-permute-start | bytes 786440 | tf_op jit(solution)/shard_map/ppermute | solution.py:590
  10.2 13.3 %collective-permute-start.4 = (bf16[16,8192]{1,0:T(8,128)(2,1)S(1)}, bf16[16,8192]{1,0:T(8,128)(2,1)S(1)}, u32[]{:S(2)}, u32[]{:S(2)}) collective-permute-start(bf16[16,8192]{1,0:T(8,128)(2,1)S(1)} %collective-permute-done.3.basis_c), channel_id=1, source_target_pairs={{0,1},{1,0},{2,3},{3,2},{4,5},{5,4},{6,7},{7,6},{8,9},{9,8},{10,11... | collective-permute-start | bytes 786440 | tf_op jit(solution)/shard_map/ppermute | solution.py:590
  24.9 12.6 %collective-permute-start.5 = (bf16[65,16,128]{2,1,0:T(8,128)(2,1)S(1)}, bf16[65,16,128]{2,1,0:T(8,128)(2,1)S(1)}, u32[]{:S(2)}, u32[]{:S(2)}) collective-permute-start(bf16[65,16,128]{2,1,0:T(8,128)(2,1)S(1)} %get-tuple-element.45), channel_id=1, source_target_pairs={{0,4},{8,12},{16,20},{24,28},{4,0},{12,8},{20,16},{28,24},{1,5},{9... | collective-permute-start | bytes 798728 | tf_op jit(solution)/shard_map/ppermute | solution.py:578
  27.5 8.3 %collective-permute-start.6 = (bf16[64,16,128]{2,1,0:T(8,128)(2,1)S(1)}, bf16[64,16,128]{2,1,0:T(8,128)(2,1)S(1)}, u32[]{:S(2)}, u32[]{:S(2)}) collective-permute-start(bf16[64,16,128]{2,1,0:T(8,128)(2,1)S(1)} %get-tuple-element.46.own), channel_id=1, source_target_pairs={{4,8},{12,16},{20,24},{8,4},{16,12},{24,20},{5,9},{13,17},{21,25},... | collective-permute-start | bytes 786440 | tf_op jit(solution)/shard_map/ppermute | solution.py:579
  28.2 4.6 %collective-permute-start.8 = (bf16[22,16,128]{2,1,0:T(8,128)(2,1)S(1)}, bf16[22,16,128]{2,1,0:T(8,128)(2,1)S(1)}, u32[]{:S(2)}, u32[]{:S(2)}) collective-permute-start(bf16[22,16,128]{2,1,0:T(8,128)(2,1)S(1)} %get-tuple-element.47.a), channel_id=1, source_target_pairs={{0,2},{1,3},{2,0},{3,1},{4,6},{5,7},{6,4},{7,5},{8,10},{9,11},{10,... | collective-permute-start | bytes 270344 | tf_op jit(solution)/shard_map/ppermute | solution.py:590
  28.8 6.2 %copy-start.1 = (bf16[8,3,128,128]{3,2,1,0:T(8,128)(2,1)S(1)}, bf16[8,3,128,128]{3,2,1,0:T(8,128)(2,1)}, u32[]{:S(2)}) copy-start(bf16[8,3,128,128]{3,2,1,0:T(8,128)(2,1)} %mid_tiles.9) | copy-start | bytes 2359300
  28.8 4.7 %collective-permute-start.11 = (bf16[16,16,128]{2,1,0:T(8,128)(2,1)S(1)}, bf16[16,16,128]{2,1,0:T(8,128)(2,1)S(1)}, u32[]{:S(2)}, u32[]{:S(2)}) collective-permute-start(bf16[16,16,128]{2,1,0:T(8,128)(2,1)S(1)} %get-tuple-element.48.rows_a), channel_id=1, source_target_pairs={{0,2},{1,3},{2,0},{3,1},{4,6},{5,7},{6,4},{7,5},{8,10},{9,11},{10,... | collective-permute-start | bytes 196616 | tf_op jit(solution)/shard_map/ppermute | solution.py:590
  30.3 3.2 %collective-permute-start.10 = (bf16[16,16,128]{2,1,0:T(8,128)(2,1)S(1)}, bf16[16,16,128]{2,1,0:T(8,128)(2,1)S(1)}, u32[]{:S(2)}, u32[]{:S(2)}) collective-permute-start(bf16[16,16,128]{2,1,0:T(8,128)(2,1)S(1)} %get-tuple-element.48.rows_a), channel_id=1, source_target_pairs={{0,1},{1,0},{2,3},{3,2},{4,5},{5,4},{6,7},{7,6},{8,9},{9,8},{10,11... | collective-permute-start | bytes 196616 | tf_op jit(solution)/shard_map/ppermute | solution.py:590
  32.8 1.3 %collective-permute-start.7 = (bf16[22,16,128]{2,1,0:T(8,128)(2,1)S(1)}, bf16[22,16,128]{2,1,0:T(8,128)(2,1)S(1)}, u32[]{:S(2)}, u32[]{:S(2)}) collective-permute-start(bf16[22,16,128]{2,1,0:T(8,128)(2,1)S(1)} %get-tuple-element.47.a), channel_id=1, source_target_pairs={{0,1},{1,0},{2,3},{3,2},{4,5},{5,4},{6,7},{7,6},{8,9},{9,8},{10,11... | collective-permute-start | bytes 270344 | tf_op jit(solution)/shard_map/ppermute | solution.py:590
  33.5 1.5 %collective-permute-start.9 = (bf16[22,16,128]{2,1,0:T(8,128)(2,1)S(1)}, bf16[22,16,128]{2,1,0:T(8,128)(2,1)S(1)}, u32[]{:S(2)}, u32[]{:S(2)}) collective-permute-start(bf16[22,16,128]{2,1,0:T(8,128)(2,1)S(1)} %relay.2), channel_id=1, source_target_pairs={{0,1},{1,0},{2,3},{3,2},{4,5},{5,4},{6,7},{7,6},{8,9},{9,8},{10,11... | collective-permute-start | bytes 270344 | tf_op jit(solution)/shard_map/ppermute | solution.py:590
  33.5 1.5 %collective-permute-start.12 = (bf16[16,16,128]{2,1,0:T(8,128)(2,1)S(1)}, bf16[16,16,128]{2,1,0:T(8,128)(2,1)S(1)}, u32[]{:S(2)}, u32[]{:S(2)}) collective-permute-start(bf16[16,16,128]{2,1,0:T(8,128)(2,1)S(1)} %relay.3), channel_id=1, source_target_pairs={{0,1},{1,0},{2,3},{3,2},{4,5},{5,4},{6,7},{7,6},{8,9},{9,8},{10,11... | collective-permute-start | bytes 196616 | tf_op jit(solution)/shard_map/ppermute | solution.py:590
  37.6 17.5 %copy-start.2 = (f32[128,1024]{1,0:T(8,128)S(1)}, f32[128,1024]{1,0:T(8,128)}, u32[]{:S(2)}) copy-start(f32[128,1024]{1,0:T(8,128)} %inverse_rows.3) | copy-start | bytes 1572868
  56.3 7.5 %collective-permute-start.13 = (bf16[9,16,128]{2,1,0:T(8,128)(2,1)S(1)}, bf16[9,16,128]{2,1,0:T(8,128)(2,1)S(1)}, u32[]{:S(2)}, u32[]{:S(2)}) collective-permute-start(bf16[9,16,128]{2,1,0:T(8,128)(2,1)S(1)} %get-tuple-element.58), channel_id=1, source_target_pairs={{0,4},{4,0},{8,12},{12,8},{16,20},{20,16},{24,28},{28,24},{1,5},{5... | collective-permute-start | bytes 110600 | tf_op jit(solution)/shard_map/ppermute | solution.py:780
  56.5 7.2 %collective-permute-start.15 = (bf16[9,16,128]{2,1,0:T(8,128)(2,1)S(1)}, bf16[9,16,128]{2,1,0:T(8,128)(2,1)S(1)}, u32[]{:S(2)}, u32[]{:S(2)}) collective-permute-start(bf16[9,16,128]{2,1,0:T(8,128)(2,1)S(1)} %get-tuple-element.59), channel_id=1, source_target_pairs={{0,12},{4,8},{8,4},{12,0},{16,28},{20,24},{24,20},{28,16},{1,13},{... | collective-permute-start | bytes 110600 | tf_op jit(solution)/shard_map/ppermute | solution.py:780
  57.7 6.1 %collective-permute-start.14 = (bf16[9,16,128]{2,1,0:T(8,128)(2,1)S(1)}, bf16[9,16,128]{2,1,0:T(8,128)(2,1)S(1)}, u32[]{:S(2)}, u32[]{:S(2)}) collective-permute-start(bf16[9,16,128]{2,1,0:T(8,128)(2,1)S(1)} %get-tuple-element.59), channel_id=1, source_target_pairs={{12,16},{8,20},{0,4},{24,28},{16,12},{20,8},{4,0},{28,24},{13,17},... | collective-permute-start | bytes 110600 | tf_op jit(solution)/shard_map/ppermute | solution.py:779
  59.1 3.6 %collective-permute-start.16 = (bf16[16,128]{1,0:T(8,128)(2,1)S(1)}, bf16[16,128]{1,0:T(8,128)(2,1)S(1)}, u32[]{:S(2)}, u32[]{:S(2)}) collective-permute-start(bf16[16,128]{1,0:T(8,128)(2,1)S(1)} %get-tuple-element.60), channel_id=1, source_target_pairs={{0,8},{4,12},{8,0},{12,4},{16,24},{20,28},{24,16},{28,20},{1,9},{5... | collective-permute-start | bytes 12296 | tf_op jit(solution)/shard_map/ppermute | solution.py:780
  60.1 3.6 %collective-permute-start.17 = (bf16[16,128]{1,0:T(8,128)(2,1)S(1)}, bf16[16,128]{1,0:T(8,128)(2,1)S(1)}, u32[]{:S(2)}, u32[]{:S(2)}) collective-permute-start(bf16[16,128]{1,0:T(8,128)(2,1)S(1)} %get-tuple-element.61), channel_id=1, source_target_pairs={{8,16},{12,20},{0,4},{24,28},{16,8},{20,12},{4,0},{28,24},{9,17},{... | collective-permute-start | bytes 12296 | tf_op jit(solution)/shard_map/ppermute | solution.py:779

commit v7 on v6

--- a/solution.py
+++ b/solution.py
@@ -580,16 +580,18 @@
     return near, far
 
 
-def relay_kernel(value, after, out):
+def relay_kernel(one, two, after, one_out, two_out):
     del after
-    out[...] = value[...]
-
-
-def from_columns(value, relay=lambda v: v):
+    one_out[...] = one[...]
+    two_out[...] = two[...]
+
+
+def from_columns(values, relay=lambda *v: v):
     peers = lax.axis_size("cols")
     swap = lambda v, n: lax.ppermute(v, "cols", [(i, i ^ n) for i in range(peers)])
-    across = swap(value, 2)
-    return [swap(value, 1), across, swap(relay(across), 1)]
+    across = [swap(v, 2) for v in values]
+    sent_on = relay(*across)
+    return [[swap(v, 1), a, swap(r, 1)] for v, a, r in zip(values, across, sent_on)]
 
 
 def on_device(
@@ -658,7 +660,7 @@
         name="own_part_and_turned_tiles",
         **params(4, ext, ext),
     )(index, place, plan, fine_tiles, a16)
-    basis_pieces = [basis.T] + from_columns(basis.T)
+    basis_pieces = [basis.T] + from_columns([basis.T])[0]
 
     b32, b16, b16_too, mine, mine_rows = pl.pallas_call(
         second_kernel,
@@ -689,16 +691,17 @@
         name="own_part_of_residual",
         **params(4, ext, ext),
     )(index, place, tiles, b16)
-    def relay(value):
+    def relay(one, two):
         return pl.pallas_call(
             relay_kernel,
-            in_specs=[VM, ANY],
-            out_specs=VM,
-            out_shape=shape(value.shape, value.dtype),
+            in_specs=[VM, VM, ANY],
+            out_specs=[VM, VM],
+            out_shape=[shape(one.shape, BF16), shape(two.shape, BF16)],
             name="relay",
             **params(4, ext, ext),
-        )(value, part)
-
+        )(one, two, part)
+
+    mine_pieces, rows_pieces = from_columns([mine, mine_rows], relay)
     from_left, from_right, partner_rows, scale, mid_hot, mid_block = pl.pallas_call(
         sides_kernel,
         in_specs=[SM] + [VM] * 10,
@@ -718,7 +721,7 @@
         name="side_messages",
         **params(4, ext, ext),
     )(
-        place, mine, *from_columns(mine, relay), mine_rows, *from_columns(mine_rows, relay), mid_tiles, owner,
+        place, mine, *mine_pieces, mine_rows, *rows_pieces, mid_tiles, owner,
     )
 
     fres, u, bpart, send = pl.pallas_call(

time: 80.6 us -> 80.6 us (level)
  no operation moved by 1% of the time
where the time goes in v7:
time: 80.6 us; the launch traced here: 80.3 us
  Pallas kernels  24.6 us (31%)
  blocking collectives  24.4 us (30%)
  starting transfers between devices  16.3 us (20%)
  waiting for transfers between devices  13.3 us (17%)
  other arithmetic  0.85 us (1%)
    all_to_all x1, blocking collectives, on_device(): got = lax.all_to_all(send, 'rows', 0, 0)  13.2 us
    all_to_all x1, blocking collectives, finish(): lax.all_to_all(grams, 'rows', 0, 0)  11.2 us
    ppermute x2, waiting for transfers between devices, halo(): near = lax.ppermute(for_partner, 'rows', swap(even))  8.89 us
    ppermute x9, starting transfers between devices, from_columns(): lax.ppermute(v, 'cols', [(i, i ^ n) for i in range(peers)])  6.16 us
    pallas_call x1, Pallas kernels, finish(): pl.pallas_call(last_kernel, in_specs=[SM, SM] + [VM] * 23, out_specs=[HBM...  4.61 us
    pallas_call x1, Pallas kernels, on_device(): pl.pallas_call(third_kernel, in_specs=[SM] * 3 + [VM] * 14, out_specs=[VM...  4.24 us
    ppermute x2, starting transfers between devices, halo(): near = lax.ppermute(for_partner, 'rows', swap(even))  4.13 us
    pallas_call x1, Pallas kernels, on_device(): pl.pallas_call(first_kernel, in_specs=[SM] + [HBM] * 3 + [VM, HBM], out_s...  3.13 us
  transfers between devices with their start and end apart: 18, of which 8 were waited for; matrix products, arithmetic and copies ran while one was open for 1% of the time, Pallas kernels for 15%

profile of v7, /device:TPU:0, one launch (start us, length us, event | category | flops | bytes accessed | tf_op | source)
XLA Modules:
  0.0 80.3 jit_solution(10736022749078896580)
XLA Ops:
  0.6 3.0 %collective-permute-start.3 = (bf16[16,8192]{1,0:T(8,128)(2,1)}, bf16[16,8192]{1,0:T(8,128)(2,1)S(1)}, u32[]{:S(2)}, u32[]{:S(2)}) collective-permute-start(bf16[16,8192]{1,0:T(8,128)(2,1)} %bitcast.9), channel_id=1, source_target_pairs={{0,2},{1,3},{2,0},{3,1},{4,6},{5,7},{6,4},{7,5},{8,10},{9,11},{10,... | collective-permute-start | bytes 786440 | tf_op jit(solution)/shard_map/ppermute | solution.py:591
  3.6 0.1 pad_add_fusion.place
  3.7 0.8 add_bitcast_fusion.owner
  4.5 3.1 %first_smoothing.1 = (bf16[64,16,128]{2,1,0:T(8,128)(2,1)S(1)}, bf16[91,16,128]{2,1,0:T(8,128)(2,1)S(1)}, bf16[75,16,128]{2,1,0:T(8,128)(2,1)S(1)}, f32[64,128]{1,0:T(8,128)S(1)}, f32[64,16,128]{2,1,0:T(8,128)S(1)}) custom-call(s32[3]{0:T(128)S(1)} %pad_add_fusion.place, f32[16,8192]{1,0:T(8,128)} %bitcast.18, bf16[64,4,128,128]{3,2,1,0:T(8,128)(2,1)} %tiles.3, ...), custom_call_target="tpu_custom_call" | custom-call | flops 1048576 | bytes 2097152 | tf_op jit(solution)/shard_map/first_smoothing/pallas_call | solution.py:620
  7.6 1.6 %collective-permute-start = (bf16[91,16,128]{2,1,0:T(8,128)(2,1)S(1)}, bf16[91,16,128]{2,1,0:T(8,128)(2,1)S(1)}, u32[]{:S(2)}, u32[]{:S(2)}) collective-permute-start(bf16[91,16,128]{2,1,0:T(8,128)(2,1)S(1)} %get-tuple-element.42), channel_id=1, source_target_pairs={{0,4},{8,12},{16,20},{24,28},{4,0},{12,8},{20,16},{28,24},{1,5},{9... | collective-permute-start | bytes 1118216 | tf_op jit(solution)/shard_map/ppermute | solution.py:578
  9.2 0.7 collective-permute-start.1
  9.9 0.1 collective-permute-start.2
  10.0 0.2 collective-permute-done.3.basis_c
  10.2 0.3 collective-permute-start.4
  10.5 2.5 %one_hot_rows.1 = (bf16[128,8192]{1,0:T(8,128)(2,1)S(1)}, s32[5,64]{1,0:T(8,128)S(1)}) custom-call(s32[3]{0:T(128)S(1)} %pad_add_fusion.place, s32[4,64]{1,0:T(4,128)S(1)} %bitcast.12, f32[64,128]{1,0:T(8,128)S(1)} %get-tuple-element.38.after.winv, s32[72,128]{1,0:T(8,128)S(1)} %add_bitcast_fusion.owner), custom_call_target="tpu_custom_call" | custom-call | flops 1048576 | bytes 33554432 | tf_op jit(solution)/shard_map/one_hot_rows/pallas_call | solution.py:644
  13.0 3.0 %own_part_and_turned_tiles.1 = (f32[64,16,128]{2,1,0:T(8,128)S(1)}, bf16[64,4,128,128]{3,2,1,0:T(8,128)(2,1)S(1)}) custom-call(s32[4,64]{1,0:T(4,128)S(1)} %bitcast.13, s32[3]{0:T(128)S(1)} %pad_add_fusion.place, s32[5,64]{1,0:T(8,128)S(1)} %get-tuple-element.39.plan, bf16[64,4,128,128]{3,2,1,0:T(8,128)(2,1)S(1)} %copy-done, ...), custom_call_target="tpu_custom_call" | custom-call | flops 128 | bytes 128 | tf_op jit(solution)/shard_map/own_part_and_turned_tiles/pallas_call | solution.py:654
  15.9 0.0 collective-permute-done.2.basis_b
  15.9 0.0 collective-permute-done.1.far
  16.0 7.5 %collective-permute-done.near = bf16[91,16,128]{2,1,0:T(8,128)(2,1)S(1)} collective-permute-done((bf16[91,16,128]{2,1,0:T(8,128)(2,1)S(1)}, bf16[91,16,128]{2,1,0:T(8,128)(2,1)S(1)}, u32[]{:S(2)}, u32[]{:S(2)}) %collective-permute-start) | collective-permute-done | bytes 372768 | tf_op jit(solution)/shard_map/ppermute | solution.py:578
  23.5 0.0 collective-permute-done.4.basis_d
  23.5 1.5 %second_smoothing.1 = (f32[64,16,128]{2,1,0:T(8,128)S(1)}, bf16[64,16,128]{2,1,0:T(8,128)(2,1)S(1)}, bf16[65,16,128]{2,1,0:T(8,128)(2,1)S(1)}, bf16[22,16,128]{2,1,0:T(8,128)(2,1)S(1)}, bf16[16,16,128]{2,1,0:T(8,128)(2,1)S(1)}) custom-call(s32[4,64]{1,0:T(4,128)S(1)} %bitcast.14, s32[5,64]{1,0:T(8,128)S(1)} %get-tuple-element.39.plan, ...), custom_call_target="tpu_custom_call" | custom-call | flops 134217728 | bytes 8388608 | tf_op jit(solution)/shard_map/second_smoothing/pallas_call | solution.py:665
  24.9 2.5 %collective-permute-start.5 = (bf16[65,16,128]{2,1,0:T(8,128)(2,1)S(1)}, bf16[65,16,128]{2,1,0:T(8,128)(2,1)S(1)}, u32[]{:S(2)}, u32[]{:S(2)}) collective-permute-start(bf16[65,16,128]{2,1,0:T(8,128)(2,1)S(1)} %get-tuple-element.47), channel_id=1, source_target_pairs={{0,4},{8,12},{16,20},{24,28},{4,0},{12,8},{20,16},{28,24},{1,5},{9... | collective-permute-start | bytes 798728 | tf_op jit(solution)/shard_map/ppermute | solution.py:578
  27.5 0.7 collective-permute-start.6
  28.2 0.6 collective-permute-start.8
  28.8 1.5 %collective-permute-start.9 = (bf16[16,16,128]{2,1,0:T(8,128)(2,1)S(1)}, bf16[16,16,128]{2,1,0:T(8,128)(2,1)S(1)}, u32[]{:S(2)}, u32[]{:S(2)}) collective-permute-start(bf16[16,16,128]{2,1,0:T(8,128)(2,1)S(1)} %get-tuple-element.50.rows_a), channel_id=1, source_target_pairs={{0,2},{1,3},{2,0},{3,1},{4,6},{5,7},{6,4},{7,5},{8,10},{9,11},{10,... | collective-permute-start | bytes 196616 | tf_op jit(solution)/shard_map/ppermute | solution.py:591
  30.3 1.8 %own_part_of_residual.1.after.part = f32[64,16,128]{2,1,0:T(8,128)S(1)} custom-call(s32[4,64]{1,0:T(4,128)S(1)} %bitcast.15, s32[3]{0:T(128)S(1)} %pad_add_fusion.place, bf16[64,4,128,128]{3,2,1,0:T(8,128)(2,1)S(1)} %get-tuple-element.41.tiles.turned, bf16[64,16,128]{2,1,0:T(8,128)(2,1)S(1)} %get-tuple-element.48.own), custom_call_target="tpu_custom_call" | custom-call | flops 128 | bytes 128 | tf_op jit(solution)/shard_map/own_part_of_residual/pallas_call | solution.py:685
  32.0 1.4 %collective-permute-done.9.two.rows_c = bf16[16,16,128]{2,1,0:T(8,128)(2,1)S(1)} collective-permute-done((bf16[16,16,128]{2,1,0:T(8,128)(2,1)S(1)}, bf16[16,16,128]{2,1,0:T(8,128)(2,1)S(1)}, u32[]{:S(2)}, u32[]{:S(2)}) %collective-permute-start.9) | collective-permute-done | bytes 65568 | tf_op jit(solution)/shard_map/ppermute | solution.py:591
  33.5 0.0 collective-permute-start.7
  33.5 0.0 collective-permute-done.8.one.c
  33.5 0.6 collective-permute-start.10
  34.1 0.0 collective-permute-done.11.rows_b
  34.1 0.1 collective-permute-start.12
  34.1 0.6 collective-permute-done.7.b
  34.8 0.6 collective-permute-done.12.rows_d
  35.3 0.0 collective-permute-done.10.d
  35.3 0.8 %side_messages.1 = (bf16[656,128]{1,0:T(8,128)(2,1)S(1)}, bf16[656,128]{1,0:T(8,128)(2,1)S(1)}, bf16[128,1024]{1,0:T(8,128)(2,1)S(1)}, f32[16,128]{1,0:T(8,128)S...) custom-call(s32[3]{0:T(128)S(1)} %pad_add_fusion.place, bf16[22,16,128]{2,1,0:T(8,128)(2,1)S(1)} %get-tuple-element.49.a, ...), custom_call_target="tpu_custom_call" | custom-call | flops 128 | bytes 128 | tf_op jit(solution)/shard_map/side_messages/pallas_call | solution.py:705
  36.2 1.4 %collective-permute-done.5.near = bf16[65,16,128]{2,1,0:T(8,128)(2,1)S(1)} collective-permute-done((bf16[65,16,128]{2,1,0:T(8,128)(2,1)S(1)}, bf16[65,16,128]{2,1,0:T(8,128)(2,1)S(1)}, u32[]{:S(2)}, u32[]{:S(2)}) %collective-permute-start.5) | collective-permute-done | bytes 266272 | tf_op jit(solution)/shard_map/ppermute | solution.py:578
  37.6 4.2 %residual_and_restriction.1 = (f32[64,16,128]{2,1,0:T(8,128)S(1)}, f32[8,16,128]{2,1,0:T(8,128)S(1)}, f32[8,16,128]{2,1,0:T(8,128)S(1)}, bf16[8,5,16,128]{3,2,1,0:T(8,128)(2,1)S(1)}) custom-call(s32[4,64]{1,0:T(4,128)S(1)} %bitcast.16, s32[5,64]{1,0:T(8,128)S(1)} %get-tuple-element.39.plan, s32[3]{0:T(128)S(1)} %pad_add_fusion.place, ...), custom_call_target="tpu_custom_call" | custom-call | flops 134217728 | bytes 8388608 | tf_op jit(solution)/shard_map/residual_and_restriction/pallas_call | solution.py:727
  41.8 13.2 %all_to_all.10.got = bf16[8,5,16,128]{3,2,1,0:T(8,128)(2,1)S(1)} all-to-all(bf16[8,5,16,128]{3,2,1,0:T(8,128)(2,1)S(1)} %get-tuple-element.58), channel_id=1, replica_groups=mesh['rows'=8,'cols'=4] {'rows'}, dimensions={0} | all-to-all | bytes 327680 | tf_op jit(solution)/shard_map/all_to_all | solution.py:748
  55.0 1.2 %coarse_and_mid_level.1 = (f32[8,16,128]{2,1,0:T(8,128)S(1)}, bf16[2,16,128]{2,1,0:T(8,128)(2,1)S(1)}, bf16[9,16,128]{2,1,0:T(8,128)(2,1)S(1)}, bf16[9,16,128]{2...) custom-call(s32[3]{0:T(128)S(1)} %pad_add_fusion.place, ...), custom_call_target="tpu_custom_call" | custom-call | flops 8388608 | bytes 524288 | tf_op jit(solution)/shard_map/coarse_and_mid_level/pallas_call | solution.py:749
  56.3 0.4 collective-permute-start.13
  56.6 1.0 %collective-permute-start.15 = (bf16[9,16,128]{2,1,0:T(8,128)(2,1)S(1)}, bf16[9,16,128]{2,1,0:T(8,128)(2,1)S(1)}, u32[]{:S(2)}, u32[]{:S(2)}) collective-permute-start(bf16[9,16,128]{2,1,0:T(8,128)(2,1)S(1)} %get-tuple-element.63), channel_id=1, source_target_pairs={{0,12},{4,8},{8,4},{12,0},{16,28},{20,24},{24,20},{28,16},{1,13},{... | collective-permute-start | bytes 110600 | tf_op jit(solution)/shard_map/ppermute | solution.py:783
  57.7 1.5 %collective-permute-start.14 = (bf16[9,16,128]{2,1,0:T(8,128)(2,1)S(1)}, bf16[9,16,128]{2,1,0:T(8,128)(2,1)S(1)}, u32[]{:S(2)}, u32[]{:S(2)}) collective-permute-start(bf16[9,16,128]{2,1,0:T(8,128)(2,1)S(1)} %get-tuple-element.63), channel_id=1, source_target_pairs={{12,16},{8,20},{0,4},{24,28},{16,12},{20,8},{4,0},{28,24},{13,17},... | collective-permute-start | bytes 110600 | tf_op jit(solution)/shard_map/ppermute | solution.py:782
  59.1 1.0 %collective-permute-start.16 = (bf16[16,128]{1,0:T(8,128)(2,1)S(1)}, bf16[16,128]{1,0:T(8,128)(2,1)S(1)}, u32[]{:S(2)}, u32[]{:S(2)}) collective-permute-start(bf16[16,128]{1,0:T(8,128)(2,1)S(1)} %get-tuple-element.64), channel_id=1, source_target_pairs={{0,8},{4,12},{8,0},{12,4},{16,24},{20,28},{24,16},{28,20},{1,9},{5... | collective-permute-start | bytes 12296 | tf_op jit(solution)/shard_map/ppermute | solution.py:783
  60.1 0.8 %collective-permute-start.17 = (bf16[16,128]{1,0:T(8,128)(2,1)S(1)}, bf16[16,128]{1,0:T(8,128)(2,1)S(1)}, u32[]{:S(2)}, u32[]{:S(2)}) collective-permute-start(bf16[16,128]{1,0:T(8,128)(2,1)S(1)} %get-tuple-element.65), channel_id=1, source_target_pairs={{8,16},{12,20},{0,4},{24,28},{16,8},{20,12},{4,0},{28,24},{9,17},{... | collective-permute-start | bytes 12296 | tf_op jit(solution)/shard_map/ppermute | solution.py:782
  61.0 1.1 %side_one_hot_rows.1 = (bf16[128,8192]{1,0:T(8,128)(2,1)S(1)}, bf16[128,8192]{1,0:T(8,128)(2,1)S(1)}) custom-call(bf16[2,16,128]{2,1,0:T(8,128)(2,1)S(1)} %get-tuple-element.67.after.c_edges, bf16[656,128]{1,0:T(8,128)(2,1)S(1)} %get-tuple-element.53.from_left, bf16[656,128]{1,0:T(8,128)(2,1)S(1)} %get-tuple-element.54.from_right), custom_call_target="tpu_custom_call" | custom-call | flops 128 | bytes 128 | tf_op jit(solution)/shard_map/side_one_hot_rows/pallas_call | solution.py:791
  62.1 0.7 collective-permute-done.16.nexts
  62.7 1.0 %collective-permute-done.17.beyond = bf16[16,128]{1,0:T(8,128)(2,1)S(1)} collective-permute-done((bf16[16,128]{1,0:T(8,128)(2,1)S(1)}, bf16[16,128]{1,0:T(8,128)(2,1)S(1)}, u32[]{:S(2)}, u32[]{:S(2)}) %collective-permute-start.17) | collective-permute-done | bytes 4128 | tf_op jit(solution)/shard_map/ppermute | solution.py:782
  63.8 0.0 collective-permute-done.15.other
  63.8 0.0 collective-permute-done.14.far
  63.8 4.6 %prolongation_and_last_smoothing.1 = (f32[16,8192]{1,0:T(8,128)}, f32[8,8,128]{2,1,0:T(8,128)S(1)}) custom-call(s32[4,64]{1,0:T(4,128)S(1)} %bitcast.17, s32[3]{0:T(128)S(1)} %pad_add_fusion.place, bf16[64,4,128,128]{3,2,1,0:T(8,128)(2,1)S(1)} %get-tuple-element.41.tiles.turned, bf16[9,16,128]{2,1,0:T(8,128)(2,1)S(1)} %collective-permute-done.13.near, ...), custom_call_target="tpu_custom_call" | custom-call | flops 134217728 | bytes 8388608 | tf_op jit(solution)/shard_map/prolongation_and_last_smoothing/pallas_call | solution.py:799
  68.4 11.2 %all_to_all.11.got = f32[8,8,128]{2,1,0:T(8,128)S(1)} all-to-all(f32[8,8,128]{2,1,0:T(8,128)S(1)} %get-tuple-element.73), channel_id=1, replica_groups=mesh['rows'=8,'cols'=4] {'rows'}, dimensions={0} | all-to-all | bytes 65536 | tf_op jit(solution)/shard_map/all_to_all | solution.py:828
  79.6 0.7 gram_sum.1
  (14 shorter events, 0.0 us)
Async XLA Ops:
  0.6 9.5 %collective-permute-start.3 = (bf16[16,8192]{1,0:T(8,128)(2,1)}, bf16[16,8192]{1,0:T(8,128)(2,1)S(1)}, u32[]{:S(2)}, u32[]{:S(2)}) collective-permute-start(bf16[16,8192]{1,0:T(8,128)(2,1)} %bitcast.9), channel_id=1, source_target_pairs={{0,2},{1,3},{2,0},{3,1},{4,6},{5,7},{6,4},{7,5},{8,10},{9,11},{10,... | collective-permute-start | bytes 786440 | tf_op jit(solution)/shard_map/ppermute | solution.py:591
  4.5 5.4 %copy-start.3 = (bf16[8192,16]{0,1:T(8,128)(2,1)S(1)}, bf16[8192,16]{0,1:T(8,128)(2,1)}, u32[]{:S(2)}) copy-start(bf16[8192,16]{0,1:T(8,128)(2,1)} %param.9) | copy-start | bytes 786436
  4.5 6.0 %copy-start.4 = (s32[64,4]{0,1:T(4,128)S(1)}, s32[64,4]{0,1:T(4,128)}, u32[]{:S(2)}) copy-start(s32[64,4]{0,1:T(4,128)} %param.11) | copy-start | bytes 3076
  4.5 8.5 %copy-start = (bf16[64,4,128,128]{3,2,1,0:T(8,128)(2,1)S(1)}, bf16[64,4,128,128]{3,2,1,0:T(8,128)(2,1)}, u32[]{:S(2)}) copy-start(bf16[64,4,128,128]{3,2,1,0:T(8,128)(2,1)} %tiles.3) | copy-start | bytes 25165828
  7.6 15.8 %collective-permute-start = (bf16[91,16,128]{2,1,0:T(8,128)(2,1)S(1)}, bf16[91,16,128]{2,1,0:T(8,128)(2,1)S(1)}, u32[]{:S(2)}, u32[]{:S(2)}) collective-permute-start(bf16[91,16,128]{2,1,0:T(8,128)(2,1)S(1)} %get-tuple-element.42), channel_id=1, source_target_pairs={{0,4},{8,12},{16,20},{24,28},{4,0},{12,8},{20,16},{28,24},{1,5},{9... | collective-permute-start | bytes 1118216 | tf_op jit(solution)/shard_map/ppermute | solution.py:578
  9.2 6.7 %collective-permute-start.1 = (bf16[75,16,128]{2,1,0:T(8,128)(2,1)S(1)}, bf16[75,16,128]{2,1,0:T(8,128)(2,1)S(1)}, u32[]{:S(2)}, u32[]{:S(2)}) collective-permute-start(bf16[75,16,128]{2,1,0:T(8,128)(2,1)S(1)} %get-tuple-element.43), channel_id=1, source_target_pairs={{4,8},{12,16},{20,24},{8,4},{16,12},{24,20},{5,9},{13,17},{21,25},... | collective-permute-start | bytes 921608 | tf_op jit(solution)/shard_map/ppermute | solution.py:579
  9.9 6.0 %collective-permute-start.2 = (bf16[16,8192]{1,0:T(8,128)(2,1)S(1)}, bf16[16,8192]{1,0:T(8,128)(2,1)S(1)}, u32[]{:S(2)}, u32[]{:S(2)}) collective-permute-start(bf16[16,8192]{1,0:T(8,128)(2,1)S(1)} %bitcast.10), channel_id=1, source_target_pairs={{0,1},{1,0},{2,3},{3,2},{4,5},{5,4},{6,7},{7,6},{8,9},{9,8},{10,11... | collective-permute-start | bytes 786440 | tf_op jit(solution)/shard_map/ppermute | solution.py:591
  10.2 13.3 %collective-permute-start.4 = (bf16[16,8192]{1,0:T(8,128)(2,1)S(1)}, bf16[16,8192]{1,0:T(8,128)(2,1)S(1)}, u32[]{:S(2)}, u32[]{:S(2)}) collective-permute-start(bf16[16,8192]{1,0:T(8,128)(2,1)S(1)} %collective-permute-done.3.basis_c), channel_id=1, source_target_pairs={{0,1},{1,0},{2,3},{3,2},{4,5},{5,4},{6,7},{7,6},{8,9},{9,8},{10,11... | collective-permute-start | bytes 786440 | tf_op jit(solution)/shard_map/ppermute | solution.py:591
  24.9 12.6 %collective-permute-start.5 = (bf16[65,16,128]{2,1,0:T(8,128)(2,1)S(1)}, bf16[65,16,128]{2,1,0:T(8,128)(2,1)S(1)}, u32[]{:S(2)}, u32[]{:S(2)}) collective-permute-start(bf16[65,16,128]{2,1,0:T(8,128)(2,1)S(1)} %get-tuple-element.47), channel_id=1, source_target_pairs={{0,4},{8,12},{16,20},{24,28},{4,0},{12,8},{20,16},{28,24},{1,5},{9... | collective-permute-start | bytes 798728 | tf_op jit(solution)/shard_map/ppermute | solution.py:578
  27.5 8.7 %collective-permute-start.6 = (bf16[64,16,128]{2,1,0:T(8,128)(2,1)S(1)}, bf16[64,16,128]{2,1,0:T(8,128)(2,1)S(1)}, u32[]{:S(2)}, u32[]{:S(2)}) collective-permute-start(bf16[64,16,128]{2,1,0:T(8,128)(2,1)S(1)} %get-tuple-element.48.own), channel_id=1, source_target_pairs={{4,8},{12,16},{20,24},{8,4},{16,12},{24,20},{5,9},{13,17},{21,25},... | collective-permute-start | bytes 786440 | tf_op jit(solution)/shard_map/ppermute | solution.py:579
  28.2 5.3 %collective-permute-start.8 = (bf16[22,16,128]{2,1,0:T(8,128)(2,1)S(1)}, bf16[22,16,128]{2,1,0:T(8,128)(2,1)S(1)}, u32[]{:S(2)}, u32[]{:S(2)}) collective-permute-start(bf16[22,16,128]{2,1,0:T(8,128)(2,1)S(1)} %get-tuple-element.49.a), channel_id=1, source_target_pairs={{0,2},{1,3},{2,0},{3,1},{4,6},{5,7},{6,4},{7,5},{8,10},{9,11},{10,... | collective-permute-start | bytes 270344 | tf_op jit(solution)/shard_map/ppermute | solution.py:591
  28.8 6.6 %copy-start.1 = (bf16[8,3,128,128]{3,2,1,0:T(8,128)(2,1)S(1)}, bf16[8,3,128,128]{3,2,1,0:T(8,128)(2,1)}, u32[]{:S(2)}) copy-start(bf16[8,3,128,128]{3,2,1,0:T(8,128)(2,1)} %mid_tiles.9) | copy-start | bytes 2359300
  28.8 4.7 %collective-permute-start.9 = (bf16[16,16,128]{2,1,0:T(8,128)(2,1)S(1)}, bf16[16,16,128]{2,1,0:T(8,128)(2,1)S(1)}, u32[]{:S(2)}, u32[]{:S(2)}) collective-permute-start(bf16[16,16,128]{2,1,0:T(8,128)(2,1)S(1)} %get-tuple-element.50.rows_a), channel_id=1, source_target_pairs={{0,2},{1,3},{2,0},{3,1},{4,6},{5,7},{6,4},{7,5},{8,10},{9,11},{10,... | collective-permute-start | bytes 196616 | tf_op jit(solution)/shard_map/ppermute | solution.py:591
  30.3 3.8 %collective-permute-start.11 = (bf16[16,16,128]{2,1,0:T(8,128)(2,1)S(1)}, bf16[16,16,128]{2,1,0:T(8,128)(2,1)S(1)}, u32[]{:S(2)}, u32[]{:S(2)}) collective-permute-start(bf16[16,16,128]{2,1,0:T(8,128)(2,1)S(1)} %get-tuple-element.50.rows_a), channel_id=1, source_target_pairs={{0,1},{1,0},{2,3},{3,2},{4,5},{5,4},{6,7},{7,6},{8,9},{9,8},{10,11... | collective-permute-start | bytes 196616 | tf_op jit(solution)/shard_map/ppermute | solution.py:591
  33.5 1.3 %collective-permute-start.7 = (bf16[22,16,128]{2,1,0:T(8,128)(2,1)S(1)}, bf16[22,16,128]{2,1,0:T(8,128)(2,1)S(1)}, u32[]{:S(2)}, u32[]{:S(2)}) collective-permute-start(bf16[22,16,128]{2,1,0:T(8,128)(2,1)S(1)} %get-tuple-element.49.a), channel_id=1, source_target_pairs={{0,1},{1,0},{2,3},{3,2},{4,5},{5,4},{6,7},{7,6},{8,9},{9,8},{10,11... | collective-permute-start | bytes 270344 | tf_op jit(solution)/shard_map/ppermute | solution.py:591
  33.5 1.8 %collective-permute-start.10 = (bf16[22,16,128]{2,1,0:T(8,128)(2,1)S(1)}, bf16[22,16,128]{2,1,0:T(8,128)(2,1)S(1)}, u32[]{:S(2)}, u32[]{:S(2)}) collective-permute-start(bf16[22,16,128]{2,1,0:T(8,128)(2,1)S(1)} %get-tuple-element.51), channel_id=1, source_target_pairs={{0,1},{1,0},{2,3},{3,2},{4,5},{5,4},{6,7},{7,6},{8,9},{9,8},{10,11... | collective-permute-start | bytes 270344 | tf_op jit(solution)/shard_map/ppermute | solution.py:591
  34.1 1.3 %collective-permute-start.12 = (bf16[16,16,128]{2,1,0:T(8,128)(2,1)S(1)}, bf16[16,16,128]{2,1,0:T(8,128)(2,1)S(1)}, u32[]{:S(2)}, u32[]{:S(2)}) collective-permute-start(bf16[16,16,128]{2,1,0:T(8,128)(2,1)S(1)} %get-tuple-element.52), channel_id=1, source_target_pairs={{0,1},{1,0},{2,3},{3,2},{4,5},{5,4},{6,7},{7,6},{8,9},{9,8},{10,11... | collective-permute-start | bytes 196616 | tf_op jit(solution)/shard_map/ppermute | solution.py:591
  37.6 17.5 %copy-start.2 = (f32[128,1024]{1,0:T(8,128)S(1)}, f32[128,1024]{1,0:T(8,128)}, u32[]{:S(2)}) copy-start(f32[128,1024]{1,0:T(8,128)} %inverse_rows.3) | copy-start | bytes 1572868
  56.3 7.5 %collective-permute-start.13 = (bf16[9,16,128]{2,1,0:T(8,128)(2,1)S(1)}, bf16[9,16,128]{2,1,0:T(8,128)(2,1)S(1)}, u32[]{:S(2)}, u32[]{:S(2)}) collective-permute-start(bf16[9,16,128]{2,1,0:T(8,128)(2,1)S(1)} %get-tuple-element.62), channel_id=1, source_target_pairs={{0,4},{4,0},{8,12},{12,8},{16,20},{20,16},{24,28},{28,24},{1,5},{5... | collective-permute-start | bytes 110600 | tf_op jit(solution)/shard_map/ppermute | solution.py:783
  56.6 7.1 %collective-permute-start.15 = (bf16[9,16,128]{2,1,0:T(8,128)(2,1)S(1)}, bf16[9,16,128]{2,1,0:T(8,128)(2,1)S(1)}, u32[]{:S(2)}, u32[]{:S(2)}) collective-permute-start(bf16[9,16,128]{2,1,0:T(8,128)(2,1)S(1)} %get-tuple-element.63), channel_id=1, source_target_pairs={{0,12},{4,8},{8,4},{12,0},{16,28},{20,24},{24,20},{28,16},{1,13},{... | collective-permute-start | bytes 110600 | tf_op jit(solution)/shard_map/ppermute | solution.py:783
  57.7 6.1 %collective-permute-start.14 = (bf16[9,16,128]{2,1,0:T(8,128)(2,1)S(1)}, bf16[9,16,128]{2,1,0:T(8,128)(2,1)S(1)}, u32[]{:S(2)}, u32[]{:S(2)}) collective-permute-start(bf16[9,16,128]{2,1,0:T(8,128)(2,1)S(1)} %get-tuple-element.63), channel_id=1, source_target_pairs={{12,16},{8,20},{0,4},{24,28},{16,12},{20,8},{4,0},{28,24},{13,17},... | collective-permute-start | bytes 110600 | tf_op jit(solution)/shard_map/ppermute | solution.py:782
  59.1 3.6 %collective-permute-start.16 = (bf16[16,128]{1,0:T(8,128)(2,1)S(1)}, bf16[16,128]{1,0:T(8,128)(2,1)S(1)}, u32[]{:S(2)}, u32[]{:S(2)}) collective-permute-start(bf16[16,128]{1,0:T(8,128)(2,1)S(1)} %get-tuple-element.64), channel_id=1, source_target_pairs={{0,8},{4,12},{8,0},{12,4},{16,24},{20,28},{24,16},{28,20},{1,9},{5... | collective-permute-start | bytes 12296 | tf_op jit(solution)/shard_map/ppermute | solution.py:783
  60.1 3.6 %collective-permute-start.17 = (bf16[16,128]{1,0:T(8,128)(2,1)S(1)}, bf16[16,128]{1,0:T(8,128)(2,1)S(1)}, u32[]{:S(2)}, u32[]{:S(2)}) collective-permute-start(bf16[16,128]{1,0:T(8,128)(2,1)S(1)} %get-tuple-element.65), channel_id=1, source_target_pairs={{8,16},{12,20},{0,4},{24,28},{16,8},{20,12},{4,0},{28,24},{9,17},{... | collective-permute-start | bytes 12296 | tf_op jit(solution)/shard_map/ppermute | solution.py:782

commit v8 on v7

--- a/solution.py
+++ b/solution.py
@@ -580,18 +580,20 @@
     return near, far
 
 
-def relay_kernel(one, two, after, one_out, two_out):
+def relay_kernel(after, *refs):
     del after
-    one_out[...] = one[...]
-    two_out[...] = two[...]
+    half = len(refs) // 2
+    for value, out in zip(refs[:half], refs[half:]):
+        out[...] = value[...]
 
 
 def from_columns(values, relay=lambda *v: v):
     peers = lax.axis_size("cols")
     swap = lambda v, n: lax.ppermute(v, "cols", [(i, i ^ n) for i in range(peers)])
     across = [swap(v, 2) for v in values]
-    sent_on = relay(*across)
-    return [[swap(v, 1), a, swap(r, 1)] for v, a, r in zip(values, across, sent_on)]
+    count = len(values)
+    held = relay(*values, *across)
+    return [[swap(held[n], 1), across[n], swap(held[count + n], 1)] for n in range(count)]
 
 
 def on_device(
@@ -691,15 +693,15 @@
         name="own_part_of_residual",
         **params(4, ext, ext),
     )(index, place, tiles, b16)
-    def relay(one, two):
+    def relay(*values):
         return pl.pallas_call(
             relay_kernel,
-            in_specs=[VM, VM, ANY],
-            out_specs=[VM, VM],
-            out_shape=[shape(one.shape, BF16), shape(two.shape, BF16)],
+            in_specs=[ANY] + [VM] * len(values),
+            out_specs=[VM] * len(values),
+            out_shape=[shape(v.shape, BF16) for v in values],
             name="relay",
             **params(4, ext, ext),
-        )(one, two, part)
+        )(part, *values)
 
     mine_pieces, rows_pieces = from_columns([mine, mine_rows], relay)
     from_left, from_right, partner_rows, scale, mid_hot, mid_block = pl.pallas_call(

time: 80.6 us -> 80.9 us (level)
  no operation moved by 1% of the time
where the time goes in v8:
time: 80.9 us; the launch traced here: 80.6 us
  Pallas kernels  24.6 us (30%)
  blocking collectives  24.4 us (30%)
  starting transfers between devices  16.7 us (21%)
  waiting for transfers between devices  13.4 us (17%)
  other arithmetic  0.85 us (1%)
    all_to_all x1, blocking collectives, on_device(): got = lax.all_to_all(send, 'rows', 0, 0)  13.5 us
    all_to_all x1, blocking collectives, finish(): lax.all_to_all(grams, 'rows', 0, 0)  10.8 us
    ppermute x2, waiting for transfers between devices, halo(): near = lax.ppermute(for_partner, 'rows', swap(even))  8.13 us
    ppermute x9, starting transfers between devices, from_columns(): lax.ppermute(v, 'cols', [(i, i ^ n) for i in range(peers)])  6.3 us
    pallas_call x1, Pallas kernels, finish(): pl.pallas_call(last_kernel, in_specs=[SM, SM] + [VM] * 23, out_specs=[HBM...  4.61 us
    pallas_call x1, Pallas kernels, on_device(): pl.pallas_call(third_kernel, in_specs=[SM] * 3 + [VM] * 14, out_specs=[VM...  4.24 us
    ppermute x2, starting transfers between devices, halo(): near = lax.ppermute(for_partner, 'rows', swap(even))  4.13 us
    ppermute x9, waiting for transfers between devices, from_columns(): lax.ppermute(v, 'cols', [(i, i ^ n) for i in range(peers)])  3.36 us
  transfers between devices with their start and end apart: 18, of which 8 were waited for; matrix products, arithmetic and copies ran while one was open for 1% of the time, Pallas kernels for 15%

profile of v8, /device:TPU:0, one launch (start us, length us, event | category | flops | bytes accessed | tf_op | source)
XLA Modules:
  0.0 80.6 jit_solution(10545000019966433901)
XLA Ops:
  0.6 3.0 %collective-permute-start.3 = (bf16[16,8192]{1,0:T(8,128)(2,1)}, bf16[16,8192]{1,0:T(8,128)(2,1)S(1)}, u32[]{:S(2)}, u32[]{:S(2)}) collective-permute-start(bf16[16,8192]{1,0:T(8,128)(2,1)} %bitcast.9), channel_id=1, source_target_pairs={{0,2},{1,3},{2,0},{3,1},{4,6},{5,7},{6,4},{7,5},{8,10},{9,11},{10,... | collective-permute-start | bytes 786440 | tf_op jit(solution)/shard_map/ppermute | solution.py:592
  3.6 0.1 pad_add_fusion.place
  3.7 0.8 add_bitcast_fusion.owner
  4.5 3.1 %first_smoothing.1 = (bf16[64,16,128]{2,1,0:T(8,128)(2,1)S(1)}, bf16[91,16,128]{2,1,0:T(8,128)(2,1)S(1)}, bf16[75,16,128]{2,1,0:T(8,128)(2,1)S(1)}, f32[64,128]{1,0:T(8,128)S(1)}, f32[64,16,128]{2,1,0:T(8,128)S(1)}) custom-call(s32[3]{0:T(128)S(1)} %pad_add_fusion.place, f32[16,8192]{1,0:T(8,128)} %bitcast.18, bf16[64,4,128,128]{3,2,1,0:T(8,128)(2,1)} %tiles.3, ...), custom_call_target="tpu_custom_call" | custom-call | flops 1048576 | bytes 2097152 | tf_op jit(solution)/shard_map/first_smoothing/pallas_call | solution.py:622
  7.6 1.6 %collective-permute-start = (bf16[91,16,128]{2,1,0:T(8,128)(2,1)S(1)}, bf16[91,16,128]{2,1,0:T(8,128)(2,1)S(1)}, u32[]{:S(2)}, u32[]{:S(2)}) collective-permute-start(bf16[91,16,128]{2,1,0:T(8,128)(2,1)S(1)} %get-tuple-element.44), channel_id=1, source_target_pairs={{0,4},{8,12},{16,20},{24,28},{4,0},{12,8},{20,16},{28,24},{1,5},{9... | collective-permute-start | bytes 1118216 | tf_op jit(solution)/shard_map/ppermute | solution.py:578
  9.2 0.7 collective-permute-start.1
  9.9 0.1 collective-permute-start.2
  10.0 0.2 collective-permute-done.3.basis_c
  10.2 0.3 collective-permute-start.4
  10.5 2.5 %one_hot_rows.1 = (bf16[128,8192]{1,0:T(8,128)(2,1)S(1)}, s32[5,64]{1,0:T(8,128)S(1)}) custom-call(s32[3]{0:T(128)S(1)} %pad_add_fusion.place, s32[4,64]{1,0:T(4,128)S(1)} %bitcast.12, f32[64,128]{1,0:T(8,128)S(1)} %get-tuple-element.40.after.winv, s32[72,128]{1,0:T(8,128)S(1)} %add_bitcast_fusion.owner), custom_call_target="tpu_custom_call" | custom-call | flops 1048576 | bytes 33554432 | tf_op jit(solution)/shard_map/one_hot_rows/pallas_call | solution.py:646
  13.0 3.0 %own_part_and_turned_tiles.1 = (f32[64,16,128]{2,1,0:T(8,128)S(1)}, bf16[64,4,128,128]{3,2,1,0:T(8,128)(2,1)S(1)}) custom-call(s32[4,64]{1,0:T(4,128)S(1)} %bitcast.13, s32[3]{0:T(128)S(1)} %pad_add_fusion.place, s32[5,64]{1,0:T(8,128)S(1)} %get-tuple-element.41.plan, bf16[64,4,128,128]{3,2,1,0:T(8,128)(2,1)S(1)} %copy-done, ...), custom_call_target="tpu_custom_call" | custom-call | flops 128 | bytes 128 | tf_op jit(solution)/shard_map/own_part_and_turned_tiles/pallas_call | solution.py:656
  15.9 0.0 collective-permute-done.2.basis_b
  15.9 0.0 collective-permute-done.1.far
  16.0 7.5 %collective-permute-done.near = bf16[91,16,128]{2,1,0:T(8,128)(2,1)S(1)} collective-permute-done((bf16[91,16,128]{2,1,0:T(8,128)(2,1)S(1)}, bf16[91,16,128]{2,1,0:T(8,128)(2,1)S(1)}, u32[]{:S(2)}, u32[]{:S(2)}) %collective-permute-start) | collective-permute-done | bytes 372768 | tf_op jit(solution)/shard_map/ppermute | solution.py:578
  23.5 0.0 collective-permute-done.4.basis_d
  23.5 1.5 %second_smoothing.1 = (f32[64,16,128]{2,1,0:T(8,128)S(1)}, bf16[64,16,128]{2,1,0:T(8,128)(2,1)S(1)}, bf16[65,16,128]{2,1,0:T(8,128)(2,1)S(1)}, bf16[22,16,128]{2,1,0:T(8,128)(2,1)S(1)}, bf16[16,16,128]{2,1,0:T(8,128)(2,1)S(1)}) custom-call(s32[4,64]{1,0:T(4,128)S(1)} %bitcast.14, s32[5,64]{1,0:T(8,128)S(1)} %get-tuple-element.41.plan, ...), custom_call_target="tpu_custom_call" | custom-call | flops 134217728 | bytes 8388608 | tf_op jit(solution)/shard_map/second_smoothing/pallas_call | solution.py:667
  24.9 2.5 %collective-permute-start.5 = (bf16[65,16,128]{2,1,0:T(8,128)(2,1)S(1)}, bf16[65,16,128]{2,1,0:T(8,128)(2,1)S(1)}, u32[]{:S(2)}, u32[]{:S(2)}) collective-permute-start(bf16[65,16,128]{2,1,0:T(8,128)(2,1)S(1)} %get-tuple-element.49), channel_id=1, source_target_pairs={{0,4},{8,12},{16,20},{24,28},{4,0},{12,8},{20,16},{28,24},{1,5},{9... | collective-permute-start | bytes 798728 | tf_op jit(solution)/shard_map/ppermute | solution.py:578
  27.5 0.7 collective-permute-start.6
  28.2 0.6 collective-permute-start.7
  28.8 1.5 %collective-permute-start.8 = (bf16[16,16,128]{2,1,0:T(8,128)(2,1)S(1)}, bf16[16,16,128]{2,1,0:T(8,128)(2,1)S(1)}, u32[]{:S(2)}, u32[]{:S(2)}) collective-permute-start(bf16[16,16,128]{2,1,0:T(8,128)(2,1)S(1)} %get-tuple-element.52.refs_1_.rows_a), channel_id=1, source_target_pairs={{0,2},{1,3},{2,0},{3,1},{4,6},{5,7},{6,4},{7,5},{8,10},{9,11},{10,... | collective-permute-start | bytes 196616 | tf_op jit(solution)/shard_map/ppermute | solution.py:592
  30.3 1.8 %own_part_of_residual.1.after.part = f32[64,16,128]{2,1,0:T(8,128)S(1)} custom-call(s32[4,64]{1,0:T(4,128)S(1)} %bitcast.15, s32[3]{0:T(128)S(1)} %pad_add_fusion.place, bf16[64,4,128,128]{3,2,1,0:T(8,128)(2,1)S(1)} %get-tuple-element.43.tiles.turned, bf16[64,16,128]{2,1,0:T(8,128)(2,1)S(1)} %get-tuple-element.50.own), custom_call_target="tpu_custom_call" | custom-call | flops 128 | bytes 128 | tf_op jit(solution)/shard_map/own_part_of_residual/pallas_call | solution.py:687
  32.0 1.4 %collective-permute-done.8.refs_3_.rows_c = bf16[16,16,128]{2,1,0:T(8,128)(2,1)S(1)} collective-permute-done((bf16[16,16,128]{2,1,0:T(8,128)(2,1)S(1)}, bf16[16,16,128]{2,1,0:T(8,128)(2,1)S(1)}, u32[]{:S(2)}, u32[]{:S(2)}) %collective-permute-start.8) | collective-permute-done | bytes 65568 | tf_op jit(solution)/shard_map/ppermute | solution.py:592
  33.5 0.0 collective-permute-done.7.refs_2_.c
  33.5 0.1 collective-permute-start.11
  33.6 0.5 collective-permute-start.9
  34.1 0.1 collective-permute-start.10
  34.1 0.7 collective-permute-done.11.rows_b
  34.8 0.2 collective-permute-start.12
  35.0 1.1 %collective-permute-done.12.rows_d = bf16[16,16,128]{2,1,0:T(8,128)(2,1)S(1)} collective-permute-done((bf16[16,16,128]{2,1,0:T(8,128)(2,1)S(1)}, bf16[16,16,128]{2,1,0:T(8,128)(2,1)S(1)}, u32[]{:S(2)}, u32[]{:S(2)}) %collective-permute-start.12) | collective-permute-done | bytes 65568 | tf_op jit(solution)/shard_map/ppermute | solution.py:592
  36.1 0.0 collective-permute-done.9.b
  36.1 0.0 collective-permute-done.10.d
  36.1 0.8 %side_messages.1 = (bf16[656,128]{1,0:T(8,128)(2,1)S(1)}, bf16[656,128]{1,0:T(8,128)(2,1)S(1)}, bf16[128,1024]{1,0:T(8,128)(2,1)S(1)}, f32[16,128]{1,0:T(8,128)S...) custom-call(s32[3]{0:T(128)S(1)} %pad_add_fusion.place, bf16[22,16,128]{2,1,0:T(8,128)(2,1)S(1)} %get-tuple-element.51.refs_0_.a, ...), custom_call_target="tpu_custom_call" | custom-call | flops 128 | bytes 128 | tf_op jit(solution)/shard_map/side_messages/pallas_call | solution.py:707
  36.9 0.0 collective-permute-done.6.far
  36.9 0.6 collective-permute-done.5.near
  37.6 4.2 %residual_and_restriction.1 = (f32[64,16,128]{2,1,0:T(8,128)S(1)}, f32[8,16,128]{2,1,0:T(8,128)S(1)}, f32[8,16,128]{2,1,0:T(8,128)S(1)}, bf16[8,5,16,128]{3,2,1,0:T(8,128)(2,1)S(1)}) custom-call(s32[4,64]{1,0:T(4,128)S(1)} %bitcast.16, s32[5,64]{1,0:T(8,128)S(1)} %get-tuple-element.41.plan, s32[3]{0:T(128)S(1)} %pad_add_fusion.place, ...), custom_call_target="tpu_custom_call" | custom-call | flops 134217728 | bytes 8388608 | tf_op jit(solution)/shard_map/residual_and_restriction/pallas_call | solution.py:729
  41.8 13.5 %all_to_all.10.got = bf16[8,5,16,128]{3,2,1,0:T(8,128)(2,1)S(1)} all-to-all(bf16[8,5,16,128]{3,2,1,0:T(8,128)(2,1)S(1)} %get-tuple-element.62), channel_id=1, replica_groups=mesh['rows'=8,'cols'=4] {'rows'}, dimensions={0} | all-to-all | bytes 327680 | tf_op jit(solution)/shard_map/all_to_all | solution.py:750
  55.4 1.2 %coarse_and_mid_level.1 = (f32[8,16,128]{2,1,0:T(8,128)S(1)}, bf16[2,16,128]{2,1,0:T(8,128)(2,1)S(1)}, bf16[9,16,128]{2,1,0:T(8,128)(2,1)S(1)}, bf16[9,16,128]{2...) custom-call(s32[3]{0:T(128)S(1)} %pad_add_fusion.place, ...), custom_call_target="tpu_custom_call" | custom-call | flops 8388608 | bytes 524288 | tf_op jit(solution)/shard_map/coarse_and_mid_level/pallas_call | solution.py:751
  56.6 0.4 collective-permute-start.13
  57.0 1.0 %collective-permute-start.15 = (bf16[9,16,128]{2,1,0:T(8,128)(2,1)S(1)}, bf16[9,16,128]{2,1,0:T(8,128)(2,1)S(1)}, u32[]{:S(2)}, u32[]{:S(2)}) collective-permute-start(bf16[9,16,128]{2,1,0:T(8,128)(2,1)S(1)} %get-tuple-element.67), channel_id=1, source_target_pairs={{0,12},{4,8},{8,4},{12,0},{16,28},{20,24},{24,20},{28,16},{1,13},{... | collective-permute-start | bytes 110600 | tf_op jit(solution)/shard_map/ppermute | solution.py:785
  58.0 1.4 %collective-permute-start.14 = (bf16[9,16,128]{2,1,0:T(8,128)(2,1)S(1)}, bf16[9,16,128]{2,1,0:T(8,128)(2,1)S(1)}, u32[]{:S(2)}, u32[]{:S(2)}) collective-permute-start(bf16[9,16,128]{2,1,0:T(8,128)(2,1)S(1)} %get-tuple-element.67), channel_id=1, source_target_pairs={{12,16},{8,20},{0,4},{24,28},{16,12},{20,8},{4,0},{28,24},{13,17},... | collective-permute-start | bytes 110600 | tf_op jit(solution)/shard_map/ppermute | solution.py:784
  59.5 1.4 %collective-permute-start.16 = (bf16[16,128]{1,0:T(8,128)(2,1)S(1)}, bf16[16,128]{1,0:T(8,128)(2,1)S(1)}, u32[]{:S(2)}, u32[]{:S(2)}) collective-permute-start(bf16[16,128]{1,0:T(8,128)(2,1)S(1)} %get-tuple-element.68), channel_id=1, source_target_pairs={{0,8},{4,12},{8,0},{12,4},{16,24},{20,28},{24,16},{28,20},{1,9},{5... | collective-permute-start | bytes 12296 | tf_op jit(solution)/shard_map/ppermute | solution.py:785
  60.9 0.6 collective-permute-start.17
  61.5 1.1 %side_one_hot_rows.1 = (bf16[128,8192]{1,0:T(8,128)(2,1)S(1)}, bf16[128,8192]{1,0:T(8,128)(2,1)S(1)}) custom-call(bf16[2,16,128]{2,1,0:T(8,128)(2,1)S(1)} %get-tuple-element.71.after.c_edges, bf16[656,128]{1,0:T(8,128)(2,1)S(1)} %get-tuple-element.57.from_left, bf16[656,128]{1,0:T(8,128)(2,1)S(1)} %get-tuple-element.58.from_right), custom_call_target="tpu_custom_call" | custom-call | flops 128 | bytes 128 | tf_op jit(solution)/shard_map/side_one_hot_rows/pallas_call | solution.py:793
  62.6 0.5 collective-permute-done.16.nexts
  63.1 1.4 %collective-permute-done.17.beyond = bf16[16,128]{1,0:T(8,128)(2,1)S(1)} collective-permute-done((bf16[16,128]{1,0:T(8,128)(2,1)S(1)}, bf16[16,128]{1,0:T(8,128)(2,1)S(1)}, u32[]{:S(2)}, u32[]{:S(2)}) %collective-permute-start.17) | collective-permute-done | bytes 4128 | tf_op jit(solution)/shard_map/ppermute | solution.py:784
  64.5 4.6 %prolongation_and_last_smoothing.1 = (f32[16,8192]{1,0:T(8,128)}, f32[8,8,128]{2,1,0:T(8,128)S(1)}) custom-call(s32[4,64]{1,0:T(4,128)S(1)} %bitcast.17, s32[3]{0:T(128)S(1)} %pad_add_fusion.place, bf16[64,4,128,128]{3,2,1,0:T(8,128)(2,1)S(1)} %get-tuple-element.43.tiles.turned, bf16[9,16,128]{2,1,0:T(8,128)(2,1)S(1)} %collective-permute-done.13.near, ...), custom_call_target="tpu_custom_call" | custom-call | flops 134217728 | bytes 8388608 | tf_op jit(solution)/shard_map/prolongation_and_last_smoothing/pallas_call | solution.py:801
  69.2 10.8 %all_to_all.11.got = f32[8,8,128]{2,1,0:T(8,128)S(1)} all-to-all(f32[8,8,128]{2,1,0:T(8,128)S(1)} %get-tuple-element.77), channel_id=1, replica_groups=mesh['rows'=8,'cols'=4] {'rows'}, dimensions={0} | all-to-all | bytes 65536 | tf_op jit(solution)/shard_map/all_to_all | solution.py:830
  80.0 0.7 gram_sum.1
  (14 shorter events, 0.0 us)
Async XLA Ops:
  0.6 9.5 %collective-permute-start.3 = (bf16[16,8192]{1,0:T(8,128)(2,1)}, bf16[16,8192]{1,0:T(8,128)(2,1)S(1)}, u32[]{:S(2)}, u32[]{:S(2)}) collective-permute-start(bf16[16,8192]{1,0:T(8,128)(2,1)} %bitcast.9), channel_id=1, source_target_pairs={{0,2},{1,3},{2,0},{3,1},{4,6},{5,7},{6,4},{7,5},{8,10},{9,11},{10,... | collective-permute-start | bytes 786440 | tf_op jit(solution)/shard_map/ppermute | solution.py:592
  4.5 5.4 %copy-start.3 = (bf16[8192,16]{0,1:T(8,128)(2,1)S(1)}, bf16[8192,16]{0,1:T(8,128)(2,1)}, u32[]{:S(2)}) copy-start(bf16[8192,16]{0,1:T(8,128)(2,1)} %param.9) | copy-start | bytes 786436
  4.5 6.0 %copy-start.4 = (s32[64,4]{0,1:T(4,128)S(1)}, s32[64,4]{0,1:T(4,128)}, u32[]{:S(2)}) copy-start(s32[64,4]{0,1:T(4,128)} %param.11) | copy-start | bytes 3076
  4.5 8.5 %copy-start = (bf16[64,4,128,128]{3,2,1,0:T(8,128)(2,1)S(1)}, bf16[64,4,128,128]{3,2,1,0:T(8,128)(2,1)}, u32[]{:S(2)}) copy-start(bf16[64,4,128,128]{3,2,1,0:T(8,128)(2,1)} %tiles.3) | copy-start | bytes 25165828
  7.6 15.8 %collective-permute-start = (bf16[91,16,128]{2,1,0:T(8,128)(2,1)S(1)}, bf16[91,16,128]{2,1,0:T(8,128)(2,1)S(1)}, u32[]{:S(2)}, u32[]{:S(2)}) collective-permute-start(bf16[91,16,128]{2,1,0:T(8,128)(2,1)S(1)} %get-tuple-element.44), channel_id=1, source_target_pairs={{0,4},{8,12},{16,20},{24,28},{4,0},{12,8},{20,16},{28,24},{1,5},{9... | collective-permute-start | bytes 1118216 | tf_op jit(solution)/shard_map/ppermute | solution.py:578
  9.2 6.7 %collective-permute-start.1 = (bf16[75,16,128]{2,1,0:T(8,128)(2,1)S(1)}, bf16[75,16,128]{2,1,0:T(8,128)(2,1)S(1)}, u32[]{:S(2)}, u32[]{:S(2)}) collective-permute-start(bf16[75,16,128]{2,1,0:T(8,128)(2,1)S(1)} %get-tuple-element.45), channel_id=1, source_target_pairs={{4,8},{12,16},{20,24},{8,4},{16,12},{24,20},{5,9},{13,17},{21,25},... | collective-permute-start | bytes 921608 | tf_op jit(solution)/shard_map/ppermute | solution.py:579
  9.9 6.0 %collective-permute-start.2 = (bf16[16,8192]{1,0:T(8,128)(2,1)S(1)}, bf16[16,8192]{1,0:T(8,128)(2,1)S(1)}, u32[]{:S(2)}, u32[]{:S(2)}) collective-permute-start(bf16[16,8192]{1,0:T(8,128)(2,1)S(1)} %bitcast.10), channel_id=1, source_target_pairs={{0,1},{1,0},{2,3},{3,2},{4,5},{5,4},{6,7},{7,6},{8,9},{9,8},{10,11... | collective-permute-start | bytes 786440 | tf_op jit(solution)/shard_map/ppermute | solution.py:592
  10.2 13.3 %collective-permute-start.4 = (bf16[16,8192]{1,0:T(8,128)(2,1)S(1)}, bf16[16,8192]{1,0:T(8,128)(2,1)S(1)}, u32[]{:S(2)}, u32[]{:S(2)}) collective-permute-start(bf16[16,8192]{1,0:T(8,128)(2,1)S(1)} %collective-permute-done.3.basis_c), channel_id=1, source_target_pairs={{0,1},{1,0},{2,3},{3,2},{4,5},{5,4},{6,7},{7,6},{8,9},{9,8},{10,11... | collective-permute-start | bytes 786440 | tf_op jit(solution)/shard_map/ppermute | solution.py:592
  24.9 12.6 %collective-permute-start.5 = (bf16[65,16,128]{2,1,0:T(8,128)(2,1)S(1)}, bf16[65,16,128]{2,1,0:T(8,128)(2,1)S(1)}, u32[]{:S(2)}, u32[]{:S(2)}) collective-permute-start(bf16[65,16,128]{2,1,0:T(8,128)(2,1)S(1)} %get-tuple-element.49), channel_id=1, source_target_pairs={{0,4},{8,12},{16,20},{24,28},{4,0},{12,8},{20,16},{28,24},{1,5},{9... | collective-permute-start | bytes 798728 | tf_op jit(solution)/shard_map/ppermute | solution.py:578
  27.5 9.4 %collective-permute-start.6 = (bf16[64,16,128]{2,1,0:T(8,128)(2,1)S(1)}, bf16[64,16,128]{2,1,0:T(8,128)(2,1)S(1)}, u32[]{:S(2)}, u32[]{:S(2)}) collective-permute-start(bf16[64,16,128]{2,1,0:T(8,128)(2,1)S(1)} %get-tuple-element.50.own), channel_id=1, source_target_pairs={{4,8},{12,16},{20,24},{8,4},{16,12},{24,20},{5,9},{13,17},{21,25},... | collective-permute-start | bytes 786440 | tf_op jit(solution)/shard_map/ppermute | solution.py:579
  28.2 5.3 %collective-permute-start.7 = (bf16[22,16,128]{2,1,0:T(8,128)(2,1)S(1)}, bf16[22,16,128]{2,1,0:T(8,128)(2,1)S(1)}, u32[]{:S(2)}, u32[]{:S(2)}) collective-permute-start(bf16[22,16,128]{2,1,0:T(8,128)(2,1)S(1)} %get-tuple-element.51.refs_0_.a), channel_id=1, source_target_pairs={{0,2},{1,3},{2,0},{3,1},{4,6},{5,7},{6,4},{7,5},{8,10},{9,11},{10,... | collective-permute-start | bytes 270344 | tf_op jit(solution)/shard_map/ppermute | solution.py:592
  28.8 7.3 %copy-start.1 = (bf16[8,3,128,128]{3,2,1,0:T(8,128)(2,1)S(1)}, bf16[8,3,128,128]{3,2,1,0:T(8,128)(2,1)}, u32[]{:S(2)}) copy-start(bf16[8,3,128,128]{3,2,1,0:T(8,128)(2,1)} %mid_tiles.9) | copy-start | bytes 2359300
  28.8 4.7 %collective-permute-start.8 = (bf16[16,16,128]{2,1,0:T(8,128)(2,1)S(1)}, bf16[16,16,128]{2,1,0:T(8,128)(2,1)S(1)}, u32[]{:S(2)}, u32[]{:S(2)}) collective-permute-start(bf16[16,16,128]{2,1,0:T(8,128)(2,1)S(1)} %get-tuple-element.52.refs_1_.rows_a), channel_id=1, source_target_pairs={{0,2},{1,3},{2,0},{3,1},{4,6},{5,7},{6,4},{7,5},{8,10},{9,11},{10,... | collective-permute-start | bytes 196616 | tf_op jit(solution)/shard_map/ppermute | solution.py:592
  33.5 1.3 %collective-permute-start.11 = (bf16[16,16,128]{2,1,0:T(8,128)(2,1)S(1)}, bf16[16,16,128]{2,1,0:T(8,128)(2,1)S(1)}, u32[]{:S(2)}, u32[]{:S(2)}) collective-permute-start(bf16[16,16,128]{2,1,0:T(8,128)(2,1)S(1)} %get-tuple-element.55), channel_id=1, source_target_pairs={{0,1},{1,0},{2,3},{3,2},{4,5},{5,4},{6,7},{7,6},{8,9},{9,8},{10,11... | collective-permute-start | bytes 196616 | tf_op jit(solution)/shard_map/ppermute | solution.py:592
  33.6 2.5 %collective-permute-start.9 = (bf16[22,16,128]{2,1,0:T(8,128)(2,1)S(1)}, bf16[22,16,128]{2,1,0:T(8,128)(2,1)S(1)}, u32[]{:S(2)}, u32[]{:S(2)}) collective-permute-start(bf16[22,16,128]{2,1,0:T(8,128)(2,1)S(1)} %get-tuple-element.53), channel_id=1, source_target_pairs={{0,1},{1,0},{2,3},{3,2},{4,5},{5,4},{6,7},{7,6},{8,9},{9,8},{10,11... | collective-permute-start | bytes 270344 | tf_op jit(solution)/shard_map/ppermute | solution.py:592
  34.1 2.0 %collective-permute-start.10 = (bf16[22,16,128]{2,1,0:T(8,128)(2,1)S(1)}, bf16[22,16,128]{2,1,0:T(8,128)(2,1)S(1)}, u32[]{:S(2)}, u32[]{:S(2)}) collective-permute-start(bf16[22,16,128]{2,1,0:T(8,128)(2,1)S(1)} %get-tuple-element.54), channel_id=1, source_target_pairs={{0,1},{1,0},{2,3},{3,2},{4,5},{5,4},{6,7},{7,6},{8,9},{9,8},{10,11... | collective-permute-start | bytes 270344 | tf_op jit(solution)/shard_map/ppermute | solution.py:592
  34.8 1.3 %collective-permute-start.12 = (bf16[16,16,128]{2,1,0:T(8,128)(2,1)S(1)}, bf16[16,16,128]{2,1,0:T(8,128)(2,1)S(1)}, u32[]{:S(2)}, u32[]{:S(2)}) collective-permute-start(bf16[16,16,128]{2,1,0:T(8,128)(2,1)S(1)} %get-tuple-element.56), channel_id=1, source_target_pairs={{0,1},{1,0},{2,3},{3,2},{4,5},{5,4},{6,7},{7,6},{8,9},{9,8},{10,11... | collective-permute-start | bytes 196616 | tf_op jit(solution)/shard_map/ppermute | solution.py:592
  37.6 17.8 %copy-start.2 = (f32[128,1024]{1,0:T(8,128)S(1)}, f32[128,1024]{1,0:T(8,128)}, u32[]{:S(2)}) copy-start(f32[128,1024]{1,0:T(8,128)} %inverse_rows.3) | copy-start | bytes 1572868
  56.6 7.9 %collective-permute-start.13 = (bf16[9,16,128]{2,1,0:T(8,128)(2,1)S(1)}, bf16[9,16,128]{2,1,0:T(8,128)(2,1)S(1)}, u32[]{:S(2)}, u32[]{:S(2)}) collective-permute-start(bf16[9,16,128]{2,1,0:T(8,128)(2,1)S(1)} %get-tuple-element.66), channel_id=1, source_target_pairs={{0,4},{4,0},{8,12},{12,8},{16,20},{20,16},{24,28},{28,24},{1,5},{5... | collective-permute-start | bytes 110600 | tf_op jit(solution)/shard_map/ppermute | solution.py:785
  57.0 7.5 %collective-permute-start.15 = (bf16[9,16,128]{2,1,0:T(8,128)(2,1)S(1)}, bf16[9,16,128]{2,1,0:T(8,128)(2,1)S(1)}, u32[]{:S(2)}, u32[]{:S(2)}) collective-permute-start(bf16[9,16,128]{2,1,0:T(8,128)(2,1)S(1)} %get-tuple-element.67), channel_id=1, source_target_pairs={{0,12},{4,8},{8,4},{12,0},{16,28},{20,24},{24,20},{28,16},{1,13},{... | collective-permute-start | bytes 110600 | tf_op jit(solution)/shard_map/ppermute | solution.py:785
  58.0 6.5 %collective-permute-start.14 = (bf16[9,16,128]{2,1,0:T(8,128)(2,1)S(1)}, bf16[9,16,128]{2,1,0:T(8,128)(2,1)S(1)}, u32[]{:S(2)}, u32[]{:S(2)}) collective-permute-start(bf16[9,16,128]{2,1,0:T(8,128)(2,1)S(1)} %get-tuple-element.67), channel_id=1, source_target_pairs={{12,16},{8,20},{0,4},{24,28},{16,12},{20,8},{4,0},{28,24},{13,17},... | collective-permute-start | bytes 110600 | tf_op jit(solution)/shard_map/ppermute | solution.py:784
  59.5 3.6 %collective-permute-start.16 = (bf16[16,128]{1,0:T(8,128)(2,1)S(1)}, bf16[16,128]{1,0:T(8,128)(2,1)S(1)}, u32[]{:S(2)}, u32[]{:S(2)}) collective-permute-start(bf16[16,128]{1,0:T(8,128)(2,1)S(1)} %get-tuple-element.68), channel_id=1, source_target_pairs={{0,8},{4,12},{8,0},{12,4},{16,24},{20,28},{24,16},{28,20},{1,9},{5... | collective-permute-start | bytes 12296 | tf_op jit(solution)/shard_map/ppermute | solution.py:785
  60.9 3.6 %collective-permute-start.17 = (bf16[16,128]{1,0:T(8,128)(2,1)S(1)}, bf16[16,128]{1,0:T(8,128)(2,1)S(1)}, u32[]{:S(2)}, u32[]{:S(2)}) collective-permute-start(bf16[16,128]{1,0:T(8,128)(2,1)S(1)} %get-tuple-element.69), channel_id=1, source_target_pairs={{8,16},{12,20},{0,4},{24,28},{16,8},{20,12},{4,0},{28,24},{9,17},{... | collective-permute-start | bytes 12296 | tf_op jit(solution)/shard_map/ppermute | solution.py:784
